TPU v7x, 32 devices: a whole 2x2x4 slice. The times are simulated.
32 devices in a mesh: edge: 8 (over z, x), feat: 4 (over y, core).
Axes of the slice: x: 2, y: 2, z: 4, core: 2. Of those that a mesh axis runs over, the one named last changes fastest.
Arguments:
- node_feat: bfloat16 [16384, 128], P('edge'), may hold values from -6 to 6
- cotangent: bfloat16 [16384, 128], P('edge'), may hold values from -6 to 6
- w_msg: bfloat16 [128, 128], replicated, may hold values from -0.5 to 0.5
- w_self: bfloat16 [128, 128], replicated, may hold values from -0.5 to 0.5
- adjacency: bfloat16 [8, 4, 64, 128, 128], P('edge', 'feat'), may hold values from -0.125 to 0.125
- edge_src: int32 [8, 4, 64], P('edge', 'feat'), may hold values from 0 to 15
- edge_dst: int32 [8, 4, 64], P('edge', 'feat'), may hold values from 0 to 15
- send_src: int32 [8, 4, 8, 2], P('edge', 'feat'), may hold values from 0 to 15
- recv_dst: int32 [8, 4, 8, 2], P('edge', 'feat'), may hold values from 0 to 15
- live: int32 [8, 4], P('edge', 'feat'), may hold values from 4 to 64, as said below
Outputs:
- out_feat: bfloat16 [16384, 128], P('edge')
- grad_feat: bfloat16 [16384, 128], P('edge')
- grad_wmsg: float32 [128, 128], replicated
- grad_wself: float32 [128, 128], replicated
Inputs may be any that keep to these rules, and one draw needn't show every extreme that they name: Each device has between 64 // 16 (at least 1) and 64 live blocks; one device always has all 64 live.
All inputs are finite; a program needn't handle non-finite values.
Results may differ from a plain program's by a relative error of at most 0.0054.
Values may be sent and summed in bfloat16 or wider, within the bound.
No kernel may reach another device: no remote copies, remote signals or barrier semaphores. Data moves between devices by JAX's collectives and lax.ppermute only.
A program may use at most 128 MiB of HBM per device.

v0:
```python
import math

import jax
import jax.numpy as jnp
from jax import lax
from jax.sharding import PartitionSpec as P


def edge_terms(blocks_adj, source_rows, pick_ids, put_ids, slot_count, live_count, forward):
    block_count = blocks_adj.shape[0]
    width = source_rows.shape[-1]
    block_size = blocks_adj.shape[-1]

    def block_terms(blocks, picked):
        if forward:
            return jnp.einsum("eij,ejh->eih", blocks, picked, preferred_element_type=jnp.float32)
        return jnp.einsum("eij,eih->ejh", blocks, picked, preferred_element_type=jnp.float32)

    empty = jnp.zeros((slot_count, block_size, width), jnp.float32)
    group_size = math.gcd(32, block_count)
    round_count = (live_count + group_size - 1) // group_size

    def one_round(turn_index, running):
        offset = turn_index * group_size
        blocks = lax.dynamic_slice_in_dim(blocks_adj, offset, group_size, 0)
        picks = lax.dynamic_slice_in_dim(pick_ids, offset, group_size, 0)
        puts = lax.dynamic_slice_in_dim(put_ids, offset, group_size, 0)
        keep_mask = (offset + jnp.arange(group_size, dtype=jnp.int32) < live_count).astype(
            jnp.float32
        )
        terms = block_terms(blocks, jnp.take(source_rows, picks, axis=0)) * keep_mask[:, None, None]
        return running.at[puts].add(terms)

    return lax.fori_loop(0, round_count, one_round, empty)


def body(
    node_feat, cotangent, w_msg, w_self, adjacency, edge_src, edge_dst, send_src, recv_dst, live
):
    block_size = adjacency.shape[-1]
    hidden = node_feat.shape[1]
    owned_blocks = node_feat.shape[0] // block_size
    peer_count = lax.axis_size("edge")
    send_slots = send_src.shape[-1]
    dest_slots = recv_dst.shape[-1]
    send_ids = send_src.reshape(-1)
    recv_ids = recv_dst.reshape(-1)
    blocks_adj = adjacency.reshape(-1, block_size, block_size)
    src_ids = edge_src.reshape(-1)
    dst_ids = edge_dst.reshape(-1)
    live_count = live.reshape(())
    outgoing = jnp.take(node_feat.reshape(owned_blocks, block_size, hidden), send_ids, axis=0)
    raw_rows = lax.all_to_all(
        outgoing.reshape(peer_count, send_slots, block_size, hidden),
        "edge",
        split_axis=0,
        concat_axis=0,
        tiled=True,
    )
    incoming = jnp.dot(
        raw_rows.reshape(-1, hidden), w_msg, preferred_element_type=jnp.float32
    ).astype(jnp.bfloat16)
    incoming = incoming.reshape(-1, block_size, hidden)
    partials = edge_terms(
        blocks_adj, incoming, src_ids, dst_ids, peer_count * dest_slots, live_count, True
    )
    returned = lax.all_to_all(
        partials.reshape(peer_count, dest_slots, block_size, hidden),
        "edge",
        split_axis=0,
        concat_axis=0,
        tiled=True,
    )
    owner_sum = (
        jnp.zeros((owned_blocks, block_size, hidden), jnp.float32)
        .at[recv_ids]
        .add(returned.reshape(-1, block_size, hidden))
    )
    aggregate = lax.psum(owner_sum, "feat")
    preact = jnp.dot(node_feat, w_self, preferred_element_type=jnp.float32) + aggregate.reshape(
        -1, hidden
    )
    sigmoid_pre = jax.nn.sigmoid(preact)
    out_feat = (preact * sigmoid_pre).astype(jnp.bfloat16)
    grad_pre = (
        cotangent.astype(jnp.float32) * sigmoid_pre * (1.0 + preact * (1.0 - sigmoid_pre))
    ).astype(jnp.bfloat16)
    wself_part = lax.dot_general(
        node_feat, grad_pre, (((0,), (0,)), ((), ())), preferred_element_type=jnp.float32
    )
    grad_out = jnp.take(grad_pre.reshape(owned_blocks, block_size, hidden), recv_ids, axis=0)
    grad_in = lax.all_to_all(
        grad_out.reshape(peer_count, dest_slots, block_size, hidden),
        "edge",
        split_axis=0,
        concat_axis=0,
        tiled=True,
    )
    grad_in = grad_in.reshape(-1, block_size, hidden)
    grad_partials = edge_terms(
        blocks_adj, grad_in, dst_ids, src_ids, peer_count * send_slots, live_count, False
    )
    grad_back = lax.all_to_all(
        grad_partials.reshape(peer_count, send_slots, block_size, hidden),
        "edge",
        split_axis=0,
        concat_axis=0,
        tiled=True,
    )
    grad_owner = (
        jnp.zeros((owned_blocks, block_size, hidden), jnp.float32)
        .at[send_ids]
        .add(grad_back.reshape(-1, block_size, hidden))
    )
    grad_sum = lax.psum(grad_owner, "feat")
    grad_msg = grad_sum.reshape(-1, hidden).astype(jnp.bfloat16)
    wmsg_part = lax.dot_general(
        node_feat, grad_msg, (((0,), (0,)), ((), ())), preferred_element_type=jnp.float32
    )
    grad_wmsg, grad_wself = lax.psum((wmsg_part, wself_part), "edge")
    grad_feat = (
        jnp.dot(grad_pre, w_self.T, preferred_element_type=jnp.float32)
        + jnp.dot(grad_msg, w_msg.T, preferred_element_type=jnp.float32)
    ).astype(jnp.bfloat16)
    return (out_feat, grad_feat, grad_wmsg, grad_wself)


def solution(mesh):
    in_specs = (
        P("edge", None),
        P("edge", None),
        P(),
        P(),
        P("edge", "feat", None, None, None),
        P("edge", "feat", None),
        P("edge", "feat", None),
        P("edge", "feat", None, None),
        P("edge", "feat", None, None),
        P("edge", "feat"),
    )
    out_specs = (P("edge", None), P("edge", None), P(), P())
    return jax.shard_map(body, mesh=mesh, in_specs=in_specs, out_specs=out_specs, check_vma=False)
```

profile of v0, /device:TPU:0, one launch (start us, length us, event | category | flops | bytes accessed | tf_op | source)
XLA Modules:
  0.0 309.1 jit_solution(1604272685182584075)
XLA Ops:
  7.2 0.8 copy.24
  8.0 0.1 reshape.152
  8.1 0.1 copy-done
  8.2 0.6 gather_fusion.2
  8.9 0.9 broadcast_select_fusion.1
  9.8 7.3 %all-to-all-start = ((bf16[8,2,128,128]{3,2,1,0:T(8,128)(2,1)}), bf16[8,2,128,128]{3,2,1,0:T(8,128)(2,1)S(1)}, u32[]{:S(2)}, u32[]{:S(2)}) async-start(bf16[8,2,128,128]{3,2,1,0:T(8,128)(2,1)} %bitcast.7), calls=%async_computation | async-start | bytes 1048576 | tf_op jit(solution)/shard_map/all_to_all | solution.py:53
  17.7 13.8 %all-to-all-done = bf16[8,2,128,128]{3,2,1,0:T(8,128)(2,1)S(1)} async-done(((bf16[8,2,128,128]{3,2,1,0:T(8,128)(2,1)}), bf16[8,2,128,128]{3,2,1,0:T(8,128)(2,1)S(1)}, u32[]{:S(2)}, u32[]{:S(2)}) %all-to-all-start) | async-done | bytes 524320 | tf_op jit(solution)/shard_map/all_to_all | solution.py:53
  31.6 0.3 convolution_convert_fusion
  31.8 1.1 broadcast.85.clone.1
  32.9 10.6 %while.20 = (s32[]{:T(128)}, f32[16,128,128]{2,1,0:T(8,128)}, s32[]{:T(128)}, s32[64]{0:T(128)S(1)}, bf16[64,128,128]{2,1,0:T(8,128)(2,1)}, /*index=5*/s32[64]{0...) while((s32[]{:T(128)}, f32[16,128,128]{2,1,0:T(8,128)}, ...), condition=%wide.region_2.5_spmd, body=%wide.region_0.4_spmd.sunk | while | flops 135792000 | bytes 12588407 | solution.py:34
  32.9 0.7 compare_and_fusion.6
  33.7 1.7 gather_fusion
  35.3 2.0 convolution_multiply_fusion.4
  37.4 0.1 compare_select_fusion.12
  37.5 6.0 %scatter_fusion = f32[16,128,128]{2,1,0:T(8,128)} fusion(f32[16,128,128]{2,1,0:T(8,128)} %get-tuple-element.285, s32[32]{0:T(128)S(1)} %compare_select_fusion.12, f32[32,128,128]{2,1,0:T(8,128)S(1)} %convolution_multiply_fusion.4), kind=kCustom, calls=%fused_computation.4.clone.1 | custom fusion | flops 524288 | bytes 6291584 | tf_op jit(solution)/shard_map/while/body/scatter-add | solution.py:32
  43.5 14.4 %all-to-all-start.1 = ((f32[8,2,128,128]{3,2,1,0:T(8,128)}), f32[8,2,128,128]{3,2,1,0:T(8,128)S(1)}, u32[]{:S(2)}, u32[]{:S(2)}) async-start(f32[8,2,128,128]{3,2,1,0:T(8,128)} %bitcast.48), calls=%async_computation.1 | async-start | bytes 2097152 | tf_op jit(solution)/shard_map/all_to_all | solution.py:67
  58.0 0.1 copy.22
  58.1 0.1 reshape.146
  58.2 24.4 %all-to-all-done.1 = f32[8,2,128,128]{3,2,1,0:T(8,128)S(1)} async-done(((f32[8,2,128,128]{3,2,1,0:T(8,128)}), f32[8,2,128,128]{3,2,1,0:T(8,128)S(1)}, u32[]{:S(2)}, u32[]{:S(2)}) %all-to-all-start.1) | async-done | bytes 1048608 | tf_op jit(solution)/shard_map/all_to_all | solution.py:67
  82.6 0.1 broadcast.85.clone
  82.7 1.6 scatter_fusion.2
  84.3 1.0 copy-done.2
  85.4 36.5 %all-reduce.5.cloned.1.call-done = f32[2048,128]{1,0:T(8,128)} async-done(((f32[2048,128]{1,0:T(8,128)}), f32[2048,128]{1,0:T(8,128)}) %all-reduce.5.cloned.1.call-update) | async-done | bytes 1048592 | tf_op jit(solution)/shard_map/psum | solution.py:79
  121.9 2.9 multiply_convert_fusion
  124.8 1.4 gather_fusion.3
  126.2 1.9 broadcast_select_fusion
  128.1 5.5 %all-to-all-start.2 = ((bf16[8,2,128,128]{3,2,1,0:T(8,128)(2,1)}), bf16[8,2,128,128]{3,2,1,0:T(8,128)(2,1)S(1)}, u32[]{:S(2)}, u32[]{:S(2)}) async-start(bf16[8,2,128,128]{3,2,1,0:T(8,128)(2,1)} %bitcast.62), calls=%async_computation.2 | async-start | bytes 1048576 | tf_op jit(solution)/shard_map/all_to_all | solution.py:92
  133.7 2.9 copy.23
  136.6 11.2 %all-to-all-done.2 = bf16[8,2,128,128]{3,2,1,0:T(8,128)(2,1)S(1)} async-done(((bf16[8,2,128,128]{3,2,1,0:T(8,128)(2,1)}), bf16[8,2,128,128]{3,2,1,0:T(8,128)(2,1)S(1)}, u32[]{:S(2)}, u32[]{:S(2)}) %all-to-all-start.2) | async-done | bytes 524320 | tf_op jit(solution)/shard_map/all_to_all | solution.py:92
  147.7 1.1 broadcast.85.clone.2
  148.8 10.6 %while.21 = (s32[]{:T(128)}, f32[16,128,128]{2,1,0:T(8,128)}, s32[]{:T(128)}, s32[64]{0:T(128)S(1)}, bf16[64,128,128]{1,2,0:T(8,128)(2,1)}, /*index=5*/s32[64]{0...) while((s32[]{:T(128)}, f32[16,128,128]{2,1,0:T(8,128)}, ...), condition=%wide.region_7.10_spmd, body=%wide.region_5.9_spmd.sunk | while | flops 135792000 | bytes 12588407 | solution.py:34
  148.8 0.7 compare_and_fusion.7
  149.5 1.7 gather_fusion.1
  151.2 2.0 convolution_multiply_fusion.5
  153.4 6.1 %scatter_fusion.1 = f32[16,128,128]{2,1,0:T(8,128)} fusion(f32[16,128,128]{2,1,0:T(8,128)} %get-tuple-element.321, s32[32]{0:T(128)S(1)} %compare_select_fusion.13, f32[32,128,128]{2,1,0:T(8,128)S(1)} %convolution_multiply_fusion.5), kind=kCustom, calls=%fused_computation.5.clone.1 | custom fusion | flops 524288 | bytes 6291584 | tf_op jit(solution)/shard_map/while/body/scatter-add | solution.py:32
  159.4 14.4 %all-to-all-start.3 = ((f32[8,2,128,128]{3,2,1,0:T(8,128)}), f32[8,2,128,128]{3,2,1,0:T(8,128)S(1)}, u32[]{:S(2)}, u32[]{:S(2)}) async-start(f32[8,2,128,128]{3,2,1,0:T(8,128)} %bitcast.49), calls=%async_computation.3 | async-start | bytes 2097152 | tf_op jit(solution)/shard_map/all_to_all | solution.py:103
  173.9 1.0 convolution_bitcast_fusion
  174.9 0.3 fusion.15
  175.2 23.2 %all-to-all-done.3 = f32[8,2,128,128]{3,2,1,0:T(8,128)S(1)} async-done(((f32[8,2,128,128]{3,2,1,0:T(8,128)}), f32[8,2,128,128]{3,2,1,0:T(8,128)S(1)}, u32[]{:S(2)}, u32[]{:S(2)}) %all-to-all-start.3) | async-done | bytes 1048608 | tf_op jit(solution)/shard_map/all_to_all | solution.py:103
  198.4 1.0 copy-done.5
  199.3 0.1 broadcast.85
  199.4 2.6 scatter_fusion.3
  202.0 26.4 %all-reduce.8 = bf16[16,128,128]{2,1,0:T(8,128)(2,1)S(1)} all-reduce(f32[16,128,128]{2,1,0:T(8,128)S(1)} %scatter_fusion.3), channel_id=1, replica_groups=mesh['edge'=8,'feat'=4] {'feat'}, use_global_device_ids=true, to_apply=%region_9.12 | all-reduce | flops 262144 | bytes 1572864 | tf_op jit(solution)/shard_map/psum | solution.py:115
  228.5 1.0 convolution_bitcast_fusion.1
  229.5 1.1 fusion.12
  230.6 68.5 %all-reduce.7.cloned.1.call-done = (f32[128,128]{0,1:T(8,128)}, f32[128,128]{0,1:T(8,128)}) async-done(((f32[128,128]{0,1:T(8,128)}, f32[128,128]{0,1:T(8,128)}), (f32[128,128]{0,1:T(8,128)}, f32[128,128]{0,1:T(8,128)})) %all-reduce.7.cloned.1.call-update) | async-done | bytes 131088 | tf_op jit(solution)/shard_map/psum | solution.py:120
  299.1 1.6 copy.28
  300.6 1.6 copy.29
  (36 shorter events, 0.5 us)
Async XLA Ops:
  7.2 1.1 copy-start
  7.2 24.4 %copy-start.6 = (bf16[128,128]{1,0:T(8,128)(2,1)S(1)}, bf16[128,128]{1,0:T(8,128)(2,1)}, u32[]{:S(2)}) copy-start(bf16[128,128]{1,0:T(8,128)(2,1)} %param.20) | copy-start | bytes 98308
  8.9 24.0 %copy-start.8 = (s32[1,1,64]{2,1,0:T(1,128)S(1)}, s32[1,1,64]{2,1,0:T(1,128)}, u32[]{:S(2)}) copy-start(s32[1,1,64]{2,1,0:T(1,128)} %param.24) | copy-start | bytes 772
  8.9 24.0 %copy-start.9 = (s32[1,1,64]{2,1,0:T(1,128)S(1)}, s32[1,1,64]{2,1,0:T(1,128)}, u32[]{:S(2)}) copy-start(s32[1,1,64]{2,1,0:T(1,128)} %param.23) | copy-start | bytes 772
  9.8 21.7 %all-to-all-start = ((bf16[8,2,128,128]{3,2,1,0:T(8,128)(2,1)}), bf16[8,2,128,128]{3,2,1,0:T(8,128)(2,1)S(1)}, u32[]{:S(2)}, u32[]{:S(2)}) async-start(bf16[8,2,128,128]{3,2,1,0:T(8,128)(2,1)} %bitcast.7), calls=%async_computation | async-start | bytes 1048576 | tf_op jit(solution)/shard_map/all_to_all | solution.py:53
  43.5 14.5 %copy-start.10 = (s32[1,1,8,2]{2,3,1,0:T(2,128)S(1)}, s32[1,1,8,2]{2,3,1,0:T(2,128)}, u32[]{:S(2)}) copy-start(s32[1,1,8,2]{2,3,1,0:T(2,128)} %param.26) | copy-start | bytes 196
  43.5 39.1 %all-to-all-start.1 = ((f32[8,2,128,128]{3,2,1,0:T(8,128)}), f32[8,2,128,128]{3,2,1,0:T(8,128)S(1)}, u32[]{:S(2)}, u32[]{:S(2)}) async-start(f32[8,2,128,128]{3,2,1,0:T(8,128)} %bitcast.48), calls=%async_computation.1 | async-start | bytes 2097152 | tf_op jit(solution)/shard_map/all_to_all | solution.py:67
  57.9 64.0 %all-reduce.5.cloned.1.call-start = ((), (), s32[]{:S(2)}) async-start(), calls=%async_computation.4 | async-start | bytes 2097152 | tf_op jit(solution)/shard_map/psum | solution.py:79
  82.7 39.2 %copy-start.7 = (bf16[128,128]{1,0:T(8,128)(2,1)S(1)}, bf16[128,128]{1,0:T(8,128)(2,1)}, u32[]{:S(2)}) copy-start(bf16[128,128]{1,0:T(8,128)(2,1)} %param.21) | copy-start | bytes 98308
  84.3 1.0 copy-start.2
  124.8 3.4 %copy-start.3 = (bf16[2048,128]{1,0:T(8,128)(2,1)}, bf16[2048,128]{1,0:T(8,128)(2,1)S(1)}, u32[]{:S(2)}) copy-start(bf16[2048,128]{1,0:T(8,128)(2,1)S(1)} %get-tuple-element.158) | copy-start | bytes 1572868
  124.8 8.9 %copy-start.1 = (bf16[64,128,128]{2,1,0:T(8,128)(2,1)S(1)}, bf16[64,128,128]{2,1,0:T(8,128)(2,1)}, u32[]{:S(2)}) copy-start(bf16[64,128,128]{2,1,0:T(8,128)(2,1)} %get-tuple-element.354) | copy-start | bytes 6291460
  128.1 19.6 %all-to-all-start.2 = ((bf16[8,2,128,128]{3,2,1,0:T(8,128)(2,1)}), bf16[8,2,128,128]{3,2,1,0:T(8,128)(2,1)S(1)}, u32[]{:S(2)}, u32[]{:S(2)}) async-start(bf16[8,2,128,128]{3,2,1,0:T(8,128)(2,1)} %bitcast.62), calls=%async_computation.2 | async-start | bytes 1048576 | tf_op jit(solution)/shard_map/all_to_all | solution.py:92
  159.4 14.5 %copy-start.4 = (bf16[2048,128]{1,0:T(8,128)(2,1)S(1)}, bf16[2048,128]{1,0:T(8,128)(2,1)}, u32[]{:S(2)}) copy-start(bf16[2048,128]{1,0:T(8,128)(2,1)} %copy-done.3) | copy-start | bytes 1572868
  159.4 38.9 %all-to-all-start.3 = ((f32[8,2,128,128]{3,2,1,0:T(8,128)}), f32[8,2,128,128]{3,2,1,0:T(8,128)S(1)}, u32[]{:S(2)}, u32[]{:S(2)}) async-start(f32[8,2,128,128]{3,2,1,0:T(8,128)} %bitcast.49), calls=%async_computation.3 | async-start | bytes 2097152 | tf_op jit(solution)/shard_map/all_to_all | solution.py:103
  173.8 125.3 %all-reduce.7.cloned.1.call-start = ((), (), s32[]{:S(2)}) async-start(), calls=%async_computation.5 | async-start | bytes 262144 | tf_op jit(solution)/shard_map/psum | solution.py:120
  198.4 1.0 copy-start.5
Sparse Core Ops, SparseCore 0:
  85.5 36.3 all-reduce.4
  229.6 69.4 all-reduce.6
where the time goes:
time: 309 us
  waiting for transfers between devices  178 us (58%)
  starting transfers between devices  41.6 us (13%)
  blocking collectives  26.4 us (9%)
  other arithmetic  20.8 us (7%)
  local copies, waits for them, and re-layouts  17.2 us (6%)
  between operations  14.9 us (5%)
  matrix products  10.6 us (3%)
    psum x1, waiting for transfers between devices, body(): grad_wmsg, grad_wself = lax.psum((wmsg_part, wself_part), 'edge')  68.5 us
    psum x1, waiting for transfers between devices, body(): aggregate = lax.psum(owner_sum, 'feat')  36.5 us
    psum x1, blocking collectives, body(): grad_sum = lax.psum(grad_owner, 'feat')  26.4 us
    all_to_all x1, waiting for transfers between devices, body(): lax.all_to_all(partials.reshape(peer_count, dest_slots, block_size, hidde...  24.4 us
    all_to_all x1, waiting for transfers between devices, body(): lax.all_to_all(grad_partials.reshape(peer_count, send_slots, block_size,...  23.2 us
    all_to_all x1, starting transfers between devices, body(): lax.all_to_all(partials.reshape(peer_count, dest_slots, block_size, hidde...  14.4 us
    all_to_all x1, starting transfers between devices, body(): lax.all_to_all(grad_partials.reshape(peer_count, send_slots, block_size,...  14.4 us
    all_to_all x1, waiting for transfers between devices, body(): lax.all_to_all(outgoing.reshape(peer_count, send_slots, block_size, hidde...  13.8 us
  transfers between devices with their start and end apart: 6, of which 6 were waited for; matrix products, arithmetic and copies ran while one was open for 2% of the time, Pallas kernels for 0%

commit v1 on v0

v1 whole, which is shorter than its diff:
```python
import functools
import math

import jax
import jax.numpy as jnp
from jax import lax
from jax.experimental import pallas as pl
from jax.experimental.pallas import tpu as pltpu
from jax.sharding import PartitionSpec as P

BOTH = ("edge", "feat")
F32 = jnp.float32
BF16 = jnp.bfloat16
VMEM = pl.BlockSpec(memory_space=pltpu.VMEM)
SMEM = pl.BlockSpec(memory_space=pltpu.SMEM)


def is_pow2(n):
    return n & (n - 1) == 0


def swap(x, axis, bit):
    size = lax.axis_size(axis)
    return lax.ppermute(x, axis, [(j, j ^ bit) for j in range(size)])


def gather_feat(x):
    size = lax.axis_size("feat")
    if not is_pow2(size):
        return lax.all_gather(x, "feat", axis=0)
    me = lax.axis_index("feat")
    held = x[None]
    bit = 1
    while bit < size:
        other = swap(held, "feat", bit)
        mine_low = (me & bit) == 0
        held = jnp.where(
            mine_low, jnp.concatenate([held, other], 0), jnp.concatenate([other, held], 0)
        )
        bit *= 2
    return held


def sum_all(x):
    for axis in ("feat", "edge"):
        size = lax.axis_size(axis)
        if not is_pow2(size):
            x = lax.psum(x, axis)
            continue
        bit = 1
        while bit < size:
            x = x + swap(x, axis, bit)
            bit *= 2
    return x


def pick_kernel(ids, rows, out):
    for i in range(out.shape[0]):
        out[i] = rows[ids[i]]


def forward_kernel(group, live, src, dst, raw, w_msg, adj, out, msgs, acc):
    slots, block, hidden = raw.shape
    per_owner, width = out.shape[1:3]
    planes = block // width
    flat = raw[...].reshape(slots * block, hidden)
    msgs[...] = (
        jnp.dot(flat, w_msg[...], preferred_element_type=F32)
        .astype(BF16)
        .reshape(slots, block, hidden)
    )
    acc[...] = jnp.zeros_like(acc)
    count = live[0]

    def step(turn, carry):
        terms = []
        for u in range(group):
            k = turn * group + u
            terms.append(jnp.dot(adj[k], msgs[src[k]], preferred_element_type=F32))
        for u in range(group):
            k = turn * group + u
            d = jnp.where(k < count, dst[k], slots)
            acc[d] += terms[u]
        return carry

    lax.fori_loop(0, (count + group - 1) // group, step, 0)
    for s in range(slots):
        for q in range(planes):
            out[s // per_owner * planes + q, s % per_owner] = acc[
                s, q * width : (q + 1) * width
            ].astype(BF16)


def owner_kernel(
    me, ids, got, feat, cot, w_self, out_feat, grad_pre, outgoing, w_part, agg, held
):
    blocks, planes, width, hidden = feat.shape
    devices, per_owner = got.shape[:2]
    q = me[0]
    agg[...] = jnp.zeros_like(agg)
    for i in range(devices):
        for j in range(per_owner):
            agg[ids[i * per_owner + j]] += got[i, j].astype(F32)
    mine = feat[:, q].reshape(blocks * width, hidden)
    preact = jnp.dot(mine, w_self[...], preferred_element_type=F32)
    preact = preact + agg[...].reshape(blocks * width, hidden)
    sig = jax.nn.sigmoid(preact)
    out_feat[...] = (preact * sig).astype(BF16).reshape(blocks, width, hidden)
    grad = cot[:, q].reshape(blocks * width, hidden).astype(F32)
    grad = (grad * sig * (1.0 + preact * (1.0 - sig))).astype(BF16)
    held[...] = grad.reshape(blocks, width, hidden)
    grad_pre[...] = held[...]
    for i in range(devices):
        for j in range(per_owner):
            outgoing[i, j] = held[ids[i * per_owner + j]]
    w_part[...] = lax.dot_general(
        mine, grad, (((0,), (0,)), ((), ())), preferred_element_type=F32
    )


def backward_kernel(group, live, src, dst, got, raw, adj, out, w_part, turned, acc):
    slots, block, hidden = raw.shape
    devices, per_owner, width = got.shape[:3]
    planes = block // width
    out_slots = out.shape[1]
    for p in range(devices // planes):
        for j in range(per_owner):
            whole = jnp.concatenate([got[p * planes + q, j] for q in range(planes)], 0)
            turned[p * per_owner + j] = whole.T
    acc[...] = jnp.zeros_like(acc)
    count = live[0]

    def step(turn, carry):
        terms = []
        for u in range(group):
            k = turn * group + u
            terms.append(jnp.dot(turned[dst[k]], adj[k], preferred_element_type=F32))
        for u in range(group):
            k = turn * group + u
            s = jnp.where(k < count, src[k], slots)
            acc[s] += terms[u]
        return carry

    lax.fori_loop(0, (count + group - 1) // group, step, 0)
    total = jnp.zeros((hidden, hidden), F32)
    for s in range(slots):
        term = acc[s]
        total += jnp.dot(term.astype(BF16), raw[s], preferred_element_type=F32)
        back = term.T.astype(BF16)
        for q in range(planes):
            out[s // out_slots * planes + q, s % out_slots] = back[
                q * width : (q + 1) * width
            ]
    w_part[...] = total.T


def last_kernel(ids, got, grad_pre, w_self, w_msg, out, agg):
    blocks, width, hidden = grad_pre.shape
    devices, per_owner = got.shape[:2]
    agg[...] = jnp.zeros_like(agg)
    for i in range(devices):
        for j in range(per_owner):
            agg[ids[i * per_owner + j]] += got[i, j].astype(F32)
    grad_msg = agg[...].reshape(blocks * width, hidden).astype(BF16)
    turn = (((1,), (1,)), ((), ()))
    total = lax.dot_general(
        grad_pre[...].reshape(blocks * width, hidden),
        w_self[...],
        turn,
        preferred_element_type=F32,
    ) + lax.dot_general(grad_msg, w_msg[...], turn, preferred_element_type=F32)
    out[...] = total.astype(BF16).reshape(blocks, width, hidden)


def shape(dims, dtype):
    return jax.ShapeDtypeStruct(dims, dtype)


def body(
    node_feat, cotangent, w_msg, w_self, adjacency, edge_src, edge_dst, send_src, recv_dst, live
):
    block = adjacency.shape[-1]
    hidden = node_feat.shape[1]
    blocks = node_feat.shape[0] // block
    peers = lax.axis_size("edge")
    planes = lax.axis_size("feat")
    devices = peers * planes
    width = block // planes
    n_send = send_src.shape[-1]
    n_recv = recv_dst.shape[-1]
    adj = adjacency.reshape(-1, block, block)
    src = edge_src.reshape(-1)
    dst = edge_dst.reshape(-1)
    count = live.reshape(1)
    group = math.gcd(4, adj.shape[0])
    me = lax.axis_index("feat").reshape(1).astype(jnp.int32)
    params = pltpu.CompilerParams(vmem_limit_bytes=32 * 2**20)

    ids = jnp.concatenate([send_src.reshape(peers, n_send), recv_dst.reshape(peers, n_recv)], 1)
    ids = gather_feat(ids).transpose(1, 0, 2)
    send_all = ids[:, :, :n_send].reshape(-1)
    recv_all = ids[:, :, n_send:].reshape(-1)

    outgoing = pl.pallas_call(
        pick_kernel,
        out_shape=shape((peers * n_send, block, hidden), BF16),
        in_specs=[SMEM, VMEM],
        out_specs=VMEM,
        compiler_params=params,
        name="pick_rows",
    )(send_src.reshape(-1), node_feat.reshape(blocks, block, hidden))
    raw = lax.all_to_all(outgoing, "edge", 0, 0, tiled=True)

    partials = pl.pallas_call(
        functools.partial(forward_kernel, group),
        out_shape=shape((devices, n_recv, width, hidden), BF16),
        in_specs=[SMEM] * 3 + [VMEM] * 3,
        out_specs=VMEM,
        scratch_shapes=[
            pltpu.VMEM((peers * n_send, block, hidden), BF16),
            pltpu.VMEM((peers * n_recv + 1, block, hidden), F32),
        ],
        compiler_params=params,
        name="edge_forward",
    )(count, src, dst, raw, w_msg, adj)
    got = lax.all_to_all(partials, BOTH, 0, 0, tiled=True)

    quarter = shape((blocks, width, hidden), BF16)
    out_part, grad_pre, grad_out, wself_part = pl.pallas_call(
        owner_kernel,
        out_shape=(
            quarter,
            quarter,
            shape((devices, n_recv, width, hidden), BF16),
            shape((hidden, hidden), F32),
        ),
        in_specs=[SMEM] * 2 + [VMEM] * 4,
        out_specs=(VMEM,) * 4,
        scratch_shapes=[
            pltpu.VMEM((blocks, width, hidden), F32),
            pltpu.VMEM((blocks, width, hidden), BF16),
        ],
        compiler_params=params,
        name="owner_dense",
    )(
        me,
        recv_all,
        got,
        node_feat.reshape(blocks, planes, width, hidden),
        cotangent.reshape(blocks, planes, width, hidden),
        w_self,
    )
    grad_in = lax.all_to_all(grad_out, BOTH, 0, 0, tiled=True)
    out_feat = gather_feat(out_part).transpose(1, 0, 2, 3).reshape(-1, hidden)

    grad_partials, wmsg_part = pl.pallas_call(
        functools.partial(backward_kernel, group),
        out_shape=(
            shape((devices, n_send, width, hidden), BF16),
            shape((hidden, hidden), F32),
        ),
        in_specs=[SMEM] * 3 + [VMEM] * 3,
        out_specs=(VMEM,) * 2,
        scratch_shapes=[
            pltpu.VMEM((peers * n_recv, hidden, block), BF16),
            pltpu.VMEM((peers * n_send + 1, hidden, block), F32),
        ],
        compiler_params=params,
        name="edge_backward",
    )(count, src, dst, grad_in, raw, adj)
    grad_back = lax.all_to_all(grad_partials, BOTH, 0, 0, tiled=True)
    grad_wself = sum_all(wself_part)
    grad_wmsg = sum_all(wmsg_part)

    grad_part = pl.pallas_call(
        last_kernel,
        out_shape=quarter,
        in_specs=[SMEM] + [VMEM] * 4,
        out_specs=VMEM,
        scratch_shapes=[pltpu.VMEM((blocks, width, hidden), F32)],
        compiler_params=params,
        name="owner_last",
    )(send_all, grad_back, grad_pre, w_self, w_msg)
    grad_feat = gather_feat(grad_part).transpose(1, 0, 2, 3).reshape(-1, hidden)
    return (out_feat, grad_feat, grad_wmsg, grad_wself)


def solution(mesh):
    in_specs = (
        P("edge", None),
        P("edge", None),
        P(),
        P(),
        P("edge", "feat", None, None, None),
        P("edge", "feat", None),
        P("edge", "feat", None),
        P("edge", "feat", None, None),
        P("edge", "feat", None, None),
        P("edge", "feat"),
    )
    out_specs = (P("edge", None), P("edge", None), P(), P())
    return jax.shard_map(body, mesh=mesh, in_specs=in_specs, out_specs=out_specs, check_vma=False)
```

time: 309 us -> 125 us (0.40)
  waiting for transfers between devices: 178 us -> 52.2 us
  other arithmetic: 20.8 us -> 1.59 us
  between operations: 14.9 us -> 1.46 us
  matrix products: 10.6 us -> 0 us
  Pallas kernels: 0 us -> 10.5 us
  local copies, waits for them, and re-layouts: 17.2 us -> 7.03 us
  starting transfers between devices: 41.6 us -> 33.1 us
  blocking collectives: 26.4 us -> 18.4 us
    psum x2 -> x0, waiting for transfers between devices: 105 us -> none  [the longest x1 68.5 us: body(): grad_wmsg, grad_wself = lax.psum((wmsg_part, wself_part), 'edge')]
    all_to_all x4 -> x3, waiting for transfers between devices: 72.5 us -> 39 us  [the longest x1 14.8 us: body(): grad_back = lax.all_to_all(grad_partials, BOTH, 0, 0, tiled=True)]
    psum x1 -> x0, blocking collectives: 26.4 us -> none  [body(): grad_sum = lax.psum(grad_owner, 'feat')]
    all_to_all x4 -> x3, starting transfers between devices: 41.5 us -> 16.6 us  [the longest x1 7.25 us: body(): raw = lax.all_to_all(outgoing, 'edge', 0, 0, tiled=True)]
    all_to_all x0 -> x1, blocking collectives: none -> 18.4 us  [body(): grad_in = lax.all_to_all(grad_out, BOTH, 0, 0, tiled=True)]
    ppermute x0 -> x16, starting transfers between devices: none -> 16.5 us  [swap(): return lax.ppermute(x, axis, [(j, j ^ bit) for j in range(size)])]
    scatter-add x4 -> x0, other arithmetic: 16.3 us -> none  [the longest x2 12.1 us: one_round(): return running.at[puts].add(terms)]
    ppermute x0 -> x16, waiting for transfers between devices: none -> 13.2 us  [swap(): return lax.ppermute(x, axis, [(j, j ^ bit) for j in range(size)])]
  transfers between devices with their start and end apart: 6 -> 19, of which waited for: 6 -> 12; matrix products, arithmetic and copies ran while one was open for 2% -> 2% of each run, Pallas kernels for 0% -> 1%
where the time goes in v1:
time: 125 us; the launch traced here: 124 us
  waiting for transfers between devices  52.2 us (42%)
  starting transfers between devices  33.1 us (26%)
  blocking collectives  18.4 us (15%)
  Pallas kernels  10.5 us (8%)
  local copies, waits for them, and re-layouts  7.03 us (6%)
  other arithmetic  1.59 us (1%)
  between operations  1.46 us (1%)
    all_to_all x1, blocking collectives, body(): grad_in = lax.all_to_all(grad_out, BOTH, 0, 0, tiled=True)  18.4 us
    ppermute x16, starting transfers between devices, swap(): return lax.ppermute(x, axis, [(j, j ^ bit) for j in range(size)])  16.5 us
    all_to_all x1, waiting for transfers between devices, body(): grad_back = lax.all_to_all(grad_partials, BOTH, 0, 0, tiled=True)  14.8 us
    all_to_all x1, waiting for transfers between devices, body(): raw = lax.all_to_all(outgoing, 'edge', 0, 0, tiled=True)  13.8 us
    ppermute x16, waiting for transfers between devices, swap(): return lax.ppermute(x, axis, [(j, j ^ bit) for j in range(size)])  13.2 us
    all_to_all x1, waiting for transfers between devices, body(): got = lax.all_to_all(partials, BOTH, 0, 0, tiled=True)  10.4 us
    all_to_all x1, starting transfers between devices, body(): raw = lax.all_to_all(outgoing, 'edge', 0, 0, tiled=True)  7.25 us
    all_to_all x1, starting transfers between devices, body(): got = lax.all_to_all(partials, BOTH, 0, 0, tiled=True)  4.99 us
  transfers between devices with their start and end apart: 19, of which 12 were waited for; matrix products, arithmetic and copies ran while one was open for 2% of the time, Pallas kernels for 1%

profile of v1, /device:TPU:0, one launch (start us, length us, event | category | flops | bytes accessed | tf_op | source)
XLA Modules:
  0.0 124.2 jit_solution(12255678612047400008)
XLA Ops:
  0.6 0.9 copy.18
  1.6 1.0 copy-done.1
  2.7 1.4 %pick_rows.1 = bf16[16,128,128]{2,1,0:T(8,128)(2,1)} custom-call(s32[16]{0:T(128)S(1)} %reshape.60.ids, bf16[16,128,128]{2,1,0:T(8,128)(2,1)S(1)} %bitcast.28), custom_call_target="tpu_custom_call" | custom-call | tf_op jit(solution)/shard_map/pick_rows/pallas_call | solution.py:204
  4.0 7.3 %all-to-all-start = ((bf16[16,128,128]{2,1,0:T(8,128)(2,1)}), bf16[16,128,128]{2,1,0:T(8,128)(2,1)S(1)}, u32[]{:S(2)}, u32[]{:S(2)}) async-start(bf16[16,128,128]{2,1,0:T(8,128)(2,1)} %pick_rows.1), calls=%async_computation | async-start | bytes 1048576 | tf_op jit(solution)/shard_map/all_to_all | solution.py:212
  12.0 13.8 %all-to-all-done.raw = bf16[16,128,128]{2,1,0:T(8,128)(2,1)S(1)} async-done(((bf16[16,128,128]{2,1,0:T(8,128)(2,1)}), bf16[16,128,128]{2,1,0:T(8,128)(2,1)S(1)}, u32[]{:S(2)}, u32[]{:S(2)}) %all-to-all-start) | async-done | bytes 524320 | tf_op jit(solution)/shard_map/all_to_all | solution.py:212
  25.8 0.7 copy-done.4
  26.6 3.3 %edge_forward.1 = bf16[32,2,32,128]{3,2,1,0:T(8,128)(2,1)} custom-call(s32[1]{0:T(128)} %bitcast.24.live, s32[64]{0:T(128)S(1)} %bitcast.35, s32[64]{0:T(128)S(1)} %bitcast.37, bf16[16,128,128]{2,1,0:T(8,128)(2,1)S(1)} %all-to-all-done.raw, bf16[128,128]{1,0:T(8,128)(2,1)S(1)} %copy-done.4, bf16[64,128,128]{2,1,0:T(8,128)(2,1)S(1)} %bitcast.26), custom_call_target="tpu_custom_call" | custom-call | tf_op jit(solution)/shard_map/edge_forward/pallas_call | solution.py:214
  29.9 5.0 %all-to-all-start.1 = ((bf16[32,2,32,128]{3,2,1,0:T(8,128)(2,1)}), bf16[32,2,32,128]{3,2,1,0:T(8,128)(2,1)S(1)}, u32[]{:S(2)}, u32[]{:S(2)}) async-start(bf16[32,2,32,128]{3,2,1,0:T(8,128)(2,1)} %edge_forward.1), calls=%async_computation.1 | async-start | bytes 1048576 | tf_op jit(solution)/shard_map/all_to_all | solution.py:226
  34.9 0.3 collective-permute-start
  35.3 0.9 collective-permute-done
  36.2 1.8 %collective-permute-start.1 = (s32[2,8,4]{1,2,0:T(4,128)S(1)}, s32[2,8,4]{1,2,0:T(4,128)S(1)}, u32[]{:S(2)}, u32[]{:S(2)}) collective-permute-start(s32[2,8,4]{1,2,0:T(4,128)S(1)} %add_select_fusion.1), channel_id=1, source_target_pairs={{0,2},{1,3},{2,0},{3,1},{4,6},{5,7},{6,4},{7,5},{8,10},{9,11},{10,... | collective-permute-start | bytes 776 | tf_op jit(solution)/shard_map/ppermute | solution.py:24
  37.9 1.8 %collective-permute-done.1 = s32[2,8,4]{1,2,0:T(4,128)S(1)} collective-permute-done((s32[2,8,4]{1,2,0:T(4,128)S(1)}, s32[2,8,4]{1,2,0:T(4,128)S(1)}, u32[]{:S(2)}, u32[]{:S(2)}) %collective-permute-start.1) | collective-permute-done | bytes 288 | tf_op jit(solution)/shard_map/ppermute | solution.py:24
  39.8 0.1 copy.17
  39.9 0.1 reshape.56.ids
  40.0 10.4 %all-to-all-done.1.got = bf16[32,2,32,128]{3,2,1,0:T(8,128)(2,1)S(1)} async-done(((bf16[32,2,32,128]{3,2,1,0:T(8,128)(2,1)}), bf16[32,2,32,128]{3,2,1,0:T(8,128)(2,1)S(1)}, u32[]{:S(2)}, u32[]{:S(2)}) %all-to-all-start.1) | async-done | bytes 524320 | tf_op jit(solution)/shard_map/all_to_all | solution.py:226
  50.5 1.0 copy-done.2
  51.5 1.0 copy-done.3
  52.5 1.2 owner_dense.1
  53.8 18.4 %all_to_all.20.got = bf16[32,2,32,128]{3,2,1,0:T(8,128)(2,1)S(1)} all-to-all(bf16[32,2,32,128]{3,2,1,0:T(8,128)(2,1)S(1)} %get-tuple-element.11), channel_id=1, replica_groups=mesh['edge'=8,'feat'=4] {'edge','feat'}, dimensions={0} | all-to-all | bytes 1048576 | tf_op jit(solution)/shard_map/all_to_all | solution.py:253
  72.2 3.5 %edge_backward.1 = (bf16[32,2,32,128]{3,2,1,0:T(8,128)(2,1)}, f32[128,128]{1,0:T(8,128)S(1)}) custom-call(s32[1]{0:T(128)} %bitcast.25.live, s32[64]{0:T(128)S(1)} %bitcast.36, s32[64]{0:T(128)S(1)} %bitcast.38, bf16[32,2,32,128]{3,2,1,0:T(8,128)(2,1)S(1)} %all_to_all.20.got, bf16[16,128,128]{2,1,0:T(8,128)(2,1)S(1)} %all-to-all-done.raw, ...), custom_call_target="tpu_custom_call" | custom-call | tf_op jit(solution)/shard_map/edge_backward/pallas_call | solution.py:256
  75.7 4.4 %all-to-all-start.3 = ((bf16[32,2,32,128]{3,2,1,0:T(8,128)(2,1)}), bf16[32,2,32,128]{3,2,1,0:T(8,128)(2,1)S(1)}, u32[]{:S(2)}, u32[]{:S(2)}) async-start(bf16[32,2,32,128]{3,2,1,0:T(8,128)(2,1)} %get-tuple-element.12), calls=%async_computation.3 | async-start | bytes 1048576 | tf_op jit(solution)/shard_map/all_to_all | solution.py:271
  80.1 0.3 collective-permute-start.2
  80.4 0.3 collective-permute-start.11
  80.7 0.1 copy.20
  80.8 0.1 reshape.66.ids
  80.9 14.8 %all-to-all-done.3.got = bf16[32,2,32,128]{3,2,1,0:T(8,128)(2,1)S(1)} async-done(((bf16[32,2,32,128]{3,2,1,0:T(8,128)(2,1)}), bf16[32,2,32,128]{3,2,1,0:T(8,128)(2,1)S(1)}, u32[]{:S(2)}, u32[]{:S(2)}) %all-to-all-start.3) | async-done | bytes 524320 | tf_op jit(solution)/shard_map/all_to_all | solution.py:271
  95.7 1.0 owner_last.1
  96.8 1.4 %collective-permute-start.12 = (f32[128,128]{1,0:T(8,128)S(1)}, f32[128,128]{1,0:T(8,128)S(1)}, u32[]{:S(2)}, u32[]{:S(2)}) collective-permute-start(f32[128,128]{1,0:T(8,128)S(1)} %add.35), channel_id=1, source_target_pairs={{0,2},{1,3},{2,0},{3,1},{4,6},{5,7},{6,4},{7,5},{8,10},{9,11},{10,... | collective-permute-start | bytes 196616 | tf_op jit(solution)/shard_map/ppermute | solution.py:24
  98.2 1.0 collective-permute-start.3
  99.2 2.2 %collective-permute-done.12 = f32[128,128]{1,0:T(8,128)S(1)} collective-permute-done((f32[128,128]{1,0:T(8,128)S(1)}, f32[128,128]{1,0:T(8,128)S(1)}, u32[]{:S(2)}, u32[]{:S(2)}) %collective-permute-start.12) | collective-permute-done | bytes 65568 | tf_op jit(solution)/shard_map/ppermute | solution.py:24
  101.3 1.5 %collective-permute-start.13 = (f32[128,128]{1,0:T(8,128)S(1)}, f32[128,128]{1,0:T(8,128)S(1)}, u32[]{:S(2)}, u32[]{:S(2)}) collective-permute-start(f32[128,128]{1,0:T(8,128)S(1)} %add.36), channel_id=1, source_target_pairs={{0,4},{4,0},{8,12},{12,8},{16,20},{20,16},{24,28},{28,24},{1,5},{5... | collective-permute-start | bytes 196616 | tf_op jit(solution)/shard_map/ppermute | solution.py:24
  102.8 1.5 %collective-permute-start.7 = (f32[128,128]{1,0:T(8,128)S(1)}, f32[128,128]{1,0:T(8,128)S(1)}, u32[]{:S(2)}, u32[]{:S(2)}) collective-permute-start(f32[128,128]{1,0:T(8,128)S(1)} %add.30), channel_id=1, source_target_pairs={{0,2},{1,3},{2,0},{3,1},{4,6},{5,7},{6,4},{7,5},{8,10},{9,11},{10,... | collective-permute-start | bytes 196616 | tf_op jit(solution)/shard_map/ppermute | solution.py:24
  104.3 0.7 collective-permute-start.5
  105.0 0.7 collective-permute-done.13
  105.7 1.7 %collective-permute-start.14 = (f32[128,128]{1,0:T(8,128)S(1)}, f32[128,128]{1,0:T(8,128)S(1)}, u32[]{:S(2)}, u32[]{:S(2)}) collective-permute-start(f32[128,128]{1,0:T(8,128)S(1)} %add.37), channel_id=1, source_target_pairs={{0,8},{4,12},{8,0},{12,4},{16,24},{20,28},{24,16},{28,20},{1,9},{5... | collective-permute-start | bytes 196616 | tf_op jit(solution)/shard_map/ppermute | solution.py:24
  107.4 1.3 %collective-permute-done.7 = f32[128,128]{1,0:T(8,128)S(1)} collective-permute-done((f32[128,128]{1,0:T(8,128)S(1)}, f32[128,128]{1,0:T(8,128)S(1)}, u32[]{:S(2)}, u32[]{:S(2)}) %collective-permute-start.7) | collective-permute-done | bytes 65568 | tf_op jit(solution)/shard_map/ppermute | solution.py:24
  108.7 1.4 %collective-permute-start.8 = (f32[128,128]{1,0:T(8,128)S(1)}, f32[128,128]{1,0:T(8,128)S(1)}, u32[]{:S(2)}, u32[]{:S(2)}) collective-permute-start(f32[128,128]{1,0:T(8,128)S(1)} %add.31), channel_id=1, source_target_pairs={{0,4},{4,0},{8,12},{12,8},{16,20},{20,16},{24,28},{28,24},{1,5},{5... | collective-permute-start | bytes 196616 | tf_op jit(solution)/shard_map/ppermute | solution.py:24
  110.2 1.7 %collective-permute-start.15 = (f32[128,128]{1,0:T(8,128)S(1)}, f32[128,128]{1,0:T(8,128)S(1)}, u32[]{:S(2)}, u32[]{:S(2)}) collective-permute-start(f32[128,128]{1,0:T(8,128)S(1)} %add.38), channel_id=1, source_target_pairs={{0,16},{4,20},{8,24},{12,28},{16,0},{20,4},{24,8},{28,12},{1,17},{... | collective-permute-start | bytes 196616 | tf_op jit(solution)/shard_map/ppermute | solution.py:24
  111.9 1.1 collective-permute-done.8
  113.1 1.3 %collective-permute-start.9 = (f32[128,128]{1,0:T(8,128)S(1)}, f32[128,128]{1,0:T(8,128)S(1)}, u32[]{:S(2)}, u32[]{:S(2)}) collective-permute-start(f32[128,128]{1,0:T(8,128)S(1)} %add.32), channel_id=1, source_target_pairs={{0,8},{4,12},{8,0},{12,4},{16,24},{20,28},{24,16},{28,20},{1,9},{5... | collective-permute-start | bytes 196616 | tf_op jit(solution)/shard_map/ppermute | solution.py:24
  114.4 1.1 collective-permute-done.15
  115.5 0.6 add.39
  116.2 1.3 %collective-permute-done.9 = f32[128,128]{1,0:T(8,128)S(1)} collective-permute-done((f32[128,128]{1,0:T(8,128)S(1)}, f32[128,128]{1,0:T(8,128)S(1)}, u32[]{:S(2)}, u32[]{:S(2)}) %collective-permute-start.9) | collective-permute-done | bytes 65568 | tf_op jit(solution)/shard_map/ppermute | solution.py:24
  117.4 1.5 %collective-permute-start.10 = (f32[128,128]{1,0:T(8,128)S(1)}, f32[128,128]{1,0:T(8,128)S(1)}, u32[]{:S(2)}, u32[]{:S(2)}) collective-permute-start(f32[128,128]{1,0:T(8,128)S(1)} %add.33), channel_id=1, source_target_pairs={{0,16},{4,20},{8,24},{12,28},{16,0},{20,4},{24,8},{28,12},{1,17},{... | collective-permute-start | bytes 196616 | tf_op jit(solution)/shard_map/ppermute | solution.py:24
  119.0 0.9 copy.19
  119.9 2.8 %collective-permute-done.10 = f32[128,128]{1,0:T(8,128)S(1)} collective-permute-done((f32[128,128]{1,0:T(8,128)S(1)}, f32[128,128]{1,0:T(8,128)S(1)}, u32[]{:S(2)}, u32[]{:S(2)}) %collective-permute-start.10) | collective-permute-done | bytes 65568 | tf_op jit(solution)/shard_map/ppermute | solution.py:24
  122.7 0.6 add.34
  123.4 0.9 copy.21
  (44 shorter events, 0.5 us)
Async XLA Ops:
  0.6 25.2 %copy-start = (bf16[1,1,64,128,128]{4,3,2,1,0:T(8,128)(2,1)S(1)}, bf16[1,1,64,128,128]{4,3,2,1,0:T(8,128)(2,1)}, u32[]{:S(2)}) copy-start(bf16[1,1,64,128,128]{4,3,2,1,0:T(8,128)(2,1)} %param.14) | copy-start | bytes 6291460
  1.6 1.0 copy-start.1
  2.7 23.1 %copy-start.7 = (s32[1,1,64]{2,1,0:T(1,128)S(1)}, s32[1,1,64]{2,1,0:T(1,128)}, u32[]{:S(2)}) copy-start(s32[1,1,64]{2,1,0:T(1,128)} %param.15) | copy-start | bytes 772
  2.7 23.1 %copy-start.8 = (s32[1,1,64]{2,1,0:T(1,128)S(1)}, s32[1,1,64]{2,1,0:T(1,128)}, u32[]{:S(2)}) copy-start(s32[1,1,64]{2,1,0:T(1,128)} %param.16) | copy-start | bytes 772
  4.0 21.7 %all-to-all-start = ((bf16[16,128,128]{2,1,0:T(8,128)(2,1)}), bf16[16,128,128]{2,1,0:T(8,128)(2,1)S(1)}, u32[]{:S(2)}, u32[]{:S(2)}) async-start(bf16[16,128,128]{2,1,0:T(8,128)(2,1)} %pick_rows.1), calls=%async_computation | async-start | bytes 1048576 | tf_op jit(solution)/shard_map/all_to_all | solution.py:212
  25.8 0.8 copy-start.4
  26.6 8.4 %copy-start.9 = (s32[1,1,8,2]{2,3,1,0:T(2,128)S(1)}, s32[1,1,8,2]{2,3,1,0:T(2,128)}, u32[]{:S(2)}) copy-start(s32[1,1,8,2]{2,3,1,0:T(2,128)} %param.17) | copy-start | bytes 196
  26.6 8.4 %copy-start.10 = (s32[1,1,8,2]{2,3,1,0:T(2,128)S(1)}, s32[1,1,8,2]{2,3,1,0:T(2,128)}, u32[]{:S(2)}) copy-start(s32[1,1,8,2]{2,3,1,0:T(2,128)} %param.18) | copy-start | bytes 196
  26.6 23.9 %copy-start.6 = (bf16[128,128]{1,0:T(8,128)(2,1)S(1)}, bf16[128,128]{1,0:T(8,128)(2,1)}, u32[]{:S(2)}) copy-start(bf16[128,128]{1,0:T(8,128)(2,1)} %w_self.3) | copy-start | bytes 98308
  29.9 20.5 %all-to-all-start.1 = ((bf16[32,2,32,128]{3,2,1,0:T(8,128)(2,1)}), bf16[32,2,32,128]{3,2,1,0:T(8,128)(2,1)S(1)}, u32[]{:S(2)}, u32[]{:S(2)}) async-start(bf16[32,2,32,128]{3,2,1,0:T(8,128)(2,1)} %edge_forward.1), calls=%async_computation.1 | async-start | bytes 1048576 | tf_op jit(solution)/shard_map/all_to_all | solution.py:226
  34.9 1.2 collective-permute-start
  36.2 3.6 %collective-permute-start.1 = (s32[2,8,4]{1,2,0:T(4,128)S(1)}, s32[2,8,4]{1,2,0:T(4,128)S(1)}, u32[]{:S(2)}, u32[]{:S(2)}) collective-permute-start(s32[2,8,4]{1,2,0:T(4,128)S(1)} %add_select_fusion.1), channel_id=1, source_target_pairs={{0,2},{1,3},{2,0},{3,1},{4,6},{5,7},{6,4},{7,5},{8,10},{9,11},{10,... | collective-permute-start | bytes 776 | tf_op jit(solution)/shard_map/ppermute | solution.py:24
  50.5 1.0 copy-start.2
  51.5 1.0 copy-start.3
  72.2 23.4 %copy-start.5 = (bf16[128,128]{1,0:T(8,128)(2,1)S(1)}, bf16[128,128]{1,0:T(8,128)(2,1)}, u32[]{:S(2)}) copy-start(bf16[128,128]{1,0:T(8,128)(2,1)} %w_msg.3) | copy-start | bytes 98308
  75.7 19.9 %all-to-all-start.3 = ((bf16[32,2,32,128]{3,2,1,0:T(8,128)(2,1)}), bf16[32,2,32,128]{3,2,1,0:T(8,128)(2,1)S(1)}, u32[]{:S(2)}, u32[]{:S(2)}) async-start(bf16[32,2,32,128]{3,2,1,0:T(8,128)(2,1)} %get-tuple-element.12), calls=%async_computation.3 | async-start | bytes 1048576 | tf_op jit(solution)/shard_map/all_to_all | solution.py:271
  80.1 18.0 %collective-permute-start.2 = (bf16[1,16,32,128]{3,2,1,0:T(8,128)(2,1)S(1)}, bf16[1,16,32,128]{3,2,1,0:T(8,128)(2,1)S(1)}, u32[]{:S(2)}, u32[]{:S(2)}) collective-permute-start(bf16[1,16,32,128]{3,2,1,0:T(8,128)(2,1)S(1)} %bitcast.33), channel_id=1, source_target_pairs={{0,1},{1,0},{2,3},{3,2},{4,5},{5,4},{6,7},{7,6},{8,9},{9,8},{10,11... | collective-permute-start | bytes 393224 | tf_op jit(solution)/shard_map/ppermute | solution.py:24
  80.4 16.3 %collective-permute-start.11 = (f32[128,128]{1,0:T(8,128)S(1)}, f32[128,128]{1,0:T(8,128)S(1)}, u32[]{:S(2)}, u32[]{:S(2)}) collective-permute-start(f32[128,128]{1,0:T(8,128)S(1)} %get-tuple-element.15), channel_id=1, source_target_pairs={{0,1},{1,0},{2,3},{3,2},{4,5},{5,4},{6,7},{7,6},{8,9},{9,8},{10,11... | collective-permute-start | bytes 196616 | tf_op jit(solution)/shard_map/ppermute | solution.py:24
  96.7 7.6 %collective-permute-start.4 = (bf16[1,16,32,128]{3,2,1,0:T(8,128)(2,1)S(1)}, bf16[1,16,32,128]{3,2,1,0:T(8,128)(2,1)S(1)}, u32[]{:S(2)}, u32[]{:S(2)}) collective-permute-start(bf16[1,16,32,128]{3,2,1,0:T(8,128)(2,1)S(1)} %bitcast.30), channel_id=1, source_target_pairs={{0,1},{1,0},{2,3},{3,2},{4,5},{5,4},{6,7},{7,6},{8,9},{9,8},{10,11... | collective-permute-start | bytes 393224 | tf_op jit(solution)/shard_map/ppermute | solution.py:24
  96.8 4.5 %collective-permute-start.12 = (f32[128,128]{1,0:T(8,128)S(1)}, f32[128,128]{1,0:T(8,128)S(1)}, u32[]{:S(2)}, u32[]{:S(2)}) collective-permute-start(f32[128,128]{1,0:T(8,128)S(1)} %add.35), channel_id=1, source_target_pairs={{0,2},{1,3},{2,0},{3,1},{4,6},{5,7},{6,4},{7,5},{8,10},{9,11},{10,... | collective-permute-start | bytes 196616 | tf_op jit(solution)/shard_map/ppermute | solution.py:24
  98.1 4.7 %collective-permute-start.6 = (f32[128,128]{1,0:T(8,128)S(1)}, f32[128,128]{1,0:T(8,128)S(1)}, u32[]{:S(2)}, u32[]{:S(2)}) collective-permute-start(f32[128,128]{1,0:T(8,128)S(1)} %get-tuple-element.14), channel_id=1, source_target_pairs={{0,1},{1,0},{2,3},{3,2},{4,5},{5,4},{6,7},{7,6},{8,9},{9,8},{10,11... | collective-permute-start | bytes 196616 | tf_op jit(solution)/shard_map/ppermute | solution.py:24
  98.2 20.8 %collective-permute-start.3 = (bf16[2,16,32,128]{3,2,1,0:T(8,128)(2,1)S(1)}, bf16[2,16,32,128]{3,2,1,0:T(8,128)(2,1)S(1)}, u32[]{:S(2)}, u32[]{:S(2)}) collective-permute-start(bf16[2,16,32,128]{3,2,1,0:T(8,128)(2,1)S(1)} %maximum_select_fusion.2), channel_id=1, source_target_pairs={{0,2},{1,3},{2,0},{3,1},{4,6},{5,7},{6,4},{7,5},{8,10},{9,11},{10,... | collective-permute-start | bytes 786440 | tf_op jit(solution)/shard_map/ppermute | solution.py:24
  101.3 4.3 %collective-permute-start.13 = (f32[128,128]{1,0:T(8,128)S(1)}, f32[128,128]{1,0:T(8,128)S(1)}, u32[]{:S(2)}, u32[]{:S(2)}) collective-permute-start(f32[128,128]{1,0:T(8,128)S(1)} %add.36), channel_id=1, source_target_pairs={{0,4},{4,0},{8,12},{12,8},{16,20},{20,16},{24,28},{28,24},{1,5},{5... | collective-permute-start | bytes 196616 | tf_op jit(solution)/shard_map/ppermute | solution.py:24
  102.8 5.9 %collective-permute-start.7 = (f32[128,128]{1,0:T(8,128)S(1)}, f32[128,128]{1,0:T(8,128)S(1)}, u32[]{:S(2)}, u32[]{:S(2)}) collective-permute-start(f32[128,128]{1,0:T(8,128)S(1)} %add.30), channel_id=1, source_target_pairs={{0,2},{1,3},{2,0},{3,1},{4,6},{5,7},{6,4},{7,5},{8,10},{9,11},{10,... | collective-permute-start | bytes 196616 | tf_op jit(solution)/shard_map/ppermute | solution.py:24
  104.3 19.0 %collective-permute-start.5 = (bf16[2,16,32,128]{3,2,1,0:T(8,128)(2,1)S(1)}, bf16[2,16,32,128]{3,2,1,0:T(8,128)(2,1)S(1)}, u32[]{:S(2)}, u32[]{:S(2)}) collective-permute-start(bf16[2,16,32,128]{3,2,1,0:T(8,128)(2,1)S(1)} %maximum_select_fusion.3), channel_id=1, source_target_pairs={{0,2},{1,3},{2,0},{3,1},{4,6},{5,7},{6,4},{7,5},{8,10},{9,11},{10,... | collective-permute-start | bytes 786440 | tf_op jit(solution)/shard_map/ppermute | solution.py:24
  105.7 4.5 %collective-permute-start.14 = (f32[128,128]{1,0:T(8,128)S(1)}, f32[128,128]{1,0:T(8,128)S(1)}, u32[]{:S(2)}, u32[]{:S(2)}) collective-permute-start(f32[128,128]{1,0:T(8,128)S(1)} %add.37), channel_id=1, source_target_pairs={{0,8},{4,12},{8,0},{12,4},{16,24},{20,28},{24,16},{28,20},{1,9},{5... | collective-permute-start | bytes 196616 | tf_op jit(solution)/shard_map/ppermute | solution.py:24
  108.7 4.3 %collective-permute-start.8 = (f32[128,128]{1,0:T(8,128)S(1)}, f32[128,128]{1,0:T(8,128)S(1)}, u32[]{:S(2)}, u32[]{:S(2)}) collective-permute-start(f32[128,128]{1,0:T(8,128)S(1)} %add.31), channel_id=1, source_target_pairs={{0,4},{4,0},{8,12},{12,8},{16,20},{20,16},{24,28},{28,24},{1,5},{5... | collective-permute-start | bytes 196616 | tf_op jit(solution)/shard_map/ppermute | solution.py:24
  110.2 5.3 %collective-permute-start.15 = (f32[128,128]{1,0:T(8,128)S(1)}, f32[128,128]{1,0:T(8,128)S(1)}, u32[]{:S(2)}, u32[]{:S(2)}) collective-permute-start(f32[128,128]{1,0:T(8,128)S(1)} %add.38), channel_id=1, source_target_pairs={{0,16},{4,20},{8,24},{12,28},{16,0},{20,4},{24,8},{28,12},{1,17},{... | collective-permute-start | bytes 196616 | tf_op jit(solution)/shard_map/ppermute | solution.py:24
  113.1 4.3 %collective-permute-start.9 = (f32[128,128]{1,0:T(8,128)S(1)}, f32[128,128]{1,0:T(8,128)S(1)}, u32[]{:S(2)}, u32[]{:S(2)}) collective-permute-start(f32[128,128]{1,0:T(8,128)S(1)} %add.32), channel_id=1, source_target_pairs={{0,8},{4,12},{8,0},{12,4},{16,24},{20,28},{24,16},{28,20},{1,9},{5... | collective-permute-start | bytes 196616 | tf_op jit(solution)/shard_map/ppermute | solution.py:24
  117.4 5.2 %collective-permute-start.10 = (f32[128,128]{1,0:T(8,128)S(1)}, f32[128,128]{1,0:T(8,128)S(1)}, u32[]{:S(2)}, u32[]{:S(2)}) collective-permute-start(f32[128,128]{1,0:T(8,128)S(1)} %add.33), channel_id=1, source_target_pairs={{0,16},{4,20},{8,24},{12,28},{16,0},{20,4},{24,8},{28,12},{1,17},{... | collective-permute-start | bytes 196616 | tf_op jit(solution)/shard_map/ppermute | solution.py:24

commit v2 on v1

v2 whole, which is shorter than its diff:
```python
import functools
import math

import jax
import jax.numpy as jnp
from jax import lax
from jax.experimental import pallas as pl
from jax.experimental.pallas import tpu as pltpu
from jax.sharding import PartitionSpec as P

BOTH = ("edge", "feat")
F32 = jnp.float32
BF16 = jnp.bfloat16
VMEM = pl.BlockSpec(memory_space=pltpu.VMEM)
SMEM = pl.BlockSpec(memory_space=pltpu.SMEM)
HBM = pl.BlockSpec(memory_space=pltpu.HBM)
ANY = pl.BlockSpec(memory_space=pl.ANY)


def is_pow2(n):
    return n & (n - 1) == 0


def swap(x, axis, bit):
    size = lax.axis_size(axis)
    return lax.ppermute(x, axis, [(j, j ^ bit) for j in range(size)])


def gather_feat(x):
    size = lax.axis_size("feat")
    if not is_pow2(size):
        return lax.all_gather(x, "feat", axis=0)
    me = lax.axis_index("feat")
    held = x[None]
    bit = 1
    while bit < size:
        other = swap(held, "feat", bit)
        mine_low = (me & bit) == 0
        held = jnp.where(
            mine_low, jnp.concatenate([held, other], 0), jnp.concatenate([other, held], 0)
        )
        bit *= 2
    return held


def pieces_feat(x, beside=None):
    bit = lax.axis_size("feat") // 2
    held = {0: x}
    other = None if beside is None else swap_all(beside, 1)
    while bit:
        held.update({m | bit: swap(v, "feat", bit) for m, v in held.items()})
        if other is not None:
            held, other = lax.optimization_barrier((held, other))
        bit //= 2
    return [held[m] for m in sorted(held)], other


def join_kernel(planes, me, *refs):
    parts, refs = refs[:planes], refs[planes:]
    halves, (out, *sums, sems) = (refs[:2], refs[2:]) if len(refs) > 2 else ((), refs)
    copies = [
        pltpu.make_async_copy(part, out.at[:, me[0] ^ m], sems.at[m])
        for m, part in enumerate(parts)
    ]
    for n, total in enumerate(sums):
        rows = total.shape[1]
        copies += [
            pltpu.make_async_copy(
                half.at[n * rows : (n + 1) * rows],
                total.at[(me[0] & 1) ^ m],
                sems.at[planes + 2 * n + m],
            )
            for m, half in enumerate(halves)
        ]
    for copy in copies:
        copy.start()
    for copy in copies:
        copy.wait()


def join_feat(x, me, params, sums=None):
    blocks, width, hidden = x.shape
    planes = lax.axis_size("feat")
    pieces, other = pieces_feat(x, sums)
    out_shape = [pltpu.HBM((blocks, planes, width, hidden), BF16)]
    if sums is not None:
        count = 2 * sums.shape[0] // hidden
        out_shape += [pltpu.HBM((2, hidden // 2, hidden), F32)] * count
        pieces = pieces + [sums, other]
    joined = pl.pallas_call(
        functools.partial(join_kernel, planes),
        out_shape=out_shape,
        in_specs=[SMEM] + [VMEM] * len(pieces),
        out_specs=[HBM] * len(out_shape),
        scratch_shapes=[pltpu.SemaphoreType.DMA((planes + 2 * len(out_shape),))],
        compiler_params=params,
        name="join_rows",
    )(me, *pieces)
    return [v.reshape(-1, hidden) for v in joined]


def stages_of(count):
    bits = [1 << n for n in range(count.bit_length() - 1)]
    return [bits[:1]] + [bits[n : n + 2] for n in range(1, len(bits), 2)]


def swap_all(x, mask):
    count = lax.axis_size(BOTH)
    return lax.ppermute(x, BOTH, [(j, j ^ mask) for j in range(count)])


def sum_stage(x, bits):
    terms = {0: x}
    for bit in bits:
        terms.update({m | bit: swap_all(x, m | bit) for m in list(terms)})
    held = [terms[m].astype(F32) for m in sorted(terms)]
    while len(held) > 1:
        held = [held[n] + held[n + 1] for n in range(0, len(held), 2)]
    return held[0]


def split_core(x, me):
    halves = x.reshape(2, -1, x.shape[-1])
    low = (me & 1) == 0
    mine = jnp.where(low, halves[0], halves[1])
    other = jnp.where(low, halves[1], halves[0])
    return mine + swap_all(other, 1)


def pick_kernel(ids, rows, w_msg, w_self, out, w_msg_out, w_self_out, room, sems, out_sems):
    n_send, peers = ids.shape
    count = peers * n_send
    ins = [
        pltpu.make_async_copy(
            rows.at[ids[j, p]], room.at[p * n_send + j], sems.at[p * n_send + j]
        )
        for p in range(peers)
        for j in range(n_send)
    ]
    others = [
        pltpu.make_async_copy(w_msg, w_msg_out, sems.at[count]),
        pltpu.make_async_copy(w_self, w_self_out, sems.at[count + 1]),
    ]
    outs = [pltpu.make_async_copy(room.at[i], out.at[i], out_sems.at[i]) for i in range(count)]
    for copy in ins + others:
        copy.start()
    for one, two in zip(ins, outs):
        one.wait()
        two.start()
    for copy in others + outs:
        copy.wait()


def edge_loop(group, count, adj, held, sems, term, put):
    chunks = sems.shape[0]
    size = held.shape[0] // chunks
    copies = [
        pltpu.make_async_copy(
            adj.at[c * size : (c + 1) * size], held.at[c * size : (c + 1) * size], sems.at[c]
        )
        for c in range(chunks)
    ]

    def start():
        for copy in copies:
            copy.start()

    def run():
        for c, copy in enumerate(copies):
            copy.wait()

            def step(turn, carry, first=c * size):
                ks = [first + turn * group + u for u in range(group)]
                terms = [term(k) for k in ks]
                for k, value in zip(ks, terms):
                    put(k, k < count, value)
                return carry

            left = jnp.clip(count - c * size, 0, size)
            lax.fori_loop(0, (left + group - 1) // group, step, 0)

    return start, run


def send_out(room, out, sems, p, size):
    copy = pltpu.make_async_copy(
        room.at[p * size : (p + 1) * size], out.at[p * size : (p + 1) * size], sems.at[p]
    )
    copy.start()
    return copy


def forward_kernel(
    group,
    live,
    me,
    src,
    dst,
    raw,
    w_msg,
    adj,
    feat,
    cot,
    out,
    feat_out,
    cot_out,
    msgs,
    acc,
    held,
    room,
    sems,
    more_sems,
    out_sems,
):
    slots, block, hidden = raw.shape
    per_owner, width = out.shape[1:3]
    planes = block // width

    def term(k):
        return jnp.dot(held[k], msgs[src[k]], preferred_element_type=F32)

    def put(k, alive, value):
        acc[jnp.where(alive, dst[k], slots)] += value

    start, run = edge_loop(group, live[0], adj, held, sems, term, put)
    start()
    parts = [
        pltpu.make_async_copy(feat.at[:, me[0]], feat_out, more_sems.at[0]),
        pltpu.make_async_copy(cot.at[:, me[0]], cot_out, more_sems.at[1]),
    ]
    for copy in parts:
        copy.start()
    flat = raw[...].reshape(slots * block, hidden)
    msgs[...] = (
        jnp.dot(flat, w_msg[...], preferred_element_type=F32)
        .astype(BF16)
        .reshape(slots, block, hidden)
    )
    acc[...] = jnp.zeros_like(acc)
    run()
    for p in range(out.shape[0] // planes):
        for j in range(per_owner):
            for q in range(planes):
                room[p * planes + q, j] = acc[
                    p * per_owner + j, q * width : (q + 1) * width
                ].astype(BF16)
        parts.append(send_out(room, out, out_sems, p, planes))
    for copy in parts:
        copy.wait()


def owner_kernel(
    ids, got, feat, cot, w_self, out_feat, grad_pre, out, w_part, agg, room, out_sems
):
    blocks, width, hidden = grad_pre.shape
    devices, per_owner = got.shape[:2]
    agg[...] = jnp.zeros_like(agg)
    for i in range(devices):
        for j in range(per_owner):
            agg[ids[i * per_owner + j]] += got[i, j].astype(F32)
    mine = feat[...].reshape(blocks * width, hidden)
    preact = jnp.dot(mine, w_self[...], preferred_element_type=F32)
    preact = preact + agg[...].reshape(blocks * width, hidden)
    sig = jax.nn.sigmoid(preact)
    grad = cot[...].reshape(blocks * width, hidden).astype(F32)
    grad = (grad * sig * (1.0 + preact * (1.0 - sig))).astype(BF16)
    grad_pre[...] = grad.reshape(blocks, width, hidden)
    copies = []
    size = devices // out_sems.shape[0]
    for p in range(out_sems.shape[0]):
        for i in range(p * size, (p + 1) * size):
            for j in range(per_owner):
                room[i, j] = grad_pre[ids[i * per_owner + j]]
        copies.append(send_out(room, out, out_sems, p, size))
    out_feat[...] = (preact * sig).astype(BF16).reshape(blocks, width, hidden)
    w_part[...] = lax.dot_general(
        mine, grad, (((0,), (0,)), ((), ())), preferred_element_type=F32
    )
    for copy in copies:
        copy.wait()


def backward_kernel(
    group, live, src, dst, got, raw, adj, out, w_part, turned, acc, held, room, sems, out_sems
):
    slots, block, hidden = raw.shape
    devices, per_owner, width = got.shape[:3]
    planes = block // width
    out_slots = out.shape[1]

    def term(k):
        return jnp.dot(turned[dst[k]], held[k], preferred_element_type=F32)

    def put(k, alive, value):
        acc[jnp.where(alive, src[k], slots)] += value

    start, run = edge_loop(group, live[0], adj, held, sems, term, put)
    start()
    for p in range(devices // planes):
        for j in range(per_owner):
            whole = jnp.concatenate([got[p * planes + q, j] for q in range(planes)], 0)
            turned[p * per_owner + j] = whole.T
    acc[...] = jnp.zeros_like(acc)
    run()
    copies = []
    for p in range(devices // planes):
        for j in range(out_slots):
            back = acc[p * out_slots + j].T.astype(BF16)
            for q in range(planes):
                room[p * planes + q, j] = back[q * width : (q + 1) * width]
        copies.append(send_out(room, out, out_sems, p, planes))
    total = jnp.zeros((hidden, hidden), F32)
    for s in range(slots):
        total += jnp.dot(acc[s].astype(BF16), raw[s], preferred_element_type=F32)
    w_part[...] = total.T
    for copy in copies:
        copy.wait()


def last_kernel(ids, got, grad_pre, w_self, w_msg, out, agg):
    blocks, width, hidden = grad_pre.shape
    devices, per_owner = got.shape[:2]
    agg[...] = jnp.zeros_like(agg)
    for i in range(devices):
        for j in range(per_owner):
            agg[ids[i * per_owner + j]] += got[i, j].astype(F32)
    grad_msg = agg[...].reshape(blocks * width, hidden).astype(BF16)
    turn = (((1,), (1,)), ((), ()))
    total = lax.dot_general(
        grad_pre[...].reshape(blocks * width, hidden),
        w_self[...],
        turn,
        preferred_element_type=F32,
    ) + lax.dot_general(grad_msg, w_msg[...], turn, preferred_element_type=F32)
    out[...] = total.astype(BF16).reshape(blocks, width, hidden)


def shape(dims, dtype):
    return jax.ShapeDtypeStruct(dims, dtype)


def in_hbm(x):
    return pltpu.with_memory_space_constraint(x, pltpu.HBM)


def body(
    node_feat, cotangent, w_msg, w_self, adjacency, edge_src, edge_dst, send_src, recv_dst, live
):
    block = adjacency.shape[-1]
    hidden = node_feat.shape[1]
    blocks = node_feat.shape[0] // block
    peers = lax.axis_size("edge")
    planes = lax.axis_size("feat")
    devices = peers * planes
    width = block // planes
    n_send = send_src.shape[-1]
    n_recv = recv_dst.shape[-1]
    adj = in_hbm(adjacency.reshape(-1, block, block))
    src = edge_src.reshape(-1)
    dst = edge_dst.reshape(-1)
    count = live.reshape(1)
    group = math.gcd(4, adj.shape[0])
    me = lax.axis_index("feat").reshape(1).astype(jnp.int32)
    params = pltpu.CompilerParams(vmem_limit_bytes=32 * 2**20)
    stages = stages_of(devices)

    ids = jnp.concatenate([send_src.reshape(peers, n_send), recv_dst.reshape(peers, n_recv)], 1)
    ids = gather_feat(ids).transpose(1, 0, 2)
    send_all = ids[:, :, :n_send].reshape(-1)
    recv_all = ids[:, :, n_send:].reshape(-1)

    wide_feat = in_hbm(node_feat.reshape(blocks, planes, width, hidden))
    wide_cot = in_hbm(cotangent.reshape(blocks, planes, width, hidden))
    square = pltpu.VMEM((hidden, hidden), BF16)
    sum_part = pltpu.VMEM((hidden, hidden), F32)
    quarter = pltpu.VMEM((blocks, width, hidden), BF16)
    rows_out = (peers * n_send, block, hidden)
    recv_out = (devices, n_recv, width, hidden)
    send_out_dims = (devices, n_send, width, hidden)
    out_sems = pltpu.SemaphoreType.DMA((peers,))
    outgoing, w_msg, w_self = pl.pallas_call(
        pick_kernel,
        out_shape=(pltpu.HBM(rows_out, BF16), square, square),
        in_specs=[SMEM] + [HBM] * 3,
        out_specs=(HBM, VMEM, VMEM),
        scratch_shapes=[
            pltpu.VMEM(rows_out, BF16),
            pltpu.SemaphoreType.DMA((peers * n_send + 2,)),
            pltpu.SemaphoreType.DMA((peers * n_send,)),
        ],
        compiler_params=params,
        name="pick_rows",
    )(
        send_src.transpose(0, 1, 3, 2).reshape(n_send, peers),
        in_hbm(node_feat.reshape(blocks, block, hidden)),
        in_hbm(w_msg),
        in_hbm(w_self),
    )
    raw = lax.all_to_all(outgoing, "edge", 0, 0, tiled=True)

    edge_room = pltpu.VMEM(adj.shape, BF16)
    edge_sems = pltpu.SemaphoreType.DMA((math.gcd(4, adj.shape[0] // group),))
    partials, feat_part, cot_part = pl.pallas_call(
        functools.partial(forward_kernel, group),
        out_shape=(pltpu.HBM(recv_out, BF16), quarter, quarter),
        in_specs=[SMEM] * 4 + [VMEM] * 2 + [HBM] * 3,
        out_specs=(HBM, VMEM, VMEM),
        scratch_shapes=[
            pltpu.VMEM((peers * n_send, block, hidden), BF16),
            pltpu.VMEM((peers * n_recv + 1, block, hidden), F32),
            edge_room,
            pltpu.VMEM(recv_out, BF16),
            edge_sems,
            pltpu.SemaphoreType.DMA((2,)),
            out_sems,
        ],
        compiler_params=params,
        name="edge_forward",
    )(count, me, src, dst, raw, w_msg, adj, wide_feat, wide_cot)
    got = lax.all_to_all(partials, BOTH, 0, 0, tiled=True)

    out_part, grad_pre, grad_out, wself_part = pl.pallas_call(
        owner_kernel,
        out_shape=(quarter, quarter, pltpu.HBM(recv_out, BF16), sum_part),
        in_specs=[SMEM] + [VMEM] * 4,
        out_specs=(VMEM, VMEM, HBM, VMEM),
        scratch_shapes=[
            pltpu.VMEM((blocks, width, hidden), F32),
            pltpu.VMEM(recv_out, BF16),
            out_sems,
        ],
        compiler_params=params,
        name="owner_dense",
    )(recv_all, got, feat_part, cot_part, w_self)
    grad_in = lax.all_to_all(grad_out, BOTH, 0, 0, tiled=True)
    (out_feat,) = join_feat(out_part, me, params)
    wself_part = split_core(wself_part, me)
    for bits in stages[1:2]:
        wself_part = sum_stage(wself_part, bits)
    grad_in, out_feat, wself_part = lax.optimization_barrier((grad_in, out_feat, wself_part))

    grad_partials, wmsg_part = pl.pallas_call(
        functools.partial(backward_kernel, group),
        out_shape=(pltpu.HBM(send_out_dims, BF16), sum_part),
        in_specs=[SMEM] * 3 + [VMEM] * 2 + [HBM],
        out_specs=(HBM, VMEM),
        scratch_shapes=[
            pltpu.VMEM((peers * n_recv, hidden, block), BF16),
            pltpu.VMEM((peers * n_send + 1, hidden, block), F32),
            edge_room,
            pltpu.VMEM(send_out_dims, BF16),
            edge_sems,
            out_sems,
        ],
        compiler_params=params,
        name="edge_backward",
    )(count, src, dst, grad_in, raw, adj)
    grad_partials, wmsg_part, wself_part = lax.optimization_barrier(
        (grad_partials, wmsg_part, wself_part)
    )
    grad_back = lax.all_to_all(grad_partials, BOTH, 0, 0, tiled=True)
    wmsg_part = split_core(wmsg_part, me)
    for bits in stages[1:2]:
        wmsg_part = sum_stage(wmsg_part, bits)
    sums = jnp.concatenate([wself_part, wmsg_part], 0)
    for bits in stages[2:]:
        sums = sum_stage(sums.astype(BF16), bits)
    grad_back, sums = lax.optimization_barrier((grad_back, sums))

    grad_part = pl.pallas_call(
        last_kernel,
        out_shape=pltpu.VMEM((blocks, width, hidden), BF16),
        in_specs=[SMEM] + [VMEM] * 4,
        out_specs=VMEM,
        scratch_shapes=[pltpu.VMEM((blocks, width, hidden), F32)],
        compiler_params=params,
        name="owner_last",
    )(send_all, grad_back, grad_pre, w_self, w_msg)
    grad_part, sums = lax.optimization_barrier((grad_part, sums))
    grad_feat, grad_wself, grad_wmsg = join_feat(grad_part, me, params, sums)
    return (out_feat, grad_feat, grad_wmsg, grad_wself)


def solution(mesh):
    in_specs = (
        P("edge", None),
        P("edge", None),
        P(),
        P(),
        P("edge", "feat", None, None, None),
        P("edge", "feat", None),
        P("edge", "feat", None),
        P("edge", "feat", None, None),
        P("edge", "feat", None, None),
        P("edge", "feat"),
    )
    out_specs = (P("edge", None), P("edge", None), P(), P())
    return jax.shard_map(body, mesh=mesh, in_specs=in_specs, out_specs=out_specs, check_vma=False)
```

time: 125 us -> 108 us (0.86)
  blocking collectives: 18.4 us -> 0 us
  Pallas kernels: 10.5 us -> 15.4 us
  local copies, waits for them, and re-layouts: 7.03 us -> 2.44 us
  starting transfers between devices: 33.1 us -> 36.6 us
  other arithmetic: 1.59 us -> 0.09 us
    all_to_all x1 -> x0, blocking collectives: 18.4 us -> none  [body(): grad_in = lax.all_to_all(grad_out, BOTH, 0, 0, tiled=True)]
    all_to_all x1, waiting for transfers between devices: 14.8 us -> 0.01 us  [body(): grad_back = lax.all_to_all(grad_partials, BOTH, 0, 0, tiled=True)]
    ppermute x0 -> x12, starting transfers between devices: none -> 12.1 us  [swap_all(): return lax.ppermute(x, BOTH, [(j, j ^ mask) for j in range(count)])]
    ppermute x0 -> x12, waiting for transfers between devices: none -> 12 us  [swap_all(): return lax.ppermute(x, BOTH, [(j, j ^ mask) for j in range(count)])]
    ppermute x16 -> x8, starting transfers between devices: 16.5 us -> 5.26 us  [swap(): return lax.ppermute(x, axis, [(j, j ^ bit) for j in range(size)])]
    pallas_call x5 -> x7, Pallas kernels: 10.5 us -> 15.4 us  [the longest x1 4.18 us: body(): pl.pallas_call(functools.partial(backward_kernel, group), out_shape=(pltp...]
    all_to_all x0 -> x1, starting transfers between devices: none -> 3.09 us  [body(): grad_in = lax.all_to_all(grad_out, BOTH, 0, 0, tiled=True)]
    unnamed x23 -> x14, local copies, waits for them, and re-layouts: 4.81 us -> 2 us
  transfers between devices with their start and end apart: 19 -> 24, of which waited for: 12 -> 18; matrix products, arithmetic and copies ran while one was open for 2% -> 0% of each run, Pallas kernels for 1% -> 1%
where the time goes in v2:
time: 108 us
  waiting for transfers between devices  51.6 us (48%)
  starting transfers between devices  36.6 us (34%)
  Pallas kernels  15.4 us (14%)
  local copies, waits for them, and re-layouts  2.44 us (2%)
  between operations  1.5 us (1%)
    all_to_all x1, waiting for transfers between devices, body(): raw = lax.all_to_all(outgoing, 'edge', 0, 0, tiled=True)  14 us
    ppermute x8, waiting for transfers between devices, swap(): return lax.ppermute(x, axis, [(j, j ^ bit) for j in range(size)])  12.9 us
    ppermute x12, starting transfers between devices, swap_all(): return lax.ppermute(x, BOTH, [(j, j ^ mask) for j in range(count)])  12.1 us
    ppermute x12, waiting for transfers between devices, swap_all(): return lax.ppermute(x, BOTH, [(j, j ^ mask) for j in range(count)])  12 us
    all_to_all x1, waiting for transfers between devices, body(): got = lax.all_to_all(partials, BOTH, 0, 0, tiled=True)  10.4 us
    all_to_all x1, starting transfers between devices, body(): raw = lax.all_to_all(outgoing, 'edge', 0, 0, tiled=True)  7.16 us
    ppermute x8, starting transfers between devices, swap(): return lax.ppermute(x, axis, [(j, j ^ bit) for j in range(size)])  5.26 us
    all_to_all x1, starting transfers between devices, body(): got = lax.all_to_all(partials, BOTH, 0, 0, tiled=True)  4.7 us
  transfers between devices with their start and end apart: 24, of which 18 were waited for; matrix products, arithmetic and copies ran while one was open for 0% of the time, Pallas kernels for 1%

profile of v2, /device:TPU:0, one launch (start us, length us, event | category | flops | bytes accessed | tf_op | source)
XLA Modules:
  0.0 107.6 jit_solution(5690918989223441071)
XLA Ops:
  0.6 0.7 copy-done
  1.3 2.6 %pick_rows.1 = (bf16[16,128,128]{2,1,0:T(8,128)(2,1)}, bf16[128,128]{1,0:T(8,128)(2,1)S(1)}, bf16[128,128]{1,0:T(8,128)(2,1)S(1)}) custom-call(s32[2,8]{1,0:T(2,128)S(1)} %bitcast.24, bf16[16,128,128]{2,1,0:T(8,128)(2,1)} %bitcast.32, bf16[128,128]{1,0:T(8,128)(2,1)} %w_msg.1, bf16[128,128]{1,0:T(8,128)(2,1)} %w_self.1), custom_call_target="tpu_custom_call" | custom-call | tf_op jit(solution)/shard_map/pick_rows/pallas_call | solution.py:381
  3.9 7.2 %all-to-all-start = ((bf16[16,128,128]{2,1,0:T(8,128)(2,1)}), bf16[16,128,128]{2,1,0:T(8,128)(2,1)S(1)}, u32[]{:S(2)}, u32[]{:S(2)}) async-start(bf16[16,128,128]{2,1,0:T(8,128)(2,1)} %get-tuple-element.37), calls=%async_computation | async-start | bytes 1048576 | tf_op jit(solution)/shard_map/all_to_all | solution.py:399
  11.7 14.0 %all-to-all-done.raw = bf16[16,128,128]{2,1,0:T(8,128)(2,1)S(1)} async-done(((bf16[16,128,128]{2,1,0:T(8,128)(2,1)}), bf16[16,128,128]{2,1,0:T(8,128)(2,1)S(1)}, u32[]{:S(2)}, u32[]{:S(2)}) %all-to-all-start) | async-done | bytes 524320 | tf_op jit(solution)/shard_map/all_to_all | solution.py:399
  25.7 0.7 copy-done.2
  26.4 0.7 copy-done.4
  27.1 4.2 %edge_forward.1 = (bf16[32,2,32,128]{3,2,1,0:T(8,128)(2,1)}, bf16[16,32,128]{2,1,0:T(8,128)(2,1)S(1)}, bf16[16,32,128]{2,1,0:T(8,128)(2,1)S(1)}) custom-call(s32[1]{0:T(128)} %bitcast.22.live, s32[1]{0:T(128)} %bitcast.5.me, s32[64]{0:T(128)S(1)} %bitcast.26, s32[64]{0:T(128)S(1)} %bitcast.28, bf16[16,128,128]{2,1,0:T(8,128)(2,1)S(1)} %all-to-all-done.raw, ...), custom_call_target="tpu_custom_call" | custom-call | tf_op jit(solution)/shard_map/edge_forward/pallas_call | solution.py:403
  31.2 4.7 %all-to-all-start.1 = ((bf16[32,2,32,128]{3,2,1,0:T(8,128)(2,1)}), bf16[32,2,32,128]{3,2,1,0:T(8,128)(2,1)S(1)}, u32[]{:S(2)}, u32[]{:S(2)}) async-start(bf16[32,2,32,128]{3,2,1,0:T(8,128)(2,1)} %get-tuple-element.39), calls=%async_computation.1 | async-start | bytes 1048576 | tf_op jit(solution)/shard_map/all_to_all | solution.py:420
  36.0 0.3 collective-permute-start
  36.3 0.9 collective-permute-done
  37.2 1.8 %collective-permute-start.1 = (s32[2,8,4]{1,2,0:T(4,128)S(1)}, s32[2,8,4]{1,2,0:T(4,128)S(1)}, u32[]{:S(2)}, u32[]{:S(2)}) collective-permute-start(s32[2,8,4]{1,2,0:T(4,128)S(1)} %add_select_fusion.1), channel_id=1, source_target_pairs={{0,2},{1,3},{2,0},{3,1},{4,6},{5,7},{6,4},{7,5},{8,10},{9,11},{10,... | collective-permute-start | bytes 776 | tf_op jit(solution)/shard_map/ppermute | solution.py:26
  39.0 1.8 %collective-permute-done.1 = s32[2,8,4]{1,2,0:T(4,128)S(1)} collective-permute-done((s32[2,8,4]{1,2,0:T(4,128)S(1)}, s32[2,8,4]{1,2,0:T(4,128)S(1)}, u32[]{:S(2)}, u32[]{:S(2)}) %collective-permute-start.1) | collective-permute-done | bytes 288 | tf_op jit(solution)/shard_map/ppermute | solution.py:26
  41.1 10.4 %all-to-all-done.1.got = bf16[32,2,32,128]{3,2,1,0:T(8,128)(2,1)S(1)} async-done(((bf16[32,2,32,128]{3,2,1,0:T(8,128)(2,1)}), bf16[32,2,32,128]{3,2,1,0:T(8,128)(2,1)S(1)}, u32[]{:S(2)}, u32[]{:S(2)}) %all-to-all-start.1) | async-done | bytes 524320 | tf_op jit(solution)/shard_map/all_to_all | solution.py:420
  51.5 1.8 %owner_dense.1 = (bf16[16,32,128]{2,1,0:T(8,128)(2,1)S(1)}, bf16[16,32,128]{2,1,0:T(8,128)(2,1)S(1)}, bf16[32,2,32,128]{3,2,1,0:T(8,128)(2,1)}, f32[128,128]{1,0:T(8,128)S(1)}) custom-call(s32[64]{0:T(128)S(1)} %reshape.72.ids, bf16[32,2,32,128]{3,2,1,0:T(8,128)(2,1)S(1)} %all-to-all-done.1.got, bf16[16,32,128]{2,1,0:T(8,128)(2,1)S(1)} %get-tuple-element.40.feat, ...), custom_call_target="tpu_custom_call" | custom-call | tf_op jit(solution)/shard_map/owner_dense/pallas_call | solution.py:422
  53.3 3.1 %all-to-all-start.2 = ((bf16[32,2,32,128]{3,2,1,0:T(8,128)(2,1)}), bf16[32,2,32,128]{3,2,1,0:T(8,128)(2,1)S(1)}, u32[]{:S(2)}, u32[]{:S(2)}) async-start(bf16[32,2,32,128]{3,2,1,0:T(8,128)(2,1)} %get-tuple-element.43), calls=%async_computation.2 | async-start | bytes 1048576 | tf_op jit(solution)/shard_map/all_to_all | solution.py:435
  56.4 0.3 collective-permute-start.5
  56.7 1.7 %collective-permute-start.3 = (bf16[16,32,128]{2,1,0:T(8,128)(2,1)S(1)}, bf16[16,32,128]{2,1,0:T(8,128)(2,1)S(1)}, u32[]{:S(2)}, u32[]{:S(2)}) collective-permute-start(bf16[16,32,128]{2,1,0:T(8,128)(2,1)S(1)} %get-tuple-element.44.refs_0_), channel_id=1, source_target_pairs={{0,2},{1,3},{2,0},{3,1},{4,6},{5,7},{6,4},{7,5},{8,10},{9,11},{10,... | collective-permute-start | bytes 393224 | tf_op jit(solution)/shard_map/ppermute | solution.py:26
  58.4 1.9 %collective-permute-start.8 = (f32[64,128]{1,0:T(8,128)S(1)}, f32[64,128]{1,0:T(8,128)S(1)}, u32[]{:S(2)}, u32[]{:S(2)}) collective-permute-start(f32[64,128]{1,0:T(8,128)S(1)} %select_add_fusion.1), channel_id=1, source_target_pairs={{0,6},{1,7},{2,4},{3,5},{4,2},{5,3},{6,0},{7,1},{8,14},{9,15},{10,... | collective-permute-start | bytes 98312 | tf_op jit(solution)/shard_map/ppermute | solution.py:109
  60.4 0.6 collective-permute-start.7
  60.9 1.1 collective-permute-start.6
  62.0 5.5 %collective-permute-done.3.refs_2_ = bf16[16,32,128]{2,1,0:T(8,128)(2,1)S(1)} collective-permute-done((bf16[16,32,128]{2,1,0:T(8,128)(2,1)S(1)}, bf16[16,32,128]{2,1,0:T(8,128)(2,1)S(1)}, u32[]{:S(2)}, u32[]{:S(2)}) %collective-permute-start.3) | collective-permute-done | bytes 131104 | tf_op jit(solution)/shard_map/ppermute | solution.py:26
  67.5 0.5 collective-permute-done.6
  68.1 0.8 collective-permute-done.4.refs_3_
  68.8 0.8 join_rows.2
  69.7 2.2 %all-to-all-done.2.got = bf16[32,2,32,128]{3,2,1,0:T(8,128)(2,1)S(1)} async-done(((bf16[32,2,32,128]{3,2,1,0:T(8,128)(2,1)}), bf16[32,2,32,128]{3,2,1,0:T(8,128)(2,1)S(1)}, u32[]{:S(2)}, u32[]{:S(2)}) %all-to-all-start.2) | async-done | bytes 524320 | tf_op jit(solution)/shard_map/all_to_all | solution.py:435
  71.9 4.2 %edge_backward.1 = (bf16[32,2,32,128]{3,2,1,0:T(8,128)(2,1)}, f32[128,128]{1,0:T(8,128)S(1)}) custom-call(s32[1]{0:T(128)} %bitcast.23.live, s32[64]{0:T(128)S(1)} %bitcast.27, s32[64]{0:T(128)S(1)} %bitcast.29, bf16[32,2,32,128]{3,2,1,0:T(8,128)(2,1)S(1)} %all-to-all-done.2.got, bf16[16,128,128]{2,1,0:T(8,128)(2,1)S(1)} %all-to-all-done.raw, ...), custom_call_target="tpu_custom_call" | custom-call | tf_op jit(solution)/shard_map/edge_backward/pallas_call | solution.py:442
  76.1 4.2 %all-to-all-start.3 = ((bf16[32,2,32,128]{3,2,1,0:T(8,128)(2,1)}), bf16[32,2,32,128]{3,2,1,0:T(8,128)(2,1)S(1)}, u32[]{:S(2)}, u32[]{:S(2)}) async-start(bf16[32,2,32,128]{3,2,1,0:T(8,128)(2,1)} %get-tuple-element.51), calls=%async_computation.3 | async-start | bytes 1048576 | tf_op jit(solution)/shard_map/all_to_all | solution.py:461
  80.4 0.3 collective-permute-start.9
  80.7 1.0 collective-permute-done.9
  81.6 2.7 %collective-permute-start.12 = (f32[64,128]{1,0:T(8,128)S(1)}, f32[64,128]{1,0:T(8,128)S(1)}, u32[]{:S(2)}, u32[]{:S(2)}) collective-permute-start(f32[64,128]{1,0:T(8,128)S(1)} %select_add_fusion), channel_id=1, source_target_pairs={{0,6},{1,7},{2,4},{3,5},{4,2},{5,3},{6,0},{7,1},{8,14},{9,15},{10,... | collective-permute-start | bytes 98312 | tf_op jit(solution)/shard_map/ppermute | solution.py:109
  84.3 0.6 collective-permute-start.11
  84.9 0.3 collective-permute-start.10
  85.1 3.4 %collective-permute-done.12 = f32[64,128]{1,0:T(8,128)S(1)} collective-permute-done((f32[64,128]{1,0:T(8,128)S(1)}, f32[64,128]{1,0:T(8,128)S(1)}, u32[]{:S(2)}, u32[]{:S(2)}) %collective-permute-start.12) | collective-permute-done | bytes 32800 | tf_op jit(solution)/shard_map/ppermute | solution.py:109
  88.5 0.4 collective-permute-done.11
  88.9 0.7 collective-permute-done.10
  89.6 1.8 %collective-permute-start.14 = (bf16[128,128]{1,0:T(8,128)(2,1)S(1)}, bf16[128,128]{1,0:T(8,128)(2,1)S(1)}, u32[]{:S(2)}, u32[]{:S(2)}) collective-permute-start(bf16[128,128]{1,0:T(8,128)(2,1)S(1)} %pad_maximum_fusion), channel_id=1, source_target_pairs={{0,16},{1,17},{2,18},{3,19},{4,20},{5,21},{6,22},{7,23},{8,24},{9,... | collective-permute-start | bytes 98312 | tf_op jit(solution)/shard_map/ppermute | solution.py:109
  91.4 2.0 %collective-permute-start.13 = (bf16[128,128]{1,0:T(8,128)(2,1)S(1)}, bf16[128,128]{1,0:T(8,128)(2,1)S(1)}, u32[]{:S(2)}, u32[]{:S(2)}) collective-permute-start(bf16[128,128]{1,0:T(8,128)(2,1)S(1)} %pad_maximum_fusion), channel_id=1, source_target_pairs={{0,8},{1,9},{2,10},{3,11},{4,12},{5,13},{6,14},{7,15},{8,0},{9,1},... | collective-permute-start | bytes 98312 | tf_op jit(solution)/shard_map/ppermute | solution.py:109
  93.4 0.7 collective-permute-start.15
  94.3 2.8 %collective-permute-done.14 = bf16[128,128]{1,0:T(8,128)(2,1)S(1)} collective-permute-done((bf16[128,128]{1,0:T(8,128)(2,1)S(1)}, bf16[128,128]{1,0:T(8,128)(2,1)S(1)}, u32[]{:S(2)}, u32[]{:S(2)}) %collective-permute-start.14) | collective-permute-done | bytes 32800 | tf_op jit(solution)/shard_map/ppermute | solution.py:109
  97.1 2.0 %collective-permute-done.15 = bf16[128,128]{1,0:T(8,128)(2,1)S(1)} collective-permute-done((bf16[128,128]{1,0:T(8,128)(2,1)S(1)}, bf16[128,128]{1,0:T(8,128)(2,1)S(1)}, u32[]{:S(2)}, u32[]{:S(2)}) %collective-permute-start.15) | collective-permute-done | bytes 32800 | tf_op jit(solution)/shard_map/ppermute | solution.py:109
  99.1 1.0 owner_last.1.refs_0_
  100.2 1.0 collective-permute-start.16
  101.2 1.3 %collective-permute-done.17.refs_5_ = f32[128,128]{1,0:T(8,128)S(1)} collective-permute-done((f32[128,128]{1,0:T(8,128)S(1)}, f32[128,128]{1,0:T(8,128)S(1)}, u32[]{:S(2)}, u32[]{:S(2)}) %collective-permute-start.17) | collective-permute-done | bytes 65568 | tf_op jit(solution)/shard_map/ppermute | solution.py:109
  102.4 2.8 %collective-permute-done.16.refs_2_ = bf16[16,32,128]{2,1,0:T(8,128)(2,1)S(1)} collective-permute-done((bf16[16,32,128]{2,1,0:T(8,128)(2,1)S(1)}, bf16[16,32,128]{2,1,0:T(8,128)(2,1)S(1)}, u32[]{:S(2)}, u32[]{:S(2)}) %collective-permute-start.16) | collective-permute-done | bytes 131104 | tf_op jit(solution)/shard_map/ppermute | solution.py:26
  105.2 0.5 collective-permute-start.19
  105.7 0.8 collective-permute-done.18.refs_1_
  106.6 0.2 collective-permute-done.19.refs_3_
  106.7 0.9 join_rows.3
  (37 shorter events, 0.6 us)
Async XLA Ops:
  0.6 0.7 copy-start
  3.9 21.8 %all-to-all-start = ((bf16[16,128,128]{2,1,0:T(8,128)(2,1)}), bf16[16,128,128]{2,1,0:T(8,128)(2,1)S(1)}, u32[]{:S(2)}, u32[]{:S(2)}) async-start(bf16[16,128,128]{2,1,0:T(8,128)(2,1)} %get-tuple-element.37), calls=%async_computation | async-start | bytes 1048576 | tf_op jit(solution)/shard_map/all_to_all | solution.py:399
  25.7 0.7 copy-start.2
  26.4 0.7 copy-start.4
  27.0 8.9 %copy-start.1 = (s32[1,1,8,2]{2,3,1,0:T(2,128)S(1)}, s32[1,1,8,2]{2,3,1,0:T(2,128)}, u32[]{:S(2)}) copy-start(s32[1,1,8,2]{2,3,1,0:T(2,128)} %param.17) | copy-start | bytes 196
  27.0 8.9 %copy-start.6 = (s32[1,1,8,2]{2,3,1,0:T(2,128)S(1)}, s32[1,1,8,2]{2,3,1,0:T(2,128)}, u32[]{:S(2)}) copy-start(s32[1,1,8,2]{2,3,1,0:T(2,128)} %param.18) | copy-start | bytes 196
  31.2 40.7 %copy-start.3 = (s32[1,1,64]{2,1,0:T(1,128)S(1)}, s32[1,1,64]{2,1,0:T(1,128)}, u32[]{:S(2)}) copy-start(s32[1,1,64]{2,1,0:T(1,128)} %param.15) | copy-start | bytes 772
  31.2 40.7 %copy-start.5 = (s32[1,1,64]{2,1,0:T(1,128)S(1)}, s32[1,1,64]{2,1,0:T(1,128)}, u32[]{:S(2)}) copy-start(s32[1,1,64]{2,1,0:T(1,128)} %param.16) | copy-start | bytes 772
  31.2 20.3 %all-to-all-start.1 = ((bf16[32,2,32,128]{3,2,1,0:T(8,128)(2,1)}), bf16[32,2,32,128]{3,2,1,0:T(8,128)(2,1)S(1)}, u32[]{:S(2)}, u32[]{:S(2)}) async-start(bf16[32,2,32,128]{3,2,1,0:T(8,128)(2,1)} %get-tuple-element.39), calls=%async_computation.1 | async-start | bytes 1048576 | tf_op jit(solution)/shard_map/all_to_all | solution.py:420
  36.0 1.2 %collective-permute-start = (s32[1,8,4]{1,2,0:T(4,128)S(1)}, s32[1,8,4]{1,2,0:T(4,128)S(1)}, u32[]{:S(2)}, u32[]{:S(2)}) collective-permute-start(s32[1,8,4]{1,2,0:T(4,128)S(1)} %add_bitcast_fusion), channel_id=1, source_target_pairs={{0,1},{1,0},{2,3},{3,2},{4,5},{5,4},{6,7},{7,6},{8,9},{9,8},{10,11... | collective-permute-start | bytes 392 | tf_op jit(solution)/shard_map/ppermute | solution.py:26
  37.2 3.6 %collective-permute-start.1 = (s32[2,8,4]{1,2,0:T(4,128)S(1)}, s32[2,8,4]{1,2,0:T(4,128)S(1)}, u32[]{:S(2)}, u32[]{:S(2)}) collective-permute-start(s32[2,8,4]{1,2,0:T(4,128)S(1)} %add_select_fusion.1), channel_id=1, source_target_pairs={{0,2},{1,3},{2,0},{3,1},{4,6},{5,7},{6,4},{7,5},{8,10},{9,11},{10,... | collective-permute-start | bytes 776 | tf_op jit(solution)/shard_map/ppermute | solution.py:26
  53.3 18.6 %all-to-all-start.2 = ((bf16[32,2,32,128]{3,2,1,0:T(8,128)(2,1)}), bf16[32,2,32,128]{3,2,1,0:T(8,128)(2,1)S(1)}, u32[]{:S(2)}, u32[]{:S(2)}) async-start(bf16[32,2,32,128]{3,2,1,0:T(8,128)(2,1)} %get-tuple-element.43), calls=%async_computation.2 | async-start | bytes 1048576 | tf_op jit(solution)/shard_map/all_to_all | solution.py:435
  56.4 2.0 %collective-permute-start.5 = (f32[64,128]{1,0:T(8,128)S(1)}, f32[64,128]{1,0:T(8,128)S(1)}, u32[]{:S(2)}, u32[]{:S(2)}) collective-permute-start(f32[64,128]{1,0:T(8,128)S(1)} %slice_select_fusion.1), channel_id=1, source_target_pairs={{0,1},{1,0},{2,3},{3,2},{4,5},{5,4},{6,7},{7,6},{8,9},{9,8},{10,11... | collective-permute-start | bytes 98312 | tf_op jit(solution)/shard_map/ppermute | solution.py:109
  56.7 10.8 %collective-permute-start.3 = (bf16[16,32,128]{2,1,0:T(8,128)(2,1)S(1)}, bf16[16,32,128]{2,1,0:T(8,128)(2,1)S(1)}, u32[]{:S(2)}, u32[]{:S(2)}) collective-permute-start(bf16[16,32,128]{2,1,0:T(8,128)(2,1)S(1)} %get-tuple-element.44.refs_0_), channel_id=1, source_target_pairs={{0,2},{1,3},{2,0},{3,1},{4,6},{5,7},{6,4},{7,5},{8,10},{9,11},{10,... | collective-permute-start | bytes 393224 | tf_op jit(solution)/shard_map/ppermute | solution.py:26
  58.4 9.1 %collective-permute-start.8 = (f32[64,128]{1,0:T(8,128)S(1)}, f32[64,128]{1,0:T(8,128)S(1)}, u32[]{:S(2)}, u32[]{:S(2)}) collective-permute-start(f32[64,128]{1,0:T(8,128)S(1)} %select_add_fusion.1), channel_id=1, source_target_pairs={{0,6},{1,7},{2,4},{3,5},{4,2},{5,3},{6,0},{7,1},{8,14},{9,15},{10,... | collective-permute-start | bytes 98312 | tf_op jit(solution)/shard_map/ppermute | solution.py:109
  60.4 7.2 %collective-permute-start.7 = (f32[64,128]{1,0:T(8,128)S(1)}, f32[64,128]{1,0:T(8,128)S(1)}, u32[]{:S(2)}, u32[]{:S(2)}) collective-permute-start(f32[64,128]{1,0:T(8,128)S(1)} %select_add_fusion.1), channel_id=1, source_target_pairs={{0,4},{1,5},{2,6},{3,7},{4,0},{5,1},{6,2},{7,3},{8,12},{9,13},{10,... | collective-permute-start | bytes 98312 | tf_op jit(solution)/shard_map/ppermute | solution.py:109
  60.9 7.1 %collective-permute-start.6 = (f32[64,128]{1,0:T(8,128)S(1)}, f32[64,128]{1,0:T(8,128)S(1)}, u32[]{:S(2)}, u32[]{:S(2)}) collective-permute-start(f32[64,128]{1,0:T(8,128)S(1)} %select_add_fusion.1), channel_id=1, source_target_pairs={{0,2},{1,3},{2,0},{3,1},{4,6},{5,7},{6,4},{7,5},{8,10},{9,11},{10,... | collective-permute-start | bytes 98312 | tf_op jit(solution)/shard_map/ppermute | solution.py:109
  62.0 6.1 %collective-permute-start.2 = (bf16[16,32,128]{2,1,0:T(8,128)(2,1)S(1)}, bf16[16,32,128]{2,1,0:T(8,128)(2,1)S(1)}, u32[]{:S(2)}, u32[]{:S(2)}) collective-permute-start(bf16[16,32,128]{2,1,0:T(8,128)(2,1)S(1)} %get-tuple-element.44.refs_0_), channel_id=1, source_target_pairs={{0,1},{1,0},{2,3},{3,2},{4,5},{5,4},{6,7},{7,6},{8,9},{9,8},{10,11... | collective-permute-start | bytes 393224 | tf_op jit(solution)/shard_map/ppermute | solution.py:26
  67.5 1.3 %collective-permute-start.4 = (bf16[16,32,128]{2,1,0:T(8,128)(2,1)S(1)}, bf16[16,32,128]{2,1,0:T(8,128)(2,1)S(1)}, u32[]{:S(2)}, u32[]{:S(2)}) collective-permute-start(bf16[16,32,128]{2,1,0:T(8,128)(2,1)S(1)} %collective-permute-done.3.refs_2_), channel_id=1, source_target_pairs={{0,1},{1,0},{2,3},{3,2},{4,5},{5,4},{6,7},{7,6},{8,9},{9,8},{10,11... | collective-permute-start | bytes 393224 | tf_op jit(solution)/shard_map/ppermute | solution.py:26
  76.1 23.0 %all-to-all-start.3 = ((bf16[32,2,32,128]{3,2,1,0:T(8,128)(2,1)}), bf16[32,2,32,128]{3,2,1,0:T(8,128)(2,1)S(1)}, u32[]{:S(2)}, u32[]{:S(2)}) async-start(bf16[32,2,32,128]{3,2,1,0:T(8,128)(2,1)} %get-tuple-element.51), calls=%async_computation.3 | async-start | bytes 1048576 | tf_op jit(solution)/shard_map/all_to_all | solution.py:461
  80.4 1.3 %collective-permute-start.9 = (f32[64,128]{1,0:T(8,128)S(1)}, f32[64,128]{1,0:T(8,128)S(1)}, u32[]{:S(2)}, u32[]{:S(2)}) collective-permute-start(f32[64,128]{1,0:T(8,128)S(1)} %slice_select_fusion), channel_id=1, source_target_pairs={{0,1},{1,0},{2,3},{3,2},{4,5},{5,4},{6,7},{7,6},{8,9},{9,8},{10,11... | collective-permute-start | bytes 98312 | tf_op jit(solution)/shard_map/ppermute | solution.py:109
  81.6 6.9 %collective-permute-start.12 = (f32[64,128]{1,0:T(8,128)S(1)}, f32[64,128]{1,0:T(8,128)S(1)}, u32[]{:S(2)}, u32[]{:S(2)}) collective-permute-start(f32[64,128]{1,0:T(8,128)S(1)} %select_add_fusion), channel_id=1, source_target_pairs={{0,6},{1,7},{2,4},{3,5},{4,2},{5,3},{6,0},{7,1},{8,14},{9,15},{10,... | collective-permute-start | bytes 98312 | tf_op jit(solution)/shard_map/ppermute | solution.py:109
  84.3 4.6 %collective-permute-start.11 = (f32[64,128]{1,0:T(8,128)S(1)}, f32[64,128]{1,0:T(8,128)S(1)}, u32[]{:S(2)}, u32[]{:S(2)}) collective-permute-start(f32[64,128]{1,0:T(8,128)S(1)} %select_add_fusion), channel_id=1, source_target_pairs={{0,4},{1,5},{2,6},{3,7},{4,0},{5,1},{6,2},{7,3},{8,12},{9,13},{10,... | collective-permute-start | bytes 98312 | tf_op jit(solution)/shard_map/ppermute | solution.py:109
  84.9 4.7 %collective-permute-start.10 = (f32[64,128]{1,0:T(8,128)S(1)}, f32[64,128]{1,0:T(8,128)S(1)}, u32[]{:S(2)}, u32[]{:S(2)}) collective-permute-start(f32[64,128]{1,0:T(8,128)S(1)} %select_add_fusion), channel_id=1, source_target_pairs={{0,2},{1,3},{2,0},{3,1},{4,6},{5,7},{6,4},{7,5},{8,10},{9,11},{10,... | collective-permute-start | bytes 98312 | tf_op jit(solution)/shard_map/ppermute | solution.py:109
  89.6 7.5 %collective-permute-start.14 = (bf16[128,128]{1,0:T(8,128)(2,1)S(1)}, bf16[128,128]{1,0:T(8,128)(2,1)S(1)}, u32[]{:S(2)}, u32[]{:S(2)}) collective-permute-start(bf16[128,128]{1,0:T(8,128)(2,1)S(1)} %pad_maximum_fusion), channel_id=1, source_target_pairs={{0,16},{1,17},{2,18},{3,19},{4,20},{5,21},{6,22},{7,23},{8,24},{9,... | collective-permute-start | bytes 98312 | tf_op jit(solution)/shard_map/ppermute | solution.py:109
  91.4 5.7 %collective-permute-start.13 = (bf16[128,128]{1,0:T(8,128)(2,1)S(1)}, bf16[128,128]{1,0:T(8,128)(2,1)S(1)}, u32[]{:S(2)}, u32[]{:S(2)}) collective-permute-start(bf16[128,128]{1,0:T(8,128)(2,1)S(1)} %pad_maximum_fusion), channel_id=1, source_target_pairs={{0,8},{1,9},{2,10},{3,11},{4,12},{5,13},{6,14},{7,15},{8,0},{9,1},... | collective-permute-start | bytes 98312 | tf_op jit(solution)/shard_map/ppermute | solution.py:109
  93.4 5.7 %collective-permute-start.15 = (bf16[128,128]{1,0:T(8,128)(2,1)S(1)}, bf16[128,128]{1,0:T(8,128)(2,1)S(1)}, u32[]{:S(2)}, u32[]{:S(2)}) collective-permute-start(bf16[128,128]{1,0:T(8,128)(2,1)S(1)} %pad_maximum_fusion), channel_id=1, source_target_pairs={{0,24},{1,25},{2,26},{3,27},{4,28},{5,29},{6,30},{7,31},{8,16},{9,... | collective-permute-start | bytes 98312 | tf_op jit(solution)/shard_map/ppermute | solution.py:109
  100.2 5.0 %collective-permute-start.16 = (bf16[16,32,128]{2,1,0:T(8,128)(2,1)S(1)}, bf16[16,32,128]{2,1,0:T(8,128)(2,1)S(1)}, u32[]{:S(2)}, u32[]{:S(2)}) collective-permute-start(bf16[16,32,128]{2,1,0:T(8,128)(2,1)S(1)} %owner_last.1.refs_0_), channel_id=1, source_target_pairs={{0,2},{1,3},{2,0},{3,1},{4,6},{5,7},{6,4},{7,5},{8,10},{9,11},{10,... | collective-permute-start | bytes 393224 | tf_op jit(solution)/shard_map/ppermute | solution.py:26
  101.1 1.3 %collective-permute-start.17 = (f32[128,128]{1,0:T(8,128)S(1)}, f32[128,128]{1,0:T(8,128)S(1)}, u32[]{:S(2)}, u32[]{:S(2)}) collective-permute-start(f32[128,128]{1,0:T(8,128)S(1)} %add_add_fusion.refs_4_), channel_id=1, source_target_pairs={{0,1},{1,0},{2,3},{3,2},{4,5},{5,4},{6,7},{7,6},{8,9},{9,8},{10,11... | collective-permute-start | bytes 196616 | tf_op jit(solution)/shard_map/ppermute | solution.py:109
  105.2 1.3 %collective-permute-start.18 = (bf16[16,32,128]{2,1,0:T(8,128)(2,1)S(1)}, bf16[16,32,128]{2,1,0:T(8,128)(2,1)S(1)}, u32[]{:S(2)}, u32[]{:S(2)}) collective-permute-start(bf16[16,32,128]{2,1,0:T(8,128)(2,1)S(1)} %owner_last.1.refs_0_), channel_id=1, source_target_pairs={{0,1},{1,0},{2,3},{3,2},{4,5},{5,4},{6,7},{7,6},{8,9},{9,8},{10,11... | collective-permute-start | bytes 393224 | tf_op jit(solution)/shard_map/ppermute | solution.py:26
  105.2 1.5 %collective-permute-start.19 = (bf16[16,32,128]{2,1,0:T(8,128)(2,1)S(1)}, bf16[16,32,128]{2,1,0:T(8,128)(2,1)S(1)}, u32[]{:S(2)}, u32[]{:S(2)}) collective-permute-start(bf16[16,32,128]{2,1,0:T(8,128)(2,1)S(1)} %collective-permute-done.16.refs_2_), channel_id=1, source_target_pairs={{0,1},{1,0},{2,3},{3,2},{4,5},{5,4},{6,7},{7,6},{8,9},{9,8},{10,11... | collective-permute-start | bytes 393224 | tf_op jit(solution)/shard_map/ppermute | solution.py:26

commit v3 on v2

v3 whole, which is shorter than its diff:
```python
import functools
import math

import jax
import jax.numpy as jnp
from jax import lax
from jax.experimental import pallas as pl
from jax.experimental.pallas import tpu as pltpu
from jax.sharding import PartitionSpec as P

BOTH = ("edge", "feat")
F32 = jnp.float32
BF16 = jnp.bfloat16
VMEM = pl.BlockSpec(memory_space=pltpu.VMEM)
SMEM = pl.BlockSpec(memory_space=pltpu.SMEM)
HBM = pl.BlockSpec(memory_space=pltpu.HBM)
ANY = pl.BlockSpec(memory_space=pl.ANY)


def is_pow2(n):
    return n & (n - 1) == 0


def swap(x, axis, bit):
    size = lax.axis_size(axis)
    return lax.ppermute(x, axis, [(j, j ^ bit) for j in range(size)])


def gather_feat(x):
    size = lax.axis_size("feat")
    if not is_pow2(size):
        return lax.all_gather(x, "feat", axis=0)
    me = lax.axis_index("feat")
    held = x[None]
    bit = 1
    while bit < size:
        other = swap(held, "feat", bit)
        mine_low = (me & bit) == 0
        held = jnp.where(
            mine_low, jnp.concatenate([held, other], 0), jnp.concatenate([other, held], 0)
        )
        bit *= 2
    return held


def pieces_feat(x, beside=None):
    top = lax.axis_size("feat") // 2
    low = [1 << n for n in range(top.bit_length() - 1)][::-1]

    def spread(base, value):
        held = {base: value}
        for bit in low:
            held.update({m | bit: swap(v, "feat", bit) for m, v in list(held.items())})
        return held

    far = swap(x, "feat", top) if top else None
    held, other = spread(0, x), None
    if beside is not None:
        far, beside = lax.optimization_barrier((far, beside))
        other = swap_all(beside, 1)
    if top:
        held.update(spread(top, far))
    return [held[m] for m in sorted(held)], beside, other


def join_kernel(planes, count, me, *refs):
    pieces, refs = refs[: planes * count], refs[planes * count :]
    halves, (*outs, sems) = ((), refs) if len(refs) == count + 1 else (refs[:2], refs[2:])
    copies = [
        (part, outs[n // planes].at[:, me[0] ^ n % planes]) for n, part in enumerate(pieces)
    ]
    for n, total in enumerate(outs[count:]):
        rows = total.shape[1]
        copies += [
            (half.at[n * rows : (n + 1) * rows], total.at[(me[0] & 1) ^ m])
            for m, half in enumerate(halves)
        ]
    copies = [pltpu.make_async_copy(a, b, sems.at[n]) for n, (a, b) in enumerate(copies)]
    for copy in copies:
        copy.start()
    for copy in copies:
        copy.wait()


def join_feat(groups, halves, me, params):
    blocks, width, hidden = groups[0][0].shape
    planes = lax.axis_size("feat")
    count = 2 * halves[0].shape[0] // hidden if halves else 0
    out_shape = [pltpu.HBM((blocks, planes, width, hidden), BF16)] * len(groups)
    out_shape += [pltpu.HBM((2, hidden // 2, hidden), F32)] * count
    pieces = [piece for group in groups for piece in group]
    joined = pl.pallas_call(
        functools.partial(join_kernel, planes, len(groups)),
        out_shape=out_shape,
        in_specs=[SMEM] + [VMEM] * (len(pieces) + len(halves)),
        out_specs=[HBM] * len(out_shape),
        scratch_shapes=[pltpu.SemaphoreType.DMA((len(pieces) + 2 * count,))],
        compiler_params=params,
        name="join_rows",
    )(me, *pieces, *halves)
    return [v.reshape(-1, hidden) for v in joined]


def stages_of(count):
    bits = [1 << n for n in range(count.bit_length() - 1)]
    return [bits[:1]] + [bits[n : n + 2] for n in range(1, len(bits), 2)]


def swap_all(x, mask):
    count = lax.axis_size(BOTH)
    return lax.ppermute(x, BOTH, [(j, j ^ mask) for j in range(count)])


def sum_stage(x, bits):
    terms = {0: x}
    for bit in bits:
        terms.update({m | bit: swap_all(x, m | bit) for m in list(terms)})
    held = [terms[m].astype(F32) for m in sorted(terms)]
    while len(held) > 1:
        held = [held[n] + held[n + 1] for n in range(0, len(held), 2)]
    return held[0]


def split_core(x, me):
    halves = x.reshape(2, -1, x.shape[-1])
    low = (me & 1) == 0
    mine = jnp.where(low, halves[0], halves[1])
    other = jnp.where(low, halves[1], halves[0])
    return mine + swap_all(other, 1)


def pick_kernel(me, ids, rows, w_msg, w_self, *refs):
    n_send, peers = ids.shape
    *outs, w_msg_out, w_self_out, room, sems, out_sems = refs
    near = outs[0].shape[0] // n_send
    first = me[0] // near * near
    order = [me[0] ^ m for m in range(near, peers)] + [first + i for i in range(near)]
    places = [(outs[1 + m], 0) for m in range(peers - near)]
    places += [(outs[0], i * n_send) for i in range(near)]
    slots = [(n, j) for n in range(peers) for j in range(n_send)]
    ins = [
        pltpu.make_async_copy(
            rows.at[ids[j, order[n]]], room.at[n * n_send + j], sems.at[n * n_send + j]
        )
        for n, j in slots
    ]
    others = [
        pltpu.make_async_copy(w_msg, w_msg_out, sems.at[len(slots)]),
        pltpu.make_async_copy(w_self, w_self_out, sems.at[len(slots) + 1]),
    ]
    copies = [
        pltpu.make_async_copy(
            room.at[n * n_send + j],
            places[n][0].at[places[n][1] + j],
            out_sems.at[n * n_send + j],
        )
        for n, j in slots
    ]
    for copy in ins + others:
        copy.start()
    for one, two in zip(ins, copies):
        one.wait()
        two.start()
    for copy in others + copies:
        copy.wait()


def pieces_of(me, raw):
    near, *far = raw
    per_owner = far[0].shape[0] if far else near.shape[0]
    owners = near.shape[0] // per_owner
    yield me // owners * owners * per_owner, near
    for m, rows in enumerate(far):
        yield (me ^ (owners + m)) * per_owner, rows


def fetch_kernel(me, *refs):
    *ins, out, sems = refs
    copies = [
        pltpu.make_async_copy(
            a if me is None else a.at[:, me[0]], out if me is None else out.at[n], sems.at[n]
        )
        for n, a in enumerate(ins)
    ]
    for copy in copies:
        copy.start()
    for copy in copies:
        copy.wait()


def fetch(me, arrays, dims, params, name):
    kernel, specs, args = fetch_kernel, [SMEM], [me]
    if me is None:
        kernel, specs, args = functools.partial(fetch_kernel, None), [], []
    return pl.pallas_call(
        kernel,
        out_shape=pltpu.VMEM(dims, BF16),
        in_specs=specs + [HBM] * len(arrays),
        out_specs=VMEM,
        scratch_shapes=[pltpu.SemaphoreType.DMA((len(arrays),))],
        compiler_params=params,
        cost_estimate=pl.CostEstimate(
            flops=0, bytes_accessed=4 * math.prod(dims), transcendentals=0
        ),
        name=name,
    )(*args, *arrays)


def edge_loop(group, count, term, put):
    def step(turn, carry):
        ks = [turn * group + u for u in range(group)]
        terms = [term(k) for k in ks]
        for k, value in zip(ks, terms):
            put(k, k < count, value)
        return carry

    lax.fori_loop(0, (count + group - 1) // group, step, 0)


def copy_ids(pairs, sems):
    copies = [pltpu.make_async_copy(a, b, sems.at[n]) for n, (a, b) in enumerate(pairs)]
    for copy in copies:
        copy.start()
    return copies


def send_out(room, out, sems, p, size):
    copy = pltpu.make_async_copy(
        room.at[p * size : (p + 1) * size], out.at[p * size : (p + 1) * size], sems.at[p]
    )
    copy.start()
    return copy


def forward_kernel(
    group, live, me, src_in, dst_in, w_msg, adj, *refs
):
    *raw, out, msgs, acc, room, src, dst, sems, out_sems = refs
    slots, block, hidden = msgs.shape
    per_owner, width = out.shape[1:3]
    planes = block // width
    ids = copy_ids([(src_in, src), (dst_in, dst)], sems)
    for first, rows in pieces_of(me[0], raw):
        flat = rows[...].reshape(-1, hidden)
        piece = jnp.dot(flat, w_msg[...], preferred_element_type=F32).astype(BF16)
        msgs[pl.ds(first, rows.shape[0])] = piece.reshape(rows.shape)
    acc[...] = jnp.zeros_like(acc)
    for copy in ids:
        copy.wait()

    def term(k):
        return jnp.dot(adj[k], msgs[src[k]], preferred_element_type=F32)

    def put(k, alive, value):
        acc[jnp.where(alive, dst[k], slots)] += value

    edge_loop(group, live[0], term, put)
    copies = []
    for p in range(out.shape[0] // planes):
        for j in range(per_owner):
            for q in range(planes):
                room[p * planes + q, j] = acc[
                    p * per_owner + j, q * width : (q + 1) * width
                ].astype(BF16)
        copies.append(send_out(room, out, out_sems, p, planes))
    for copy in copies:
        copy.wait()


def owner_kernel(
    ids, got, rows, w_self, out_feat, grad_pre, out, w_part, agg, held, room, out_room, out_sems
):
    blocks, width, hidden = held.shape
    devices, per_owner = got.shape[:2]
    agg[...] = jnp.zeros_like(agg)
    for i in range(devices):
        for j in range(per_owner):
            agg[ids[i * per_owner + j]] += got[i, j].astype(F32)
    mine = rows[0].reshape(blocks * width, hidden)
    preact = jnp.dot(mine, w_self[...], preferred_element_type=F32)
    preact = preact + agg[...].reshape(blocks * width, hidden)
    sig = jax.nn.sigmoid(preact)
    grad = rows[1].reshape(blocks * width, hidden).astype(F32)
    grad = (grad * sig * (1.0 + preact * (1.0 - sig))).astype(BF16)
    held[...] = grad.reshape(blocks, width, hidden)
    copies = []
    peers = out_sems.shape[0] - 2
    size = devices // peers
    for p in range(peers):
        for i in range(p * size, (p + 1) * size):
            for j in range(per_owner):
                room[i, j] = held[ids[i * per_owner + j]]
        copies.append(send_out(room, out, out_sems, p, size))
    out_room[...] = (preact * sig).astype(BF16).reshape(blocks, width, hidden)
    for n, (a, b) in enumerate([(out_room, out_feat), (held, grad_pre)]):
        copies.append(pltpu.make_async_copy(a, b, out_sems.at[peers + n]))
        copies[-1].start()
    w_part[...] = lax.dot_general(
        mine, grad, (((0,), (0,)), ((), ())), preferred_element_type=F32
    )
    for copy in copies:
        copy.wait()


def backward_kernel(group, live, me, src_in, dst_in, got, adj, *refs):
    *raw, out, w_part, turned, acc, room, src, dst, sems, out_sems = refs
    slots, hidden, block = acc.shape
    slots -= 1
    devices, per_owner, width = got.shape[:3]
    planes = block // width
    out_slots = out.shape[1]
    ids = copy_ids([(src_in, src), (dst_in, dst)], sems)
    for p in range(devices // planes):
        for j in range(per_owner):
            whole = jnp.concatenate([got[p * planes + q, j] for q in range(planes)], 0)
            turned[p * per_owner + j] = whole.T
    acc[...] = jnp.zeros_like(acc)
    for copy in ids:
        copy.wait()

    def term(k):
        return jnp.dot(turned[dst[k]], adj[k], preferred_element_type=F32)

    def put(k, alive, value):
        acc[jnp.where(alive, src[k], slots)] += value

    edge_loop(group, live[0], term, put)
    copies = []
    for p in range(devices // planes):
        for j in range(out_slots):
            back = acc[p * out_slots + j].T.astype(BF16)
            for q in range(planes):
                room[p * planes + q, j] = back[q * width : (q + 1) * width]
        copies.append(send_out(room, out, out_sems, p, planes))
    total = jnp.zeros((hidden, hidden), F32)
    for first, rows in pieces_of(me[0], raw):
        for s in range(rows.shape[0]):
            total += jnp.dot(acc[first + s].astype(BF16), rows[s], preferred_element_type=F32)
    w_part[...] = total.T
    for copy in copies:
        copy.wait()


def last_kernel(ids, got, grad_pre, w_self, w_msg, out, agg):
    blocks, width, hidden = grad_pre.shape
    devices, per_owner = got.shape[:2]
    agg[...] = jnp.zeros_like(agg)
    for i in range(devices):
        for j in range(per_owner):
            agg[ids[i * per_owner + j]] += got[i, j].astype(F32)
    grad_msg = agg[...].reshape(blocks * width, hidden).astype(BF16)
    turn = (((1,), (1,)), ((), ()))
    total = lax.dot_general(
        grad_pre[...].reshape(blocks * width, hidden),
        w_self[...],
        turn,
        preferred_element_type=F32,
    ) + lax.dot_general(grad_msg, w_msg[...], turn, preferred_element_type=F32)
    out[...] = total.astype(BF16).reshape(blocks, width, hidden)


def shape(dims, dtype):
    return jax.ShapeDtypeStruct(dims, dtype)


def in_hbm(x):
    return pltpu.with_memory_space_constraint(x, pltpu.HBM)


def body(
    node_feat, cotangent, w_msg, w_self, adjacency, edge_src, edge_dst, send_src, recv_dst, live
):
    block = adjacency.shape[-1]
    hidden = node_feat.shape[1]
    blocks = node_feat.shape[0] // block
    peers = lax.axis_size("edge")
    planes = lax.axis_size("feat")
    devices = peers * planes
    width = block // planes
    n_send = send_src.shape[-1]
    n_recv = recv_dst.shape[-1]
    adj = in_hbm(adjacency.reshape(-1, block, block))
    src = in_hbm(edge_src.reshape(-1))
    dst = in_hbm(edge_dst.reshape(-1))
    count = live.reshape(1)
    group = math.gcd(16, adj.shape[0])
    me = lax.axis_index("feat").reshape(1).astype(jnp.int32)
    params = pltpu.CompilerParams(vmem_limit_bytes=32 * 2**20)
    stages = stages_of(devices)

    ids = jnp.concatenate([send_src.reshape(peers, n_send), recv_dst.reshape(peers, n_recv)], 1)
    ids = gather_feat(ids).transpose(1, 0, 2)
    send_all = ids[:, :, :n_send].reshape(-1)
    recv_all = ids[:, :, n_send:].reshape(-1)

    wide_feat = in_hbm(node_feat.reshape(blocks, planes, width, hidden))
    wide_cot = in_hbm(cotangent.reshape(blocks, planes, width, hidden))
    square = pltpu.VMEM((hidden, hidden), BF16)
    sum_part = pltpu.VMEM((hidden, hidden), F32)
    rows_out = (peers * n_send, block, hidden)
    recv_out = (devices, n_recv, width, hidden)
    send_out_dims = (devices, n_send, width, hidden)
    out_sems = pltpu.SemaphoreType.DMA((peers,))
    here = lax.axis_index("edge").reshape(1).astype(jnp.int32)
    near = peers // 2 if is_pow2(peers) and 1 < peers <= 16 else peers
    few = (n_send, block, hidden)
    *outgoing, w_msg, w_self = pl.pallas_call(
        pick_kernel,
        out_shape=[pltpu.HBM((near * n_send, block, hidden), BF16)]
        + [pltpu.HBM(few, BF16)] * (peers - near)
        + [square, square],
        in_specs=[SMEM] * 2 + [HBM] * 3,
        out_specs=[HBM] * (peers - near + 1) + [VMEM, VMEM],
        scratch_shapes=[
            pltpu.VMEM(rows_out, BF16),
            pltpu.SemaphoreType.DMA((peers * n_send + 2,)),
            pltpu.SemaphoreType.DMA((peers * n_send,)),
        ],
        compiler_params=params,
        name="pick_rows",
    )(
        here,
        in_hbm(send_src.transpose(0, 1, 3, 2).reshape(n_send, peers)),
        in_hbm(node_feat.reshape(blocks, block, hidden)),
        in_hbm(w_msg),
        in_hbm(w_self),
    )
    raw = [swap(rows, "edge", near + m) for m, rows in enumerate(outgoing[1:])]
    groups = [list(range(g, g + near)) for g in range(0, peers, near)]
    raw = [
        lax.all_to_all(outgoing[0], "edge", 0, 0, tiled=True, axis_index_groups=groups)
    ] + raw

    adj = fetch(None, [adj], adj.shape, params, "fetch_edges")
    ids_room = [pltpu.SMEM(src.shape, src.dtype)] * 2 + [pltpu.SemaphoreType.DMA((2,))]
    partials = pl.pallas_call(
        functools.partial(forward_kernel, group),
        out_shape=pltpu.HBM(recv_out, BF16),
        in_specs=[SMEM] * 2 + [HBM] * 2 + [VMEM] * (2 + len(raw)),
        out_specs=HBM,
        scratch_shapes=[
            pltpu.VMEM((peers * n_send, block, hidden), BF16),
            pltpu.VMEM((peers * n_recv + 1, block, hidden), F32),
            pltpu.VMEM(recv_out, BF16),
            *ids_room,
            out_sems,
        ],
        compiler_params=params,
        name="edge_forward",
    )(count, here, src, dst, w_msg, adj, *raw)
    later, partials = lax.optimization_barrier((me, partials))
    got = lax.all_to_all(partials, BOTH, 0, 0, tiled=True)
    rows = fetch(later, [wide_feat, wide_cot], (2, blocks, width, hidden), params, "fetch_rows")

    out_part, grad_pre, grad_out, wself_part = pl.pallas_call(
        owner_kernel,
        out_shape=(
            pltpu.HBM((blocks, width, hidden), BF16),
            pltpu.HBM((blocks, width, hidden), BF16),
            pltpu.HBM(recv_out, BF16),
            sum_part,
        ),
        in_specs=[SMEM] + [VMEM] * 3,
        out_specs=(HBM, HBM, HBM, VMEM),
        scratch_shapes=[
            pltpu.VMEM((blocks, width, hidden), F32),
            pltpu.VMEM((blocks, width, hidden), BF16),
            pltpu.VMEM(recv_out, BF16),
            pltpu.VMEM((blocks, width, hidden), BF16),
            pltpu.SemaphoreType.DMA((peers + 2,)),
        ],
        compiler_params=params,
        name="owner_dense",
    )(recv_all, got, rows, w_self)
    grad_in = lax.all_to_all(grad_out, BOTH, 0, 0, tiled=True)
    out_pieces, _, _ = pieces_feat(out_part)
    (out_feat,) = join_feat([out_pieces], [], me, params)
    wself_part = split_core(wself_part, me)
    for bits in stages[1:2]:
        wself_part = sum_stage(wself_part, bits)
    grad_in, out_feat, wself_part = lax.optimization_barrier((grad_in, out_feat, wself_part))

    grad_partials, wmsg_part = pl.pallas_call(
        functools.partial(backward_kernel, group),
        out_shape=(pltpu.HBM(send_out_dims, BF16), sum_part),
        in_specs=[SMEM] * 2 + [HBM] * 2 + [VMEM] * (2 + len(raw)),
        out_specs=(HBM, VMEM),
        scratch_shapes=[
            pltpu.VMEM((peers * n_recv, hidden, block), BF16),
            pltpu.VMEM((peers * n_send + 1, hidden, block), F32),
            pltpu.VMEM(send_out_dims, BF16),
            *ids_room,
            out_sems,
        ],
        compiler_params=params,
        name="edge_backward",
    )(count, here, src, dst, grad_in, adj, *raw)
    grad_partials, wmsg_part, wself_part = lax.optimization_barrier(
        (grad_partials, wmsg_part, wself_part)
    )
    grad_back = lax.all_to_all(grad_partials, BOTH, 0, 0, tiled=True)
    wmsg_part = split_core(wmsg_part, me)
    for bits in stages[1:2]:
        wmsg_part = sum_stage(wmsg_part, bits)
    sums = jnp.concatenate([wself_part, wmsg_part], 0)
    for bits in stages[2:]:
        sums = sum_stage(sums.astype(BF16), bits)

    grad_part = pl.pallas_call(
        last_kernel,
        out_shape=pltpu.VMEM((blocks, width, hidden), BF16),
        in_specs=[SMEM] + [VMEM] * 4,
        out_specs=VMEM,
        scratch_shapes=[pltpu.VMEM((blocks, width, hidden), F32)],
        compiler_params=params,
        name="owner_last",
    )(send_all, grad_back, grad_pre, w_self, w_msg)
    grad_pieces, sums, other = pieces_feat(grad_part, sums)
    grad_feat, grad_wself, grad_wmsg = join_feat([grad_pieces], [sums, other], me, params)
    return (out_feat, grad_feat, grad_wmsg, grad_wself)


def solution(mesh):
    in_specs = (
        P("edge", None),
        P("edge", None),
        P(),
        P(),
        P("edge", "feat", None, None, None),
        P("edge", "feat", None),
        P("edge", "feat", None),
        P("edge", "feat", None, None),
        P("edge", "feat", None, None),
        P("edge", "feat"),
    )
    out_specs = (P("edge", None), P("edge", None), P(), P())
    return jax.shard_map(body, mesh=mesh, in_specs=in_specs, out_specs=out_specs, check_vma=False)
```

time: 108 us -> 98.8 us (0.915)
  waiting for transfers between devices: 51.6 us -> 37.3 us
  starting transfers between devices: 36.6 us -> 41.9 us
  local copies, waits for them, and re-layouts: 2.44 us -> 1.35 us
    all_to_all x1, waiting for transfers between devices: 14 us -> 0.01 us  [body(): lax.all_to_all(outgoing[0], 'edge', 0, 0, tiled=True, axis_index_groups=g...]
    ppermute x8 -> x12, starting transfers between devices: 5.26 us -> 13.6 us  [swap(): return lax.ppermute(x, axis, [(j, j ^ bit) for j in range(size)])]
    ppermute x12, waiting for transfers between devices: 12 us -> 6.92 us  [swap_all(): return lax.ppermute(x, BOTH, [(j, j ^ mask) for j in range(count)])]
    ppermute x8 -> x12, waiting for transfers between devices: 12.9 us -> 17.6 us  [swap(): return lax.ppermute(x, axis, [(j, j ^ bit) for j in range(size)])]
    all_to_all x1, waiting for transfers between devices: 0.01 us -> 2.25 us  [body(): grad_back = lax.all_to_all(grad_partials, BOTH, 0, 0, tiled=True)]
    all_to_all x1, starting transfers between devices: 7.16 us -> 5.25 us  [body(): lax.all_to_all(outgoing[0], 'edge', 0, 0, tiled=True, axis_index_groups=g...]
    pallas_call x5 -> x7, Pallas kernels: 10.2 us -> 11.9 us  [the longest x1 2.95 us: body(): pl.pallas_call(functools.partial(forward_kernel, group), out_shape=pltpu....]
    all_to_all x1, waiting for transfers between devices: 2.24 us -> 1.04 us  [body(): grad_in = lax.all_to_all(grad_out, BOTH, 0, 0, tiled=True)]
  transfers between devices with their start and end apart: 24 -> 28, of which waited for: 18 -> 16; matrix products, arithmetic and copies ran while one was open for 0% -> 1% of each run, Pallas kernels for 1% -> 4%
where the time goes in v3:
time: 98.8 us; the launch traced here: 98.1 us
  starting transfers between devices  41.9 us (42%)
  waiting for transfers between devices  37.3 us (38%)
  Pallas kernels  16 us (16%)
  between operations  1.51 us (2%)
  local copies, waits for them, and re-layouts  1.35 us (1%)
    ppermute x12, waiting for transfers between devices, swap(): return lax.ppermute(x, axis, [(j, j ^ bit) for j in range(size)])  17.6 us
    ppermute x12, starting transfers between devices, swap(): return lax.ppermute(x, axis, [(j, j ^ bit) for j in range(size)])  13.6 us
    ppermute x12, starting transfers between devices, swap_all(): return lax.ppermute(x, BOTH, [(j, j ^ mask) for j in range(count)])  12.6 us
    all_to_all x1, waiting for transfers between devices, body(): got = lax.all_to_all(partials, BOTH, 0, 0, tiled=True)  9.44 us
    ppermute x12, waiting for transfers between devices, swap_all(): return lax.ppermute(x, BOTH, [(j, j ^ mask) for j in range(count)])  6.92 us
    all_to_all x1, starting transfers between devices, body(): lax.all_to_all(outgoing[0], 'edge', 0, 0, tiled=True, axis_index_groups=g...  5.25 us
    all_to_all x1, starting transfers between devices, body(): grad_back = lax.all_to_all(grad_partials, BOTH, 0, 0, tiled=True)  3.64 us
    all_to_all x1, starting transfers between devices, body(): got = lax.all_to_all(partials, BOTH, 0, 0, tiled=True)  3.64 us
  transfers between devices with their start and end apart: 28, of which 16 were waited for; matrix products, arithmetic and copies ran while one was open for 1% of the time, Pallas kernels for 4%

profile of v3, /device:TPU:0, one launch (start us, length us, event | category | flops | bytes accessed | tf_op | source)
XLA Modules:
  0.0 98.1 jit_solution(17993026782412068536)
XLA Ops:
  0.6 2.8 %pick_rows.1 = (bf16[8,128,128]{2,1,0:T(8,128)(2,1)}, bf16[2,128,128]{2,1,0:T(8,128)(2,1)}, bf16[2,128,128]{2,1,0:T(8,128)(2,1)}, bf16[2,128,128]{2,1,0:T(8,128)...) custom-call(s32[1]{0:T(128)} %bitcast.6.me, s32[2,8]{1,0:T(2,128)} %bitcast.30, ...), custom_call_target="tpu_custom_call" | custom-call | tf_op jit(solution)/shard_map/pick_rows/pallas_call | solution.py:407
  3.4 5.2 %all-to-all-start = ((bf16[8,128,128]{2,1,0:T(8,128)(2,1)}), bf16[8,128,128]{2,1,0:T(8,128)(2,1)S(1)}, u32[]{:S(2)}, u32[]{:S(2)}) async-start(bf16[8,128,128]{2,1,0:T(8,128)(2,1)} %get-tuple-element.31), calls=%async_computation | async-start | bytes 524288 | tf_op jit(solution)/shard_map/all_to_all | solution.py:431
  8.7 2.6 %collective-permute-start.2 = (bf16[2,128,128]{2,1,0:T(8,128)(2,1)}, bf16[2,128,128]{2,1,0:T(8,128)(2,1)S(1)}, u32[]{:S(2)}, u32[]{:S(2)}) collective-permute-start(bf16[2,128,128]{2,1,0:T(8,128)(2,1)} %get-tuple-element.32), channel_id=1, source_target_pairs={{0,16},{4,20},{8,24},{12,28},{16,0},{20,4},{24,8},{28,12},{1,17},{... | collective-permute-start | bytes 196616 | tf_op jit(solution)/shard_map/ppermute | solution.py:26
  11.3 1.8 %collective-permute-start.3 = (bf16[2,128,128]{2,1,0:T(8,128)(2,1)}, bf16[2,128,128]{2,1,0:T(8,128)(2,1)S(1)}, u32[]{:S(2)}, u32[]{:S(2)}) collective-permute-start(bf16[2,128,128]{2,1,0:T(8,128)(2,1)} %get-tuple-element.33), channel_id=1, source_target_pairs={{0,20},{4,16},{8,28},{12,24},{16,4},{20,0},{24,12},{28,8},{1,21},{... | collective-permute-start | bytes 196616 | tf_op jit(solution)/shard_map/ppermute | solution.py:26
  13.0 3.5 %collective-permute-start.4 = (bf16[2,128,128]{2,1,0:T(8,128)(2,1)}, bf16[2,128,128]{2,1,0:T(8,128)(2,1)S(1)}, u32[]{:S(2)}, u32[]{:S(2)}) collective-permute-start(bf16[2,128,128]{2,1,0:T(8,128)(2,1)} %get-tuple-element.34), channel_id=1, source_target_pairs={{0,24},{4,28},{8,16},{12,20},{16,8},{20,12},{24,0},{28,4},{1,25},{... | collective-permute-start | bytes 196616 | tf_op jit(solution)/shard_map/ppermute | solution.py:26
  17.2 1.6 %fetch_edges.1.adj = bf16[64,128,128]{2,1,0:T(8,128)(2,1)S(1)} custom-call(bf16[64,128,128]{2,1,0:T(8,128)(2,1)} %bitcast.27), custom_call_target="tpu_custom_call" | custom-call | bytes 4194304 | tf_op jit(solution)/shard_map/fetch_edges/pallas_call | solution.py:195
  18.8 3.6 %collective-permute-done.3.refs_2_ = bf16[2,128,128]{2,1,0:T(8,128)(2,1)S(1)} collective-permute-done((bf16[2,128,128]{2,1,0:T(8,128)(2,1)}, bf16[2,128,128]{2,1,0:T(8,128)(2,1)S(1)}, u32[]{:S(2)}, u32[]{:S(2)}) %collective-permute-start.3) | collective-permute-done | bytes 65568 | tf_op jit(solution)/shard_map/ppermute | solution.py:26
  22.5 1.4 %collective-permute-done.5.refs_4_ = bf16[2,128,128]{2,1,0:T(8,128)(2,1)S(1)} collective-permute-done((bf16[2,128,128]{2,1,0:T(8,128)(2,1)}, bf16[2,128,128]{2,1,0:T(8,128)(2,1)S(1)}, u32[]{:S(2)}, u32[]{:S(2)}) %collective-permute-start.5) | collective-permute-done | bytes 65568 | tf_op jit(solution)/shard_map/ppermute | solution.py:26
  23.8 3.0 %edge_forward.1 = bf16[32,2,32,128]{3,2,1,0:T(8,128)(2,1)} custom-call(s32[1]{0:T(128)} %bitcast.23.live, s32[1]{0:T(128)} %bitcast.6.me, s32[64]{0:T(128)} %bitcast.32, s32[64]{0:T(128)} %bitcast.34, bf16[128,128]{1,0:T(8,128)(2,1)S(1)} %get-tuple-element.30.w_msg, bf16[64,128,128]{2,1,0:T(8,128)(2,1)S(1)} %fetch_edges.1.adj, ...), custom_call_target="tpu_custom_call" | custom-call | tf_op jit(solution)/shard_map/edge_forward/pallas_call | solution.py:436
  26.8 3.6 %all-to-all-start.1 = ((bf16[32,2,32,128]{3,2,1,0:T(8,128)(2,1)}), bf16[32,2,32,128]{3,2,1,0:T(8,128)(2,1)S(1)}, u32[]{:S(2)}, u32[]{:S(2)}) async-start(bf16[32,2,32,128]{3,2,1,0:T(8,128)(2,1)} %edge_forward.1), calls=%async_computation.1 | async-start | bytes 1048576 | tf_op jit(solution)/shard_map/all_to_all | solution.py:452
  30.5 0.3 collective-permute-start
  30.8 0.9 collective-permute-done
  31.7 1.8 %collective-permute-start.1 = (s32[2,8,4]{1,2,0:T(4,128)S(1)}, s32[2,8,4]{1,2,0:T(4,128)S(1)}, u32[]{:S(2)}, u32[]{:S(2)}) collective-permute-start(s32[2,8,4]{1,2,0:T(4,128)S(1)} %add_select_fusion.1), channel_id=1, source_target_pairs={{0,2},{1,3},{2,0},{3,1},{4,6},{5,7},{6,4},{7,5},{8,10},{9,11},{10,... | collective-permute-start | bytes 776 | tf_op jit(solution)/shard_map/ppermute | solution.py:26
  33.5 1.8 %collective-permute-done.1 = s32[2,8,4]{1,2,0:T(4,128)S(1)} collective-permute-done((s32[2,8,4]{1,2,0:T(4,128)S(1)}, s32[2,8,4]{1,2,0:T(4,128)S(1)}, u32[]{:S(2)}, u32[]{:S(2)}) %collective-permute-start.1) | collective-permute-done | bytes 288 | tf_op jit(solution)/shard_map/ppermute | solution.py:26
  35.5 1.0 %fetch_rows.1.rows = bf16[2,16,32,128]{3,2,1,0:T(8,128)(2,1)S(1)} custom-call(s32[1]{0:T(128)} %bitcast.4.me, bf16[16,4,32,128]{3,2,1,0:T(8,128)(2,1)} %bitcast.26, bf16[16,4,32,128]{3,2,1,0:T(8,128)(2,1)} %bitcast.28), custom_call_target="tpu_custom_call" | custom-call | bytes 524288 | tf_op jit(solution)/shard_map/fetch_rows/pallas_call | solution.py:195
  36.5 9.4 %all-to-all-done.1.got = bf16[32,2,32,128]{3,2,1,0:T(8,128)(2,1)S(1)} async-done(((bf16[32,2,32,128]{3,2,1,0:T(8,128)(2,1)}), bf16[32,2,32,128]{3,2,1,0:T(8,128)(2,1)S(1)}, u32[]{:S(2)}, u32[]{:S(2)}) %all-to-all-start.1) | async-done | bytes 524320 | tf_op jit(solution)/shard_map/all_to_all | solution.py:452
  46.0 1.9 %owner_dense.1 = (bf16[16,32,128]{2,1,0:T(8,128)(2,1)}, bf16[16,32,128]{2,1,0:T(8,128)(2,1)}, bf16[32,2,32,128]{3,2,1,0:T(8,128)(2,1)}, f32[128,128]{1,0:T(8,128)S(1)}) custom-call(s32[64]{0:T(128)S(1)} %reshape.75.ids, bf16[32,2,32,128]{3,2,1,0:T(8,128)(2,1)S(1)} %all-to-all-done.1.got, bf16[2,16,32,128]{3,2,1,0:T(8,128)(2,1)S(1)} %fetch_rows.1.rows, ...), custom_call_target="tpu_custom_call" | custom-call | tf_op jit(solution)/shard_map/owner_dense/pallas_call | solution.py:455
  47.9 3.1 %all-to-all-start.2 = ((bf16[32,2,32,128]{3,2,1,0:T(8,128)(2,1)}), bf16[32,2,32,128]{3,2,1,0:T(8,128)(2,1)S(1)}, u32[]{:S(2)}, u32[]{:S(2)}) async-start(bf16[32,2,32,128]{3,2,1,0:T(8,128)(2,1)} %get-tuple-element.39), calls=%async_computation.2 | async-start | bytes 1048576 | tf_op jit(solution)/shard_map/all_to_all | solution.py:475
  51.0 0.3 collective-permute-start.9
  51.3 1.7 %collective-permute-start.7 = (bf16[16,32,128]{2,1,0:T(8,128)(2,1)}, bf16[16,32,128]{2,1,0:T(8,128)(2,1)S(1)}, u32[]{:S(2)}, u32[]{:S(2)}) collective-permute-start(bf16[16,32,128]{2,1,0:T(8,128)(2,1)} %get-tuple-element.40.refs_0_), channel_id=1, source_target_pairs={{0,2},{1,3},{2,0},{3,1},{4,6},{5,7},{6,4},{7,5},{8,10},{9,11},{10,... | collective-permute-start | bytes 393224 | tf_op jit(solution)/shard_map/ppermute | solution.py:26
  53.0 1.9 %collective-permute-start.12 = (f32[64,128]{1,0:T(8,128)S(1)}, f32[64,128]{1,0:T(8,128)S(1)}, u32[]{:S(2)}, u32[]{:S(2)}) collective-permute-start(f32[64,128]{1,0:T(8,128)S(1)} %select_add_fusion.1), channel_id=1, source_target_pairs={{0,6},{1,7},{2,4},{3,5},{4,2},{5,3},{6,0},{7,1},{8,14},{9,15},{10,... | collective-permute-start | bytes 98312 | tf_op jit(solution)/shard_map/ppermute | solution.py:111
  54.9 0.6 collective-permute-start.11
  55.5 1.1 %collective-permute-start.10 = (f32[64,128]{1,0:T(8,128)S(1)}, f32[64,128]{1,0:T(8,128)S(1)}, u32[]{:S(2)}, u32[]{:S(2)}) collective-permute-start(f32[64,128]{1,0:T(8,128)S(1)} %select_add_fusion.1), channel_id=1, source_target_pairs={{0,2},{1,3},{2,0},{3,1},{4,6},{5,7},{6,4},{7,5},{8,10},{9,11},{10,... | collective-permute-start | bytes 98312 | tf_op jit(solution)/shard_map/ppermute | solution.py:111
  56.6 5.8 %collective-permute-done.7.refs_2_ = bf16[16,32,128]{2,1,0:T(8,128)(2,1)S(1)} collective-permute-done((bf16[16,32,128]{2,1,0:T(8,128)(2,1)}, bf16[16,32,128]{2,1,0:T(8,128)(2,1)S(1)}, u32[]{:S(2)}, u32[]{:S(2)}) %collective-permute-start.7) | collective-permute-done | bytes 131104 | tf_op jit(solution)/shard_map/ppermute | solution.py:26
  62.4 0.6 collective-permute-done.10
  63.0 0.7 collective-permute-done.8.refs_3_
  63.7 0.9 copy-done.1
  64.6 0.8 join_rows.2
  65.5 1.0 %all-to-all-done.2.got = bf16[32,2,32,128]{3,2,1,0:T(8,128)(2,1)S(1)} async-done(((bf16[32,2,32,128]{3,2,1,0:T(8,128)(2,1)}), bf16[32,2,32,128]{3,2,1,0:T(8,128)(2,1)S(1)}, u32[]{:S(2)}, u32[]{:S(2)}) %all-to-all-start.2) | async-done | bytes 524320 | tf_op jit(solution)/shard_map/all_to_all | solution.py:475
  66.5 3.1 %edge_backward.1 = (bf16[32,2,32,128]{3,2,1,0:T(8,128)(2,1)}, f32[128,128]{1,0:T(8,128)S(1)}) custom-call(s32[1]{0:T(128)} %bitcast.24.live, s32[1]{0:T(128)} %bitcast.6.me, s32[64]{0:T(128)} %bitcast.33, s32[64]{0:T(128)} %bitcast.35, bf16[32,2,32,128]{3,2,1,0:T(8,128)(2,1)S(1)} %all-to-all-done.2.got, bf16[64,128,128]{2,1,0:T(8,128)(2,1)S(1)} %fetch_edges.1.adj, ...), custom_call_target="tpu_custom_call" | custom-call | tf_op jit(solution)/shard_map/edge_backward/pallas_call | solution.py:483
  69.7 3.6 %all-to-all-start.3 = ((bf16[32,2,32,128]{3,2,1,0:T(8,128)(2,1)}), bf16[32,2,32,128]{3,2,1,0:T(8,128)(2,1)S(1)}, u32[]{:S(2)}, u32[]{:S(2)}) async-start(bf16[32,2,32,128]{3,2,1,0:T(8,128)(2,1)} %get-tuple-element.47), calls=%async_computation.3 | async-start | bytes 1048576 | tf_op jit(solution)/shard_map/all_to_all | solution.py:501
  73.3 0.3 collective-permute-start.15
  73.6 1.0 collective-permute-done.15
  74.6 2.7 %collective-permute-start.18 = (f32[64,128]{1,0:T(8,128)S(1)}, f32[64,128]{1,0:T(8,128)S(1)}, u32[]{:S(2)}, u32[]{:S(2)}) collective-permute-start(f32[64,128]{1,0:T(8,128)S(1)} %select_add_fusion), channel_id=1, source_target_pairs={{0,6},{1,7},{2,4},{3,5},{4,2},{5,3},{6,0},{7,1},{8,14},{9,15},{10,... | collective-permute-start | bytes 98312 | tf_op jit(solution)/shard_map/ppermute | solution.py:111
  77.3 0.6 collective-permute-start.17
  78.1 3.4 %collective-permute-done.18 = f32[64,128]{1,0:T(8,128)S(1)} collective-permute-done((f32[64,128]{1,0:T(8,128)S(1)}, f32[64,128]{1,0:T(8,128)S(1)}, u32[]{:S(2)}, u32[]{:S(2)}) %collective-permute-start.18) | collective-permute-done | bytes 32800 | tf_op jit(solution)/shard_map/ppermute | solution.py:111
  81.5 0.4 collective-permute-done.17
  81.9 0.7 collective-permute-done.16
  82.6 1.8 %collective-permute-start.20 = (bf16[128,128]{1,0:T(8,128)(2,1)S(1)}, bf16[128,128]{1,0:T(8,128)(2,1)S(1)}, u32[]{:S(2)}, u32[]{:S(2)}) collective-permute-start(bf16[128,128]{1,0:T(8,128)(2,1)S(1)} %pad_maximum_fusion), channel_id=1, source_target_pairs={{0,16},{1,17},{2,18},{3,19},{4,20},{5,21},{6,22},{7,23},{8,24},{9,... | collective-permute-start | bytes 98312 | tf_op jit(solution)/shard_map/ppermute | solution.py:111
  84.4 2.0 %collective-permute-start.19 = (bf16[128,128]{1,0:T(8,128)(2,1)S(1)}, bf16[128,128]{1,0:T(8,128)(2,1)S(1)}, u32[]{:S(2)}, u32[]{:S(2)}) collective-permute-start(bf16[128,128]{1,0:T(8,128)(2,1)S(1)} %pad_maximum_fusion), channel_id=1, source_target_pairs={{0,8},{1,9},{2,10},{3,11},{4,12},{5,13},{6,14},{7,15},{8,0},{9,1},... | collective-permute-start | bytes 98312 | tf_op jit(solution)/shard_map/ppermute | solution.py:111
  86.4 0.7 collective-permute-start.21
  87.2 2.2 %all-to-all-done.3.got = bf16[32,2,32,128]{3,2,1,0:T(8,128)(2,1)S(1)} async-done(((bf16[32,2,32,128]{3,2,1,0:T(8,128)(2,1)}), bf16[32,2,32,128]{3,2,1,0:T(8,128)(2,1)S(1)}, u32[]{:S(2)}, u32[]{:S(2)}) %all-to-all-start.3) | async-done | bytes 524320 | tf_op jit(solution)/shard_map/all_to_all | solution.py:501
  89.5 1.0 %owner_last.1.refs_0_ = bf16[16,32,128]{2,1,0:T(8,128)(2,1)S(1)} custom-call(s32[64]{0:T(128)S(1)} %reshape.87.ids, bf16[32,2,32,128]{3,2,1,0:T(8,128)(2,1)S(1)} %all-to-all-done.3.got, bf16[16,32,128]{2,1,0:T(8,128)(2,1)S(1)} %copy-done, bf16[128,128]{1,0:T(8,128)(2,1)S(1)} %get-tuple-element.38.w_self, bf16[128,128]{1,0:T(8,128)(2,1)S(1)} %get-tuple-element.30.w_msg), custom_call_target="tpu_custom_call" | custom-call | tf_op jit(solution)/shard_map/owner_last/pallas_call | solution.py:509
  90.5 1.9 %collective-permute-start.14 = (bf16[16,32,128]{2,1,0:T(8,128)(2,1)S(1)}, bf16[16,32,128]{2,1,0:T(8,128)(2,1)S(1)}, u32[]{:S(2)}, u32[]{:S(2)}) collective-permute-start(bf16[16,32,128]{2,1,0:T(8,128)(2,1)S(1)} %owner_last.1.refs_0_), channel_id=1, source_target_pairs={{0,2},{1,3},{2,0},{3,1},{4,6},{5,7},{6,4},{7,5},{8,10},{9,11},{10,... | collective-permute-start | bytes 393224 | tf_op jit(solution)/shard_map/ppermute | solution.py:26
  92.5 3.3 %collective-permute-done.14.refs_2_ = bf16[16,32,128]{2,1,0:T(8,128)(2,1)S(1)} collective-permute-done((bf16[16,32,128]{2,1,0:T(8,128)(2,1)S(1)}, bf16[16,32,128]{2,1,0:T(8,128)(2,1)S(1)}, u32[]{:S(2)}, u32[]{:S(2)}) %collective-permute-start.14) | collective-permute-done | bytes 131104 | tf_op jit(solution)/shard_map/ppermute | solution.py:26
  95.8 0.5 collective-permute-start.23
  96.3 0.9 collective-permute-done.23.refs_5_
  97.2 0.9 join_rows.3
  (41 shorter events, 0.9 us)
Async XLA Ops:
  3.4 20.4 %all-to-all-start = ((bf16[8,128,128]{2,1,0:T(8,128)(2,1)}), bf16[8,128,128]{2,1,0:T(8,128)(2,1)S(1)}, u32[]{:S(2)}, u32[]{:S(2)}) async-start(bf16[8,128,128]{2,1,0:T(8,128)(2,1)} %get-tuple-element.31), calls=%async_computation | async-start | bytes 524288 | tf_op jit(solution)/shard_map/all_to_all | solution.py:431
  8.7 10.2 %collective-permute-start.2 = (bf16[2,128,128]{2,1,0:T(8,128)(2,1)}, bf16[2,128,128]{2,1,0:T(8,128)(2,1)S(1)}, u32[]{:S(2)}, u32[]{:S(2)}) collective-permute-start(bf16[2,128,128]{2,1,0:T(8,128)(2,1)} %get-tuple-element.32), channel_id=1, source_target_pairs={{0,16},{4,20},{8,24},{12,28},{16,0},{20,4},{24,8},{28,12},{1,17},{... | collective-permute-start | bytes 196616 | tf_op jit(solution)/shard_map/ppermute | solution.py:26
  11.3 11.2 %collective-permute-start.3 = (bf16[2,128,128]{2,1,0:T(8,128)(2,1)}, bf16[2,128,128]{2,1,0:T(8,128)(2,1)S(1)}, u32[]{:S(2)}, u32[]{:S(2)}) collective-permute-start(bf16[2,128,128]{2,1,0:T(8,128)(2,1)} %get-tuple-element.33), channel_id=1, source_target_pairs={{0,20},{4,16},{8,28},{12,24},{16,4},{20,0},{24,12},{28,8},{1,21},{... | collective-permute-start | bytes 196616 | tf_op jit(solution)/shard_map/ppermute | solution.py:26
  13.0 9.4 %collective-permute-start.4 = (bf16[2,128,128]{2,1,0:T(8,128)(2,1)}, bf16[2,128,128]{2,1,0:T(8,128)(2,1)S(1)}, u32[]{:S(2)}, u32[]{:S(2)}) collective-permute-start(bf16[2,128,128]{2,1,0:T(8,128)(2,1)} %get-tuple-element.34), channel_id=1, source_target_pairs={{0,24},{4,28},{8,16},{12,20},{16,8},{20,12},{24,0},{28,4},{1,25},{... | collective-permute-start | bytes 196616 | tf_op jit(solution)/shard_map/ppermute | solution.py:26
  16.6 7.3 %collective-permute-start.5 = (bf16[2,128,128]{2,1,0:T(8,128)(2,1)}, bf16[2,128,128]{2,1,0:T(8,128)(2,1)S(1)}, u32[]{:S(2)}, u32[]{:S(2)}) collective-permute-start(bf16[2,128,128]{2,1,0:T(8,128)(2,1)} %get-tuple-element.35), channel_id=1, source_target_pairs={{0,28},{4,24},{8,20},{12,16},{16,12},{20,8},{24,4},{28,0},{1,29},{... | collective-permute-start | bytes 196616 | tf_op jit(solution)/shard_map/ppermute | solution.py:26
  23.8 6.6 %copy-start.2 = (s32[1,1,8,2]{2,3,1,0:T(2,128)S(1)}, s32[1,1,8,2]{2,3,1,0:T(2,128)}, u32[]{:S(2)}) copy-start(s32[1,1,8,2]{2,3,1,0:T(2,128)} %param.17) | copy-start | bytes 196
  23.8 6.6 %copy-start.3 = (s32[1,1,8,2]{2,3,1,0:T(2,128)S(1)}, s32[1,1,8,2]{2,3,1,0:T(2,128)}, u32[]{:S(2)}) copy-start(s32[1,1,8,2]{2,3,1,0:T(2,128)} %param.18) | copy-start | bytes 196
  26.8 19.2 %all-to-all-start.1 = ((bf16[32,2,32,128]{3,2,1,0:T(8,128)(2,1)}), bf16[32,2,32,128]{3,2,1,0:T(8,128)(2,1)S(1)}, u32[]{:S(2)}, u32[]{:S(2)}) async-start(bf16[32,2,32,128]{3,2,1,0:T(8,128)(2,1)} %edge_forward.1), calls=%async_computation.1 | async-start | bytes 1048576 | tf_op jit(solution)/shard_map/all_to_all | solution.py:452
  30.5 1.2 %collective-permute-start = (s32[1,8,4]{1,2,0:T(4,128)S(1)}, s32[1,8,4]{1,2,0:T(4,128)S(1)}, u32[]{:S(2)}, u32[]{:S(2)}) collective-permute-start(s32[1,8,4]{1,2,0:T(4,128)S(1)} %add_bitcast_fusion), channel_id=1, source_target_pairs={{0,1},{1,0},{2,3},{3,2},{4,5},{5,4},{6,7},{7,6},{8,9},{9,8},{10,11... | collective-permute-start | bytes 392 | tf_op jit(solution)/shard_map/ppermute | solution.py:26
  31.7 3.6 %collective-permute-start.1 = (s32[2,8,4]{1,2,0:T(4,128)S(1)}, s32[2,8,4]{1,2,0:T(4,128)S(1)}, u32[]{:S(2)}, u32[]{:S(2)}) collective-permute-start(s32[2,8,4]{1,2,0:T(4,128)S(1)} %add_select_fusion.1), channel_id=1, source_target_pairs={{0,2},{1,3},{2,0},{3,1},{4,6},{5,7},{6,4},{7,5},{8,10},{9,11},{10,... | collective-permute-start | bytes 776 | tf_op jit(solution)/shard_map/ppermute | solution.py:26
  47.9 18.6 %all-to-all-start.2 = ((bf16[32,2,32,128]{3,2,1,0:T(8,128)(2,1)}), bf16[32,2,32,128]{3,2,1,0:T(8,128)(2,1)S(1)}, u32[]{:S(2)}, u32[]{:S(2)}) async-start(bf16[32,2,32,128]{3,2,1,0:T(8,128)(2,1)} %get-tuple-element.39), calls=%async_computation.2 | async-start | bytes 1048576 | tf_op jit(solution)/shard_map/all_to_all | solution.py:475
  51.0 2.0 %collective-permute-start.9 = (f32[64,128]{1,0:T(8,128)S(1)}, f32[64,128]{1,0:T(8,128)S(1)}, u32[]{:S(2)}, u32[]{:S(2)}) collective-permute-start(f32[64,128]{1,0:T(8,128)S(1)} %slice_select_fusion.1), channel_id=1, source_target_pairs={{0,1},{1,0},{2,3},{3,2},{4,5},{5,4},{6,7},{7,6},{8,9},{9,8},{10,11... | collective-permute-start | bytes 98312 | tf_op jit(solution)/shard_map/ppermute | solution.py:111
  51.3 11.1 %collective-permute-start.7 = (bf16[16,32,128]{2,1,0:T(8,128)(2,1)}, bf16[16,32,128]{2,1,0:T(8,128)(2,1)S(1)}, u32[]{:S(2)}, u32[]{:S(2)}) collective-permute-start(bf16[16,32,128]{2,1,0:T(8,128)(2,1)} %get-tuple-element.40.refs_0_), channel_id=1, source_target_pairs={{0,2},{1,3},{2,0},{3,1},{4,6},{5,7},{6,4},{7,5},{8,10},{9,11},{10,... | collective-permute-start | bytes 393224 | tf_op jit(solution)/shard_map/ppermute | solution.py:26
  53.0 9.4 %collective-permute-start.12 = (f32[64,128]{1,0:T(8,128)S(1)}, f32[64,128]{1,0:T(8,128)S(1)}, u32[]{:S(2)}, u32[]{:S(2)}) collective-permute-start(f32[64,128]{1,0:T(8,128)S(1)} %select_add_fusion.1), channel_id=1, source_target_pairs={{0,6},{1,7},{2,4},{3,5},{4,2},{5,3},{6,0},{7,1},{8,14},{9,15},{10,... | collective-permute-start | bytes 98312 | tf_op jit(solution)/shard_map/ppermute | solution.py:111
  54.9 7.5 %collective-permute-start.11 = (f32[64,128]{1,0:T(8,128)S(1)}, f32[64,128]{1,0:T(8,128)S(1)}, u32[]{:S(2)}, u32[]{:S(2)}) collective-permute-start(f32[64,128]{1,0:T(8,128)S(1)} %select_add_fusion.1), channel_id=1, source_target_pairs={{0,4},{1,5},{2,6},{3,7},{4,0},{5,1},{6,2},{7,3},{8,12},{9,13},{10,... | collective-permute-start | bytes 98312 | tf_op jit(solution)/shard_map/ppermute | solution.py:111
  55.5 7.5 %collective-permute-start.10 = (f32[64,128]{1,0:T(8,128)S(1)}, f32[64,128]{1,0:T(8,128)S(1)}, u32[]{:S(2)}, u32[]{:S(2)}) collective-permute-start(f32[64,128]{1,0:T(8,128)S(1)} %select_add_fusion.1), channel_id=1, source_target_pairs={{0,2},{1,3},{2,0},{3,1},{4,6},{5,7},{6,4},{7,5},{8,10},{9,11},{10,... | collective-permute-start | bytes 98312 | tf_op jit(solution)/shard_map/ppermute | solution.py:111
  56.6 6.4 %collective-permute-start.6 = (bf16[16,32,128]{2,1,0:T(8,128)(2,1)}, bf16[16,32,128]{2,1,0:T(8,128)(2,1)S(1)}, u32[]{:S(2)}, u32[]{:S(2)}) collective-permute-start(bf16[16,32,128]{2,1,0:T(8,128)(2,1)} %get-tuple-element.40.refs_0_), channel_id=1, source_target_pairs={{0,1},{1,0},{2,3},{3,2},{4,5},{5,4},{6,7},{7,6},{8,9},{9,8},{10,11... | collective-permute-start | bytes 393224 | tf_op jit(solution)/shard_map/ppermute | solution.py:26
  62.4 1.3 %collective-permute-start.8 = (bf16[16,32,128]{2,1,0:T(8,128)(2,1)S(1)}, bf16[16,32,128]{2,1,0:T(8,128)(2,1)S(1)}, u32[]{:S(2)}, u32[]{:S(2)}) collective-permute-start(bf16[16,32,128]{2,1,0:T(8,128)(2,1)S(1)} %collective-permute-done.7.refs_2_), channel_id=1, source_target_pairs={{0,1},{1,0},{2,3},{3,2},{4,5},{5,4},{6,7},{7,6},{8,9},{9,8},{10,11... | collective-permute-start | bytes 393224 | tf_op jit(solution)/shard_map/ppermute | solution.py:26
  63.7 0.9 copy-start.1
  66.5 23.0 %copy-start = (bf16[16,32,128]{2,1,0:T(8,128)(2,1)S(1)}, bf16[16,32,128]{2,1,0:T(8,128)(2,1)}, u32[]{:S(2)}) copy-start(bf16[16,32,128]{2,1,0:T(8,128)(2,1)} %get-tuple-element.48.grad_pre) | copy-start | bytes 393220
  69.7 19.8 %all-to-all-start.3 = ((bf16[32,2,32,128]{3,2,1,0:T(8,128)(2,1)}), bf16[32,2,32,128]{3,2,1,0:T(8,128)(2,1)S(1)}, u32[]{:S(2)}, u32[]{:S(2)}) async-start(bf16[32,2,32,128]{3,2,1,0:T(8,128)(2,1)} %get-tuple-element.47), calls=%async_computation.3 | async-start | bytes 1048576 | tf_op jit(solution)/shard_map/all_to_all | solution.py:501
  73.3 1.3 %collective-permute-start.15 = (f32[64,128]{1,0:T(8,128)S(1)}, f32[64,128]{1,0:T(8,128)S(1)}, u32[]{:S(2)}, u32[]{:S(2)}) collective-permute-start(f32[64,128]{1,0:T(8,128)S(1)} %slice_select_fusion), channel_id=1, source_target_pairs={{0,1},{1,0},{2,3},{3,2},{4,5},{5,4},{6,7},{7,6},{8,9},{9,8},{10,11... | collective-permute-start | bytes 98312 | tf_op jit(solution)/shard_map/ppermute | solution.py:111
  74.6 6.9 %collective-permute-start.18 = (f32[64,128]{1,0:T(8,128)S(1)}, f32[64,128]{1,0:T(8,128)S(1)}, u32[]{:S(2)}, u32[]{:S(2)}) collective-permute-start(f32[64,128]{1,0:T(8,128)S(1)} %select_add_fusion), channel_id=1, source_target_pairs={{0,6},{1,7},{2,4},{3,5},{4,2},{5,3},{6,0},{7,1},{8,14},{9,15},{10,... | collective-permute-start | bytes 98312 | tf_op jit(solution)/shard_map/ppermute | solution.py:111
  77.3 4.6 %collective-permute-start.17 = (f32[64,128]{1,0:T(8,128)S(1)}, f32[64,128]{1,0:T(8,128)S(1)}, u32[]{:S(2)}, u32[]{:S(2)}) collective-permute-start(f32[64,128]{1,0:T(8,128)S(1)} %select_add_fusion), channel_id=1, source_target_pairs={{0,4},{1,5},{2,6},{3,7},{4,0},{5,1},{6,2},{7,3},{8,12},{9,13},{10,... | collective-permute-start | bytes 98312 | tf_op jit(solution)/shard_map/ppermute | solution.py:111
  77.8 4.7 %collective-permute-start.16 = (f32[64,128]{1,0:T(8,128)S(1)}, f32[64,128]{1,0:T(8,128)S(1)}, u32[]{:S(2)}, u32[]{:S(2)}) collective-permute-start(f32[64,128]{1,0:T(8,128)S(1)} %select_add_fusion), channel_id=1, source_target_pairs={{0,2},{1,3},{2,0},{3,1},{4,6},{5,7},{6,4},{7,5},{8,10},{9,11},{10,... | collective-permute-start | bytes 98312 | tf_op jit(solution)/shard_map/ppermute | solution.py:111
  82.6 9.8 %collective-permute-start.20 = (bf16[128,128]{1,0:T(8,128)(2,1)S(1)}, bf16[128,128]{1,0:T(8,128)(2,1)S(1)}, u32[]{:S(2)}, u32[]{:S(2)}) collective-permute-start(bf16[128,128]{1,0:T(8,128)(2,1)S(1)} %pad_maximum_fusion), channel_id=1, source_target_pairs={{0,16},{1,17},{2,18},{3,19},{4,20},{5,21},{6,22},{7,23},{8,24},{9,... | collective-permute-start | bytes 98312 | tf_op jit(solution)/shard_map/ppermute | solution.py:111
  84.4 8.0 %collective-permute-start.19 = (bf16[128,128]{1,0:T(8,128)(2,1)S(1)}, bf16[128,128]{1,0:T(8,128)(2,1)S(1)}, u32[]{:S(2)}, u32[]{:S(2)}) collective-permute-start(bf16[128,128]{1,0:T(8,128)(2,1)S(1)} %pad_maximum_fusion), channel_id=1, source_target_pairs={{0,8},{1,9},{2,10},{3,11},{4,12},{5,13},{6,14},{7,15},{8,0},{9,1},... | collective-permute-start | bytes 98312 | tf_op jit(solution)/shard_map/ppermute | solution.py:111
  86.4 6.0 %collective-permute-start.21 = (bf16[128,128]{1,0:T(8,128)(2,1)S(1)}, bf16[128,128]{1,0:T(8,128)(2,1)S(1)}, u32[]{:S(2)}, u32[]{:S(2)}) collective-permute-start(bf16[128,128]{1,0:T(8,128)(2,1)S(1)} %pad_maximum_fusion), channel_id=1, source_target_pairs={{0,24},{1,25},{2,26},{3,27},{4,28},{5,29},{6,30},{7,31},{8,16},{9,... | collective-permute-start | bytes 98312 | tf_op jit(solution)/shard_map/ppermute | solution.py:111
  90.5 5.3 %collective-permute-start.14 = (bf16[16,32,128]{2,1,0:T(8,128)(2,1)S(1)}, bf16[16,32,128]{2,1,0:T(8,128)(2,1)S(1)}, u32[]{:S(2)}, u32[]{:S(2)}) collective-permute-start(bf16[16,32,128]{2,1,0:T(8,128)(2,1)S(1)} %owner_last.1.refs_0_), channel_id=1, source_target_pairs={{0,2},{1,3},{2,0},{3,1},{4,6},{5,7},{6,4},{7,5},{8,10},{9,11},{10,... | collective-permute-start | bytes 393224 | tf_op jit(solution)/shard_map/ppermute | solution.py:26
  92.4 3.9 %collective-permute-start.13 = (bf16[16,32,128]{2,1,0:T(8,128)(2,1)S(1)}, bf16[16,32,128]{2,1,0:T(8,128)(2,1)S(1)}, u32[]{:S(2)}, u32[]{:S(2)}) collective-permute-start(bf16[16,32,128]{2,1,0:T(8,128)(2,1)S(1)} %owner_last.1.refs_0_), channel_id=1, source_target_pairs={{0,1},{1,0},{2,3},{3,2},{4,5},{5,4},{6,7},{7,6},{8,9},{9,8},{10,11... | collective-permute-start | bytes 393224 | tf_op jit(solution)/shard_map/ppermute | solution.py:26
  95.8 1.4 %collective-permute-start.22 = (bf16[16,32,128]{2,1,0:T(8,128)(2,1)S(1)}, bf16[16,32,128]{2,1,0:T(8,128)(2,1)S(1)}, u32[]{:S(2)}, u32[]{:S(2)}) collective-permute-start(bf16[16,32,128]{2,1,0:T(8,128)(2,1)S(1)} %collective-permute-done.14.refs_2_), channel_id=1, source_target_pairs={{0,1},{1,0},{2,3},{3,2},{4,5},{5,4},{6,7},{7,6},{8,9},{9,8},{10,11... | collective-permute-start | bytes 393224 | tf_op jit(solution)/shard_map/ppermute | solution.py:26
  95.8 1.4 %collective-permute-start.23 = (f32[128,128]{1,0:T(8,128)S(1)}, f32[128,128]{1,0:T(8,128)S(1)}, u32[]{:S(2)}, u32[]{:S(2)}) collective-permute-start(f32[128,128]{1,0:T(8,128)S(1)} %add_add_fusion.refs_4_), channel_id=1, source_target_pairs={{0,1},{1,0},{2,3},{3,2},{4,5},{5,4},{6,7},{7,6},{8,9},{9,8},{10,11... | collective-permute-start | bytes 196616 | tf_op jit(solution)/shard_map/ppermute | solution.py:111

commit v4 on v3

--- a/solution.py
+++ b/solution.py
@@ -63,41 +63,56 @@
     return [held[m] for m in sorted(held)], beside, other
 
 
-def join_kernel(planes, count, me, *refs):
-    pieces, refs = refs[: planes * count], refs[planes * count :]
-    halves, (*outs, sems) = ((), refs) if len(refs) == count + 1 else (refs[:2], refs[2:])
-    copies = [
-        (part, outs[n // planes].at[:, me[0] ^ n % planes]) for n, part in enumerate(pieces)
-    ]
-    for n, total in enumerate(outs[count:]):
-        rows = total.shape[1]
-        copies += [
-            (half.at[n * rows : (n + 1) * rows], total.at[(me[0] & 1) ^ m])
-            for m, half in enumerate(halves)
+def join_kernel(planes, bounce, *refs):
+    me = lax.axis_index("feat")
+    pieces, refs = refs[:planes], refs[planes:]
+    if bounce:
+        out, room, sems, in_sems = refs
+        ins = [
+            pltpu.make_async_copy(piece, room.at[n], in_sems.at[n])
+            for n, piece in enumerate(pieces)
         ]
+        for copy in ins:
+            copy.start()
+        copies = [(room.at[n], out.at[:, me ^ n]) for n in range(planes)]
+    else:
+        ins = []
+        halves, (out, *sums, sems) = refs[:2], refs[2:]
+        copies = [(piece, out.at[:, me ^ n]) for n, piece in enumerate(pieces)]
+        for n, total in enumerate(sums):
+            rows = total.shape[1]
+            copies += [
+                (half.at[n * rows : (n + 1) * rows], total.at[(me & 1) ^ m])
+                for m, half in enumerate(halves)
+            ]
     copies = [pltpu.make_async_copy(a, b, sems.at[n]) for n, (a, b) in enumerate(copies)]
-    for copy in copies:
+    for n, copy in enumerate(copies):
+        if bounce:
+            ins[n].wait()
         copy.start()
     for copy in copies:
         copy.wait()
 
 
-def join_feat(groups, halves, me, params):
-    blocks, width, hidden = groups[0][0].shape
-    planes = lax.axis_size("feat")
+def join_feat(pieces, halves, params):
+    blocks, width, hidden = pieces[0].shape
+    planes = len(pieces)
     count = 2 * halves[0].shape[0] // hidden if halves else 0
-    out_shape = [pltpu.HBM((blocks, planes, width, hidden), BF16)] * len(groups)
+    out_shape = [pltpu.HBM((blocks, planes, width, hidden), BF16)]
     out_shape += [pltpu.HBM((2, hidden // 2, hidden), F32)] * count
-    pieces = [piece for group in groups for piece in group]
+    scratch = [pltpu.SemaphoreType.DMA((planes + 2 * count,))]
+    if not halves:
+        pieces = [in_hbm(piece) for piece in pieces]
+        scratch = [pltpu.VMEM((planes, blocks, width, hidden), BF16), *scratch * 2]
     joined = pl.pallas_call(
-        functools.partial(join_kernel, planes, len(groups)),
+        functools.partial(join_kernel, planes, not halves),
         out_shape=out_shape,
-        in_specs=[SMEM] + [VMEM] * (len(pieces) + len(halves)),
+        in_specs=[VMEM if halves else HBM] * planes + [VMEM] * len(halves),
         out_specs=[HBM] * len(out_shape),
-        scratch_shapes=[pltpu.SemaphoreType.DMA((len(pieces) + 2 * count,))],
+        scratch_shapes=scratch,
         compiler_params=params,
         name="join_rows",
-    )(me, *pieces, *halves)
+    )(*pieces, *halves)
     return [v.reshape(-1, hidden) for v in joined]
 
 
@@ -129,18 +144,14 @@
     return mine + swap_all(other, 1)
 
 
-def pick_kernel(me, ids, rows, w_msg, w_self, *refs):
+def pick_kernel(masks, ids, rows, w_msg, w_self, *refs):
     n_send, peers = ids.shape
     *outs, w_msg_out, w_self_out, room, sems, out_sems = refs
-    near = outs[0].shape[0] // n_send
-    first = me[0] // near * near
-    order = [me[0] ^ m for m in range(near, peers)] + [first + i for i in range(near)]
-    places = [(outs[1 + m], 0) for m in range(peers - near)]
-    places += [(outs[0], i * n_send) for i in range(near)]
+    me = lax.axis_index("edge")
     slots = [(n, j) for n in range(peers) for j in range(n_send)]
     ins = [
         pltpu.make_async_copy(
-            rows.at[ids[j, order[n]]], room.at[n * n_send + j], sems.at[n * n_send + j]
+            rows.at[ids[j, me ^ masks[n]]], room.at[n * n_send + j], sems.at[n * n_send + j]
         )
         for n, j in slots
     ]
@@ -151,7 +162,7 @@
     copies = [
         pltpu.make_async_copy(
             room.at[n * n_send + j],
-            places[n][0].at[places[n][1] + j],
+            outs[n].at[j],
             out_sems.at[n * n_send + j],
         )
         for n, j in slots
@@ -165,20 +176,21 @@
         copy.wait()
 
 
-def pieces_of(me, raw):
-    near, *far = raw
-    per_owner = far[0].shape[0] if far else near.shape[0]
-    owners = near.shape[0] // per_owner
-    yield me // owners * owners * per_owner, near
-    for m, rows in enumerate(far):
-        yield (me ^ (owners + m)) * per_owner, rows
-
-
-def fetch_kernel(me, *refs):
+def pieces_of(masks, raw):
+    me = lax.axis_index("edge")
+    return [((me ^ mask) * rows.shape[0], rows) for mask, rows in zip(masks, raw)]
+
+
+def mask_order(peers):
+    return sorted(range(peers), key=lambda m: (-m.bit_length(), -m))
+
+
+def fetch_kernel(quarter, *refs):
     *ins, out, sems = refs
+    me = lax.axis_index("feat")
     copies = [
         pltpu.make_async_copy(
-            a if me is None else a.at[:, me[0]], out if me is None else out.at[n], sems.at[n]
+            a.at[:, me] if quarter else a, out.at[n] if quarter else out, sems.at[n]
         )
         for n, a in enumerate(ins)
     ]
@@ -188,14 +200,11 @@
         copy.wait()
 
 
-def fetch(me, arrays, dims, params, name):
-    kernel, specs, args = fetch_kernel, [SMEM], [me]
-    if me is None:
-        kernel, specs, args = functools.partial(fetch_kernel, None), [], []
+def fetch(quarter, arrays, dims, params, name):
     return pl.pallas_call(
-        kernel,
+        functools.partial(fetch_kernel, quarter),
         out_shape=pltpu.VMEM(dims, BF16),
-        in_specs=specs + [HBM] * len(arrays),
+        in_specs=[HBM] * len(arrays),
         out_specs=VMEM,
         scratch_shapes=[pltpu.SemaphoreType.DMA((len(arrays),))],
         compiler_params=params,
@@ -203,7 +212,7 @@
             flops=0, bytes_accessed=4 * math.prod(dims), transcendentals=0
         ),
         name=name,
-    )(*args, *arrays)
+    )(*arrays)
 
 
 def edge_loop(group, count, term, put):
@@ -233,14 +242,14 @@
 
 
 def forward_kernel(
-    group, live, me, src_in, dst_in, w_msg, adj, *refs
+    group, masks, live, src_in, dst_in, w_msg, adj, *refs
 ):
     *raw, out, msgs, acc, room, src, dst, sems, out_sems = refs
     slots, block, hidden = msgs.shape
     per_owner, width = out.shape[1:3]
     planes = block // width
     ids = copy_ids([(src_in, src), (dst_in, dst)], sems)
-    for first, rows in pieces_of(me[0], raw):
+    for first, rows in pieces_of(masks, raw):
         flat = rows[...].reshape(-1, hidden)
         piece = jnp.dot(flat, w_msg[...], preferred_element_type=F32).astype(BF16)
         msgs[pl.ds(first, rows.shape[0])] = piece.reshape(rows.shape)
@@ -302,7 +311,7 @@
         copy.wait()
 
 
-def backward_kernel(group, live, me, src_in, dst_in, got, adj, *refs):
+def backward_kernel(group, masks, live, src_in, dst_in, got, adj, *refs):
     *raw, out, w_part, turned, acc, room, src, dst, sems, out_sems = refs
     slots, hidden, block = acc.shape
     slots -= 1
@@ -328,12 +337,12 @@
     copies = []
     for p in range(devices // planes):
         for j in range(out_slots):
-            back = acc[p * out_slots + j].T.astype(BF16)
+            back = acc[p * out_slots + j].astype(BF16).T
             for q in range(planes):
                 room[p * planes + q, j] = back[q * width : (q + 1) * width]
         copies.append(send_out(room, out, out_sems, p, planes))
     total = jnp.zeros((hidden, hidden), F32)
-    for first, rows in pieces_of(me[0], raw):
+    for first, rows in pieces_of(masks, raw):
         for s in range(rows.shape[0]):
             total += jnp.dot(acc[first + s].astype(BF16), rows[s], preferred_element_type=F32)
     w_part[...] = total.T
@@ -393,24 +402,19 @@
     send_all = ids[:, :, :n_send].reshape(-1)
     recv_all = ids[:, :, n_send:].reshape(-1)
 
-    wide_feat = in_hbm(node_feat.reshape(blocks, planes, width, hidden))
-    wide_cot = in_hbm(cotangent.reshape(blocks, planes, width, hidden))
     square = pltpu.VMEM((hidden, hidden), BF16)
     sum_part = pltpu.VMEM((hidden, hidden), F32)
     rows_out = (peers * n_send, block, hidden)
     recv_out = (devices, n_recv, width, hidden)
     send_out_dims = (devices, n_send, width, hidden)
     out_sems = pltpu.SemaphoreType.DMA((peers,))
-    here = lax.axis_index("edge").reshape(1).astype(jnp.int32)
-    near = peers // 2 if is_pow2(peers) and 1 < peers <= 16 else peers
+    masks = mask_order(peers)
     few = (n_send, block, hidden)
     *outgoing, w_msg, w_self = pl.pallas_call(
-        pick_kernel,
-        out_shape=[pltpu.HBM((near * n_send, block, hidden), BF16)]
-        + [pltpu.HBM(few, BF16)] * (peers - near)
-        + [square, square],
-        in_specs=[SMEM] * 2 + [HBM] * 3,
-        out_specs=[HBM] * (peers - near + 1) + [VMEM, VMEM],
+        functools.partial(pick_kernel, masks),
+        out_shape=[pltpu.HBM(few, BF16)] * peers + [square, square],
+        in_specs=[SMEM] + [HBM] * 3,
+        out_specs=[HBM] * peers + [VMEM, VMEM],
         scratch_shapes=[
             pltpu.VMEM(rows_out, BF16),
             pltpu.SemaphoreType.DMA((peers * n_send + 2,)),
@@ -419,24 +423,20 @@
         compiler_params=params,
         name="pick_rows",
     )(
-        here,
         in_hbm(send_src.transpose(0, 1, 3, 2).reshape(n_send, peers)),
         in_hbm(node_feat.reshape(blocks, block, hidden)),
         in_hbm(w_msg),
         in_hbm(w_self),
     )
-    raw = [swap(rows, "edge", near + m) for m, rows in enumerate(outgoing[1:])]
-    groups = [list(range(g, g + near)) for g in range(0, peers, near)]
-    raw = [
-        lax.all_to_all(outgoing[0], "edge", 0, 0, tiled=True, axis_index_groups=groups)
-    ] + raw
-
-    adj = fetch(None, [adj], adj.shape, params, "fetch_edges")
-    ids_room = [pltpu.SMEM(src.shape, src.dtype)] * 2 + [pltpu.SemaphoreType.DMA((2,))]
+    raw = [swap(rows, "edge", mask) if mask else rows for mask, rows in zip(masks, outgoing)]
+
+    adj = fetch(False, [adj], adj.shape, params, "fetch_edges")
+    ids_room = [pltpu.SMEM(v.shape, v.dtype) for v in (src, dst)]
+    ids_room.append(pltpu.SemaphoreType.DMA((2,)))
     partials = pl.pallas_call(
-        functools.partial(forward_kernel, group),
+        functools.partial(forward_kernel, group, masks),
         out_shape=pltpu.HBM(recv_out, BF16),
-        in_specs=[SMEM] * 2 + [HBM] * 2 + [VMEM] * (2 + len(raw)),
+        in_specs=[SMEM] + [HBM] * 2 + [VMEM] * (2 + len(raw)),
         out_specs=HBM,
         scratch_shapes=[
             pltpu.VMEM((peers * n_send, block, hidden), BF16),
@@ -447,10 +447,14 @@
         ],
         compiler_params=params,
         name="edge_forward",
-    )(count, here, src, dst, w_msg, adj, *raw)
-    later, partials = lax.optimization_barrier((me, partials))
+    )(count, src, dst, w_msg, adj, *raw)
+    wide_feat, wide_cot, partials = lax.optimization_barrier(
+        (node_feat, cotangent, partials)
+    )
+    wide_feat = in_hbm(wide_feat.reshape(blocks, planes, width, hidden))
+    wide_cot = in_hbm(wide_cot.reshape(blocks, planes, width, hidden))
     got = lax.all_to_all(partials, BOTH, 0, 0, tiled=True)
-    rows = fetch(later, [wide_feat, wide_cot], (2, blocks, width, hidden), params, "fetch_rows")
+    rows = fetch(True, [wide_feat, wide_cot], (2, blocks, width, hidden), params, "fetch_rows")
 
     out_part, grad_pre, grad_out, wself_part = pl.pallas_call(
         owner_kernel,
@@ -474,16 +478,17 @@
     )(recv_all, got, rows, w_self)
     grad_in = lax.all_to_all(grad_out, BOTH, 0, 0, tiled=True)
     out_pieces, _, _ = pieces_feat(out_part)
-    (out_feat,) = join_feat([out_pieces], [], me, params)
     wself_part = split_core(wself_part, me)
     for bits in stages[1:2]:
         wself_part = sum_stage(wself_part, bits)
-    grad_in, out_feat, wself_part = lax.optimization_barrier((grad_in, out_feat, wself_part))
+    grad_in, out_pieces, wself_part = lax.optimization_barrier(
+        (grad_in, out_pieces, wself_part)
+    )
 
     grad_partials, wmsg_part = pl.pallas_call(
-        functools.partial(backward_kernel, group),
+        functools.partial(backward_kernel, group, masks),
         out_shape=(pltpu.HBM(send_out_dims, BF16), sum_part),
-        in_specs=[SMEM] * 2 + [HBM] * 2 + [VMEM] * (2 + len(raw)),
+        in_specs=[SMEM] + [HBM] * 2 + [VMEM] * (2 + len(raw)),
         out_specs=(HBM, VMEM),
         scratch_shapes=[
             pltpu.VMEM((peers * n_recv, hidden, block), BF16),
@@ -494,10 +499,11 @@
         ],
         compiler_params=params,
         name="edge_backward",
-    )(count, here, src, dst, grad_in, adj, *raw)
-    grad_partials, wmsg_part, wself_part = lax.optimization_barrier(
-        (grad_partials, wmsg_part, wself_part)
-    )
+    )(count, src, dst, grad_in, adj, *raw)
+    grad_partials, wmsg_part, wself_part, out_pieces = lax.optimization_barrier(
+        (grad_partials, wmsg_part, wself_part, out_pieces)
+    )
+    (out_feat,) = join_feat(out_pieces, [], params)
     grad_back = lax.all_to_all(grad_partials, BOTH, 0, 0, tiled=True)
     wmsg_part = split_core(wmsg_part, me)
     for bits in stages[1:2]:
@@ -506,6 +512,8 @@
     for bits in stages[2:]:
         sums = sum_stage(sums.astype(BF16), bits)
 
+    grad_back, out_feat = lax.optimization_barrier((grad_back, out_feat))
+
     grad_part = pl.pallas_call(
         last_kernel,
         out_shape=pltpu.VMEM((blocks, width, hidden), BF16),
@@ -516,7 +524,7 @@
         name="owner_last",
     )(send_all, grad_back, grad_pre, w_self, w_msg)
     grad_pieces, sums, other = pieces_feat(grad_part, sums)
-    grad_feat, grad_wself, grad_wmsg = join_feat([grad_pieces], [sums, other], me, params)
+    grad_feat, grad_wself, grad_wmsg = join_feat(grad_pieces, [sums, other], params)
     return (out_feat, grad_feat, grad_wmsg, grad_wself)
 
 

time: 98.8 us -> 96.8 us (0.980)
  waiting for transfers between devices: 37.3 us -> 34.5 us
    all_to_all x1 -> x0, starting transfers between devices: 5.25 us -> none  [body(): lax.all_to_all(outgoing[0], 'edge', 0, 0, tiled=True, axis_index_groups=g...]
    ppermute x12 -> x15, starting transfers between devices: 13.6 us -> 18.4 us  [swap(): return lax.ppermute(x, axis, [(j, j ^ bit) for j in range(size)])]
    ppermute x12 -> x15, waiting for transfers between devices: 17.6 us -> 15.1 us  [swap(): return lax.ppermute(x, axis, [(j, j ^ bit) for j in range(size)])]
    all_to_all x1, starting transfers between devices: 3.64 us -> 5.48 us  [body(): got = lax.all_to_all(partials, BOTH, 0, 0, tiled=True)]
    all_to_all x1, waiting for transfers between devices: 2.25 us -> 0.42 us  [body(): grad_back = lax.all_to_all(grad_partials, BOTH, 0, 0, tiled=True)]
    all_to_all x1, waiting for transfers between devices: 1.04 us -> 2.63 us  [body(): grad_in = lax.all_to_all(grad_out, BOTH, 0, 0, tiled=True)]
  transfers between devices with their start and end apart: 28 -> 30, of which waited for: 16 -> 18; matrix products, arithmetic and copies ran while one was open for 1% -> 1% of each run, Pallas kernels for 4% -> 6%
where the time goes in v4:
time: 96.8 us; the launch traced here: 96.5 us
  starting transfers between devices  42.3 us (44%)
  waiting for transfers between devices  34.5 us (36%)
  Pallas kernels  16.9 us (17%)
  between operations  1.53 us (2%)
  local copies, waits for them, and re-layouts  1.11 us (1%)
    ppermute x15, starting transfers between devices, swap(): return lax.ppermute(x, axis, [(j, j ^ bit) for j in range(size)])  18.4 us
    ppermute x15, waiting for transfers between devices, swap(): return lax.ppermute(x, axis, [(j, j ^ bit) for j in range(size)])  15.1 us
    ppermute x12, starting transfers between devices, swap_all(): return lax.ppermute(x, BOTH, [(j, j ^ mask) for j in range(count)])  12.6 us
    all_to_all x1, waiting for transfers between devices, body(): got = lax.all_to_all(partials, BOTH, 0, 0, tiled=True)  9.44 us
    ppermute x12, waiting for transfers between devices, swap_all(): return lax.ppermute(x, BOTH, [(j, j ^ mask) for j in range(count)])  6.9 us
    all_to_all x1, starting transfers between devices, body(): got = lax.all_to_all(partials, BOTH, 0, 0, tiled=True)  5.48 us
    pallas_call x1, Pallas kernels, body(): pl.pallas_call(functools.partial(backward_kernel, group, masks), out_shap...  3.11 us
    all_to_all x1, starting transfers between devices, body(): grad_in = lax.all_to_all(grad_out, BOTH, 0, 0, tiled=True)  3.08 us
  transfers between devices with their start and end apart: 30, of which 18 were waited for; matrix products, arithmetic and copies ran while one was open for 1% of the time, Pallas kernels for 6%

profile of v4, /device:TPU:0, one launch (start us, length us, event | category | flops | bytes accessed | tf_op | source)
XLA Modules:
  0.0 96.5 jit_solution(8295795729430077942)
XLA Ops:
  0.6 2.7 %pick_rows.1 = (bf16[2,128,128]{2,1,0:T(8,128)(2,1)}, bf16[2,128,128]{2,1,0:T(8,128)(2,1)}, bf16[2,128,128]{2,1,0:T(8,128)(2,1)}, bf16[2,128,128]{2,1,0:T(8,128)...) custom-call(s32[2,8]{1,0:T(2,128)} %bitcast.27, ...), custom_call_target="tpu_custom_call" | custom-call | tf_op jit(solution)/shard_map/pick_rows/pallas_call | solution.py:413
  3.4 6.0 %collective-permute-start.2 = (bf16[2,128,128]{2,1,0:T(8,128)(2,1)}, bf16[2,128,128]{2,1,0:T(8,128)(2,1)S(1)}, u32[]{:S(2)}, u32[]{:S(2)}) collective-permute-start(bf16[2,128,128]{2,1,0:T(8,128)(2,1)} %get-tuple-element.44), channel_id=1, source_target_pairs={{0,28},{4,24},{8,20},{12,16},{16,12},{20,8},{24,4},{28,0},{1,29},{... | collective-permute-start | bytes 196616 | tf_op jit(solution)/shard_map/ppermute | solution.py:26
  9.7 0.8 collective-permute-start.4
  10.5 2.0 %collective-permute-start.5 = (bf16[2,128,128]{2,1,0:T(8,128)(2,1)}, bf16[2,128,128]{2,1,0:T(8,128)(2,1)S(1)}, u32[]{:S(2)}, u32[]{:S(2)}) collective-permute-start(bf16[2,128,128]{2,1,0:T(8,128)(2,1)} %get-tuple-element.47), channel_id=1, source_target_pairs={{0,16},{4,20},{8,24},{12,28},{16,0},{20,4},{24,8},{28,12},{1,17},{... | collective-permute-start | bytes 196616 | tf_op jit(solution)/shard_map/ppermute | solution.py:26
  12.4 2.3 %collective-permute-start.6 = (bf16[2,128,128]{2,1,0:T(8,128)(2,1)}, bf16[2,128,128]{2,1,0:T(8,128)(2,1)S(1)}, u32[]{:S(2)}, u32[]{:S(2)}) collective-permute-start(bf16[2,128,128]{2,1,0:T(8,128)(2,1)} %get-tuple-element.48), channel_id=1, source_target_pairs={{0,12},{4,8},{8,4},{12,0},{16,28},{20,24},{24,20},{28,16},{1,13},{... | collective-permute-start | bytes 196616 | tf_op jit(solution)/shard_map/ppermute | solution.py:26
  14.7 0.8 collective-permute-start.7
  15.9 0.4 collective-permute-start.8
  17.0 1.6 %fetch_edges.1.adj = bf16[64,128,128]{2,1,0:T(8,128)(2,1)S(1)} custom-call(bf16[64,128,128]{2,1,0:T(8,128)(2,1)} %bitcast.22), custom_call_target="tpu_custom_call" | custom-call | bytes 4194304 | tf_op jit(solution)/shard_map/fetch_edges/pallas_call | solution.py:204
  18.6 0.4 collective-permute-done.4.refs_2_
  19.0 1.9 %collective-permute-done.5.refs_3_ = bf16[2,128,128]{2,1,0:T(8,128)(2,1)S(1)} collective-permute-done((bf16[2,128,128]{2,1,0:T(8,128)(2,1)}, bf16[2,128,128]{2,1,0:T(8,128)(2,1)S(1)}, u32[]{:S(2)}, u32[]{:S(2)}) %collective-permute-start.5) | collective-permute-done | bytes 65568 | tf_op jit(solution)/shard_map/ppermute | solution.py:26
  20.9 0.4 collective-permute-done.7.refs_5_
  21.3 2.9 %edge_forward.1 = bf16[32,2,32,128]{3,2,1,0:T(8,128)(2,1)} custom-call(s32[1]{0:T(128)} %bitcast.20.live, s32[64]{0:T(128)} %bitcast.29, s32[64]{0:T(128)} %bitcast.31, bf16[128,128]{1,0:T(8,128)(2,1)S(1)} %get-tuple-element.43.w_msg, bf16[64,128,128]{2,1,0:T(8,128)(2,1)S(1)} %fetch_edges.1.adj, bf16[2,128,128]{2,1,0:T(8,128)(2,1)S(1)} %collective-permute-done.2.refs_0_, ...), custom_call_target="tpu_custom_call" | custom-call | tf_op jit(solution)/shard_map/edge_forward/pallas_call | solution.py:436
  24.2 5.5 %all-to-all-start = ((bf16[32,2,32,128]{3,2,1,0:T(8,128)(2,1)}), bf16[32,2,32,128]{3,2,1,0:T(8,128)(2,1)S(1)}, u32[]{:S(2)}, u32[]{:S(2)}) async-start(bf16[32,2,32,128]{3,2,1,0:T(8,128)(2,1)} %edge_forward.1), calls=%async_computation | async-start | bytes 1048576 | tf_op jit(solution)/shard_map/all_to_all | solution.py:456
  29.8 0.3 collective-permute-start
  30.1 0.9 collective-permute-done
  31.0 1.8 %collective-permute-start.1 = (s32[2,8,4]{1,2,0:T(4,128)S(1)}, s32[2,8,4]{1,2,0:T(4,128)S(1)}, u32[]{:S(2)}, u32[]{:S(2)}) collective-permute-start(s32[2,8,4]{1,2,0:T(4,128)S(1)} %add_select_fusion.1), channel_id=1, source_target_pairs={{0,2},{1,3},{2,0},{3,1},{4,6},{5,7},{6,4},{7,5},{8,10},{9,11},{10,... | collective-permute-start | bytes 776 | tf_op jit(solution)/shard_map/ppermute | solution.py:26
  32.8 1.8 %collective-permute-done.1 = s32[2,8,4]{1,2,0:T(4,128)S(1)} collective-permute-done((s32[2,8,4]{1,2,0:T(4,128)S(1)}, s32[2,8,4]{1,2,0:T(4,128)S(1)}, u32[]{:S(2)}, u32[]{:S(2)}) %collective-permute-start.1) | collective-permute-done | bytes 288 | tf_op jit(solution)/shard_map/ppermute | solution.py:26
  34.8 1.0 %fetch_rows.1.rows = bf16[2,16,32,128]{3,2,1,0:T(8,128)(2,1)S(1)} custom-call(bf16[16,4,32,128]{3,2,1,0:T(8,128)(2,1)} %bitcast.24, bf16[16,4,32,128]{3,2,1,0:T(8,128)(2,1)} %bitcast.25), custom_call_target="tpu_custom_call" | custom-call | bytes 524288 | tf_op jit(solution)/shard_map/fetch_rows/pallas_call | solution.py:204
  35.8 9.4 %all-to-all-done.got = bf16[32,2,32,128]{3,2,1,0:T(8,128)(2,1)S(1)} async-done(((bf16[32,2,32,128]{3,2,1,0:T(8,128)(2,1)}), bf16[32,2,32,128]{3,2,1,0:T(8,128)(2,1)S(1)}, u32[]{:S(2)}, u32[]{:S(2)}) %all-to-all-start) | async-done | bytes 524320 | tf_op jit(solution)/shard_map/all_to_all | solution.py:456
  45.3 1.9 %owner_dense.1 = (bf16[16,32,128]{2,1,0:T(8,128)(2,1)}, bf16[16,32,128]{2,1,0:T(8,128)(2,1)}, bf16[32,2,32,128]{3,2,1,0:T(8,128)(2,1)}, f32[128,128]{1,0:T(8,128)S(1)}) custom-call(s32[64]{0:T(128)S(1)} %reshape.78.ids, bf16[32,2,32,128]{3,2,1,0:T(8,128)(2,1)S(1)} %all-to-all-done.got, bf16[2,16,32,128]{3,2,1,0:T(8,128)(2,1)S(1)} %fetch_rows.1.rows, ...), custom_call_target="tpu_custom_call" | custom-call | tf_op jit(solution)/shard_map/owner_dense/pallas_call | solution.py:459
  47.1 3.1 %all-to-all-start.1 = ((bf16[32,2,32,128]{3,2,1,0:T(8,128)(2,1)}), bf16[32,2,32,128]{3,2,1,0:T(8,128)(2,1)S(1)}, u32[]{:S(2)}, u32[]{:S(2)}) async-start(bf16[32,2,32,128]{3,2,1,0:T(8,128)(2,1)} %get-tuple-element.56), calls=%async_computation.1 | async-start | bytes 1048576 | tf_op jit(solution)/shard_map/all_to_all | solution.py:479
  50.6 1.7 %collective-permute-start.10 = (bf16[16,32,128]{2,1,0:T(8,128)(2,1)}, bf16[16,32,128]{2,1,0:T(8,128)(2,1)S(1)}, u32[]{:S(2)}, u32[]{:S(2)}) collective-permute-start(bf16[16,32,128]{2,1,0:T(8,128)(2,1)} %get-tuple-element.68.refs_0_), channel_id=1, source_target_pairs={{0,2},{1,3},{2,0},{3,1},{4,6},{5,7},{6,4},{7,5},{8,10},{9,11},{10,... | collective-permute-start | bytes 393224 | tf_op jit(solution)/shard_map/ppermute | solution.py:26
  52.3 1.9 %collective-permute-start.15 = (f32[64,128]{1,0:T(8,128)S(1)}, f32[64,128]{1,0:T(8,128)S(1)}, u32[]{:S(2)}, u32[]{:S(2)}) collective-permute-start(f32[64,128]{1,0:T(8,128)S(1)} %select_add_fusion.1), channel_id=1, source_target_pairs={{0,6},{1,7},{2,4},{3,5},{4,2},{5,3},{6,0},{7,1},{8,14},{9,15},{10,... | collective-permute-start | bytes 98312 | tf_op jit(solution)/shard_map/ppermute | solution.py:126
  54.2 0.6 collective-permute-start.14
  54.8 1.1 %collective-permute-start.13 = (f32[64,128]{1,0:T(8,128)S(1)}, f32[64,128]{1,0:T(8,128)S(1)}, u32[]{:S(2)}, u32[]{:S(2)}) collective-permute-start(f32[64,128]{1,0:T(8,128)S(1)} %select_add_fusion.1), channel_id=1, source_target_pairs={{0,2},{1,3},{2,0},{3,1},{4,6},{5,7},{6,4},{7,5},{8,10},{9,11},{10,... | collective-permute-start | bytes 98312 | tf_op jit(solution)/shard_map/ppermute | solution.py:126
  55.8 5.9 %collective-permute-done.10.refs_2_ = bf16[16,32,128]{2,1,0:T(8,128)(2,1)S(1)} collective-permute-done((bf16[16,32,128]{2,1,0:T(8,128)(2,1)}, bf16[16,32,128]{2,1,0:T(8,128)(2,1)S(1)}, u32[]{:S(2)}, u32[]{:S(2)}) %collective-permute-start.10) | collective-permute-done | bytes 131104 | tf_op jit(solution)/shard_map/ppermute | solution.py:26
  61.7 0.6 collective-permute-done.13
  62.3 0.6 copy-done.3
  63.2 2.6 %all-to-all-done.1.got = bf16[32,2,32,128]{3,2,1,0:T(8,128)(2,1)S(1)} async-done(((bf16[32,2,32,128]{3,2,1,0:T(8,128)(2,1)}), bf16[32,2,32,128]{3,2,1,0:T(8,128)(2,1)S(1)}, u32[]{:S(2)}, u32[]{:S(2)}) %all-to-all-start.1) | async-done | bytes 524320 | tf_op jit(solution)/shard_map/all_to_all | solution.py:479
  65.8 3.1 %edge_backward.1 = (bf16[32,2,32,128]{3,2,1,0:T(8,128)(2,1)}, f32[128,128]{1,0:T(8,128)S(1)}) custom-call(s32[1]{0:T(128)} %bitcast.21.live, s32[64]{0:T(128)} %bitcast.30, s32[64]{0:T(128)} %bitcast.32, bf16[32,2,32,128]{3,2,1,0:T(8,128)(2,1)S(1)} %all-to-all-done.1.got, bf16[64,128,128]{2,1,0:T(8,128)(2,1)S(1)} %fetch_edges.1.adj, ...), custom_call_target="tpu_custom_call" | custom-call | tf_op jit(solution)/shard_map/edge_backward/pallas_call | solution.py:488
  68.9 2.8 %all-to-all-start.2 = ((bf16[32,2,32,128]{3,2,1,0:T(8,128)(2,1)}), bf16[32,2,32,128]{3,2,1,0:T(8,128)(2,1)S(1)}, u32[]{:S(2)}, u32[]{:S(2)}) async-start(bf16[32,2,32,128]{3,2,1,0:T(8,128)(2,1)} %get-tuple-element.67), calls=%async_computation.2 | async-start | bytes 1048576 | tf_op jit(solution)/shard_map/all_to_all | solution.py:507
  72.0 1.0 collective-permute-done.18
  73.0 2.7 %collective-permute-start.21 = (f32[64,128]{1,0:T(8,128)S(1)}, f32[64,128]{1,0:T(8,128)S(1)}, u32[]{:S(2)}, u32[]{:S(2)}) collective-permute-start(f32[64,128]{1,0:T(8,128)S(1)} %select_add_fusion), channel_id=1, source_target_pairs={{0,6},{1,7},{2,4},{3,5},{4,2},{5,3},{6,0},{7,1},{8,14},{9,15},{10,... | collective-permute-start | bytes 98312 | tf_op jit(solution)/shard_map/ppermute | solution.py:126
  75.6 0.6 collective-permute-start.20
  76.5 3.4 %collective-permute-done.21 = f32[64,128]{1,0:T(8,128)S(1)} collective-permute-done((f32[64,128]{1,0:T(8,128)S(1)}, f32[64,128]{1,0:T(8,128)S(1)}, u32[]{:S(2)}, u32[]{:S(2)}) %collective-permute-start.21) | collective-permute-done | bytes 32800 | tf_op jit(solution)/shard_map/ppermute | solution.py:126
  79.8 0.4 collective-permute-done.20
  80.2 0.7 collective-permute-done.19
  80.9 1.8 %collective-permute-start.23 = (bf16[128,128]{1,0:T(8,128)(2,1)S(1)}, bf16[128,128]{1,0:T(8,128)(2,1)S(1)}, u32[]{:S(2)}, u32[]{:S(2)}) collective-permute-start(bf16[128,128]{1,0:T(8,128)(2,1)S(1)} %pad_maximum_fusion), channel_id=1, source_target_pairs={{0,16},{1,17},{2,18},{3,19},{4,20},{5,21},{6,22},{7,23},{8,24},{9,... | collective-permute-start | bytes 98312 | tf_op jit(solution)/shard_map/ppermute | solution.py:126
  82.8 2.0 %collective-permute-start.22 = (bf16[128,128]{1,0:T(8,128)(2,1)S(1)}, bf16[128,128]{1,0:T(8,128)(2,1)S(1)}, u32[]{:S(2)}, u32[]{:S(2)}) collective-permute-start(bf16[128,128]{1,0:T(8,128)(2,1)S(1)} %pad_maximum_fusion), channel_id=1, source_target_pairs={{0,8},{1,9},{2,10},{3,11},{4,12},{5,13},{6,14},{7,15},{8,0},{9,1},... | collective-permute-start | bytes 98312 | tf_op jit(solution)/shard_map/ppermute | solution.py:126
  84.7 0.7 collective-permute-start.24
  85.6 1.8 %join_rows.2 = bf16[16,4,32,128]{3,2,1,0:T(8,128)(2,1)} custom-call(bf16[16,32,128]{2,1,0:T(8,128)(2,1)} %get-tuple-element.68.refs_0_, bf16[16,32,128]{2,1,0:T(8,128)(2,1)} %copy-done.3, bf16[16,32,128]{2,1,0:T(8,128)(2,1)} %copy-done.2, bf16[16,32,128]{2,1,0:T(8,128)(2,1)} %collective-permute-done.11.refs_3_), custom_call_target="tpu_custom_call" | custom-call | tf_op jit(solution)/shard_map/join_rows/pallas_call | solution.py:107
  87.4 0.4 all-to-all-done.2.got
  87.9 1.0 %owner_last.1.refs_0_ = bf16[16,32,128]{2,1,0:T(8,128)(2,1)S(1)} custom-call(s32[64]{0:T(128)S(1)} %reshape.85.ids, bf16[32,2,32,128]{3,2,1,0:T(8,128)(2,1)S(1)} %all-to-all-done.2.got, bf16[16,32,128]{2,1,0:T(8,128)(2,1)S(1)} %copy-done.1, bf16[128,128]{1,0:T(8,128)(2,1)S(1)} %get-tuple-element.55.w_self, bf16[128,128]{1,0:T(8,128)(2,1)S(1)} %get-tuple-element.43.w_msg), custom_call_target="tpu_custom_call" | custom-call | tf_op jit(solution)/shard_map/owner_last/pallas_call | solution.py:517
  88.9 1.9 %collective-permute-start.17 = (bf16[16,32,128]{2,1,0:T(8,128)(2,1)S(1)}, bf16[16,32,128]{2,1,0:T(8,128)(2,1)S(1)}, u32[]{:S(2)}, u32[]{:S(2)}) collective-permute-start(bf16[16,32,128]{2,1,0:T(8,128)(2,1)S(1)} %owner_last.1.refs_0_), channel_id=1, source_target_pairs={{0,2},{1,3},{2,0},{3,1},{4,6},{5,7},{6,4},{7,5},{8,10},{9,11},{10,... | collective-permute-start | bytes 393224 | tf_op jit(solution)/shard_map/ppermute | solution.py:26
  90.9 3.3 %collective-permute-done.17.refs_2_ = bf16[16,32,128]{2,1,0:T(8,128)(2,1)S(1)} collective-permute-done((bf16[16,32,128]{2,1,0:T(8,128)(2,1)S(1)}, bf16[16,32,128]{2,1,0:T(8,128)(2,1)S(1)}, u32[]{:S(2)}, u32[]{:S(2)}) %collective-permute-start.17) | collective-permute-done | bytes 131104 | tf_op jit(solution)/shard_map/ppermute | solution.py:26
  94.2 0.5 collective-permute-start.26
  94.7 0.9 collective-permute-done.26.refs_5_
  95.6 0.9 join_rows.3
  (49 shorter events, 2.4 us)
Async XLA Ops:
  3.4 11.3 %collective-permute-start.2 = (bf16[2,128,128]{2,1,0:T(8,128)(2,1)}, bf16[2,128,128]{2,1,0:T(8,128)(2,1)S(1)}, u32[]{:S(2)}, u32[]{:S(2)}) collective-permute-start(bf16[2,128,128]{2,1,0:T(8,128)(2,1)} %get-tuple-element.44), channel_id=1, source_target_pairs={{0,28},{4,24},{8,20},{12,16},{16,12},{20,8},{24,4},{28,0},{1,29},{... | collective-permute-start | bytes 196616 | tf_op jit(solution)/shard_map/ppermute | solution.py:26
  9.4 6.4 %collective-permute-start.3 = (bf16[2,128,128]{2,1,0:T(8,128)(2,1)}, bf16[2,128,128]{2,1,0:T(8,128)(2,1)S(1)}, u32[]{:S(2)}, u32[]{:S(2)}) collective-permute-start(bf16[2,128,128]{2,1,0:T(8,128)(2,1)} %get-tuple-element.45), channel_id=1, source_target_pairs={{0,24},{4,28},{8,16},{12,20},{16,8},{20,12},{24,0},{28,4},{1,25},{... | collective-permute-start | bytes 196616 | tf_op jit(solution)/shard_map/ppermute | solution.py:26
  9.7 9.3 %collective-permute-start.4 = (bf16[2,128,128]{2,1,0:T(8,128)(2,1)}, bf16[2,128,128]{2,1,0:T(8,128)(2,1)S(1)}, u32[]{:S(2)}, u32[]{:S(2)}) collective-permute-start(bf16[2,128,128]{2,1,0:T(8,128)(2,1)} %get-tuple-element.46), channel_id=1, source_target_pairs={{0,20},{4,16},{8,28},{12,24},{16,4},{20,0},{24,12},{28,8},{1,21},{... | collective-permute-start | bytes 196616 | tf_op jit(solution)/shard_map/ppermute | solution.py:26
  10.5 10.5 %collective-permute-start.5 = (bf16[2,128,128]{2,1,0:T(8,128)(2,1)}, bf16[2,128,128]{2,1,0:T(8,128)(2,1)S(1)}, u32[]{:S(2)}, u32[]{:S(2)}) collective-permute-start(bf16[2,128,128]{2,1,0:T(8,128)(2,1)} %get-tuple-element.47), channel_id=1, source_target_pairs={{0,16},{4,20},{8,24},{12,28},{16,0},{20,4},{24,8},{28,12},{1,17},{... | collective-permute-start | bytes 196616 | tf_op jit(solution)/shard_map/ppermute | solution.py:26
  12.4 8.5 %collective-permute-start.6 = (bf16[2,128,128]{2,1,0:T(8,128)(2,1)}, bf16[2,128,128]{2,1,0:T(8,128)(2,1)S(1)}, u32[]{:S(2)}, u32[]{:S(2)}) collective-permute-start(bf16[2,128,128]{2,1,0:T(8,128)(2,1)} %get-tuple-element.48), channel_id=1, source_target_pairs={{0,12},{4,8},{8,4},{12,0},{16,28},{20,24},{24,20},{28,16},{1,13},{... | collective-permute-start | bytes 196616 | tf_op jit(solution)/shard_map/ppermute | solution.py:26
  14.7 6.6 %collective-permute-start.7 = (bf16[2,128,128]{2,1,0:T(8,128)(2,1)}, bf16[2,128,128]{2,1,0:T(8,128)(2,1)S(1)}, u32[]{:S(2)}, u32[]{:S(2)}) collective-permute-start(bf16[2,128,128]{2,1,0:T(8,128)(2,1)} %get-tuple-element.49), channel_id=1, source_target_pairs={{0,8},{4,12},{8,0},{12,4},{16,24},{20,28},{24,16},{28,20},{1,9},{5... | collective-permute-start | bytes 196616 | tf_op jit(solution)/shard_map/ppermute | solution.py:26
  15.9 5.5 %collective-permute-start.8 = (bf16[2,128,128]{2,1,0:T(8,128)(2,1)}, bf16[2,128,128]{2,1,0:T(8,128)(2,1)S(1)}, u32[]{:S(2)}, u32[]{:S(2)}) collective-permute-start(bf16[2,128,128]{2,1,0:T(8,128)(2,1)} %get-tuple-element.50), channel_id=1, source_target_pairs={{0,4},{4,0},{8,12},{12,8},{16,20},{20,16},{24,28},{28,24},{1,5},{5... | collective-permute-start | bytes 196616 | tf_op jit(solution)/shard_map/ppermute | solution.py:26
  16.9 4.4 %copy-start = (bf16[2,128,128]{2,1,0:T(8,128)(2,1)S(1)}, bf16[2,128,128]{2,1,0:T(8,128)(2,1)}, u32[]{:S(2)}) copy-start(bf16[2,128,128]{2,1,0:T(8,128)(2,1)} %get-tuple-element.51.refs_7_) | copy-start | bytes 196612
  21.3 8.4 %copy-start.4 = (s32[1,1,8,2]{2,3,1,0:T(2,128)S(1)}, s32[1,1,8,2]{2,3,1,0:T(2,128)}, u32[]{:S(2)}) copy-start(s32[1,1,8,2]{2,3,1,0:T(2,128)} %param.17) | copy-start | bytes 196
  21.3 8.4 %copy-start.5 = (s32[1,1,8,2]{2,3,1,0:T(2,128)S(1)}, s32[1,1,8,2]{2,3,1,0:T(2,128)}, u32[]{:S(2)}) copy-start(s32[1,1,8,2]{2,3,1,0:T(2,128)} %param.18) | copy-start | bytes 196
  24.2 21.0 %all-to-all-start = ((bf16[32,2,32,128]{3,2,1,0:T(8,128)(2,1)}), bf16[32,2,32,128]{3,2,1,0:T(8,128)(2,1)S(1)}, u32[]{:S(2)}, u32[]{:S(2)}) async-start(bf16[32,2,32,128]{3,2,1,0:T(8,128)(2,1)} %edge_forward.1), calls=%async_computation | async-start | bytes 1048576 | tf_op jit(solution)/shard_map/all_to_all | solution.py:456
  29.8 1.2 %collective-permute-start = (s32[1,8,4]{1,2,0:T(4,128)S(1)}, s32[1,8,4]{1,2,0:T(4,128)S(1)}, u32[]{:S(2)}, u32[]{:S(2)}) collective-permute-start(s32[1,8,4]{1,2,0:T(4,128)S(1)} %add_bitcast_fusion), channel_id=1, source_target_pairs={{0,1},{1,0},{2,3},{3,2},{4,5},{5,4},{6,7},{7,6},{8,9},{9,8},{10,11... | collective-permute-start | bytes 392 | tf_op jit(solution)/shard_map/ppermute | solution.py:26
  31.0 3.6 %collective-permute-start.1 = (s32[2,8,4]{1,2,0:T(4,128)S(1)}, s32[2,8,4]{1,2,0:T(4,128)S(1)}, u32[]{:S(2)}, u32[]{:S(2)}) collective-permute-start(s32[2,8,4]{1,2,0:T(4,128)S(1)} %add_select_fusion.1), channel_id=1, source_target_pairs={{0,2},{1,3},{2,0},{3,1},{4,6},{5,7},{6,4},{7,5},{8,10},{9,11},{10,... | collective-permute-start | bytes 776 | tf_op jit(solution)/shard_map/ppermute | solution.py:26
  47.1 18.6 %all-to-all-start.1 = ((bf16[32,2,32,128]{3,2,1,0:T(8,128)(2,1)}), bf16[32,2,32,128]{3,2,1,0:T(8,128)(2,1)S(1)}, u32[]{:S(2)}, u32[]{:S(2)}) async-start(bf16[32,2,32,128]{3,2,1,0:T(8,128)(2,1)} %get-tuple-element.56), calls=%async_computation.1 | async-start | bytes 1048576 | tf_op jit(solution)/shard_map/all_to_all | solution.py:479
  50.2 2.0 %collective-permute-start.12 = (f32[64,128]{1,0:T(8,128)S(1)}, f32[64,128]{1,0:T(8,128)S(1)}, u32[]{:S(2)}, u32[]{:S(2)}) collective-permute-start(f32[64,128]{1,0:T(8,128)S(1)} %slice_select_fusion.1), channel_id=1, source_target_pairs={{0,1},{1,0},{2,3},{3,2},{4,5},{5,4},{6,7},{7,6},{8,9},{9,8},{10,11... | collective-permute-start | bytes 98312 | tf_op jit(solution)/shard_map/ppermute | solution.py:126
  50.6 11.1 %collective-permute-start.10 = (bf16[16,32,128]{2,1,0:T(8,128)(2,1)}, bf16[16,32,128]{2,1,0:T(8,128)(2,1)S(1)}, u32[]{:S(2)}, u32[]{:S(2)}) collective-permute-start(bf16[16,32,128]{2,1,0:T(8,128)(2,1)} %get-tuple-element.68.refs_0_), channel_id=1, source_target_pairs={{0,2},{1,3},{2,0},{3,1},{4,6},{5,7},{6,4},{7,5},{8,10},{9,11},{10,... | collective-permute-start | bytes 393224 | tf_op jit(solution)/shard_map/ppermute | solution.py:26
  52.3 9.4 %collective-permute-start.15 = (f32[64,128]{1,0:T(8,128)S(1)}, f32[64,128]{1,0:T(8,128)S(1)}, u32[]{:S(2)}, u32[]{:S(2)}) collective-permute-start(f32[64,128]{1,0:T(8,128)S(1)} %select_add_fusion.1), channel_id=1, source_target_pairs={{0,6},{1,7},{2,4},{3,5},{4,2},{5,3},{6,0},{7,1},{8,14},{9,15},{10,... | collective-permute-start | bytes 98312 | tf_op jit(solution)/shard_map/ppermute | solution.py:126
  54.2 7.5 %collective-permute-start.14 = (f32[64,128]{1,0:T(8,128)S(1)}, f32[64,128]{1,0:T(8,128)S(1)}, u32[]{:S(2)}, u32[]{:S(2)}) collective-permute-start(f32[64,128]{1,0:T(8,128)S(1)} %select_add_fusion.1), channel_id=1, source_target_pairs={{0,4},{1,5},{2,6},{3,7},{4,0},{5,1},{6,2},{7,3},{8,12},{9,13},{10,... | collective-permute-start | bytes 98312 | tf_op jit(solution)/shard_map/ppermute | solution.py:126
  54.8 7.5 %collective-permute-start.13 = (f32[64,128]{1,0:T(8,128)S(1)}, f32[64,128]{1,0:T(8,128)S(1)}, u32[]{:S(2)}, u32[]{:S(2)}) collective-permute-start(f32[64,128]{1,0:T(8,128)S(1)} %select_add_fusion.1), channel_id=1, source_target_pairs={{0,2},{1,3},{2,0},{3,1},{4,6},{5,7},{6,4},{7,5},{8,10},{9,11},{10,... | collective-permute-start | bytes 98312 | tf_op jit(solution)/shard_map/ppermute | solution.py:126
  55.8 6.4 %collective-permute-start.9 = (bf16[16,32,128]{2,1,0:T(8,128)(2,1)}, bf16[16,32,128]{2,1,0:T(8,128)(2,1)S(1)}, u32[]{:S(2)}, u32[]{:S(2)}) collective-permute-start(bf16[16,32,128]{2,1,0:T(8,128)(2,1)} %get-tuple-element.68.refs_0_), channel_id=1, source_target_pairs={{0,1},{1,0},{2,3},{3,2},{4,5},{5,4},{6,7},{7,6},{8,9},{9,8},{10,11... | collective-permute-start | bytes 393224 | tf_op jit(solution)/shard_map/ppermute | solution.py:26
  61.7 4.1 %copy-start.2 = (bf16[16,32,128]{2,1,0:T(8,128)(2,1)}, bf16[16,32,128]{2,1,0:T(8,128)(2,1)S(1)}, u32[]{:S(2)}) copy-start(bf16[16,32,128]{2,1,0:T(8,128)(2,1)S(1)} %collective-permute-done.10.refs_2_) | copy-start | bytes 393220
  61.7 1.5 %collective-permute-start.11 = (bf16[16,32,128]{2,1,0:T(8,128)(2,1)S(1)}, bf16[16,32,128]{2,1,0:T(8,128)(2,1)}, u32[]{:S(2)}, u32[]{:S(2)}) collective-permute-start(bf16[16,32,128]{2,1,0:T(8,128)(2,1)S(1)} %collective-permute-done.10.refs_2_), channel_id=1, source_target_pairs={{0,1},{1,0},{2,3},{3,2},{4,5},{5,4},{6,7},{7,6},{8,9},{9,8},{10,11... | collective-permute-start | bytes 393224 | tf_op jit(solution)/shard_map/ppermute | solution.py:26
  62.3 0.7 copy-start.3
  65.8 22.1 %copy-start.1 = (bf16[16,32,128]{2,1,0:T(8,128)(2,1)S(1)}, bf16[16,32,128]{2,1,0:T(8,128)(2,1)}, u32[]{:S(2)}) copy-start(bf16[16,32,128]{2,1,0:T(8,128)(2,1)} %get-tuple-element.74.grad_pre) | copy-start | bytes 393220
  68.9 18.9 %all-to-all-start.2 = ((bf16[32,2,32,128]{3,2,1,0:T(8,128)(2,1)}), bf16[32,2,32,128]{3,2,1,0:T(8,128)(2,1)S(1)}, u32[]{:S(2)}, u32[]{:S(2)}) async-start(bf16[32,2,32,128]{3,2,1,0:T(8,128)(2,1)} %get-tuple-element.67), calls=%async_computation.2 | async-start | bytes 1048576 | tf_op jit(solution)/shard_map/all_to_all | solution.py:507
  71.7 1.3 %collective-permute-start.18 = (f32[64,128]{1,0:T(8,128)S(1)}, f32[64,128]{1,0:T(8,128)S(1)}, u32[]{:S(2)}, u32[]{:S(2)}) collective-permute-start(f32[64,128]{1,0:T(8,128)S(1)} %slice_select_fusion), channel_id=1, source_target_pairs={{0,1},{1,0},{2,3},{3,2},{4,5},{5,4},{6,7},{7,6},{8,9},{9,8},{10,11... | collective-permute-start | bytes 98312 | tf_op jit(solution)/shard_map/ppermute | solution.py:126
  73.0 6.9 %collective-permute-start.21 = (f32[64,128]{1,0:T(8,128)S(1)}, f32[64,128]{1,0:T(8,128)S(1)}, u32[]{:S(2)}, u32[]{:S(2)}) collective-permute-start(f32[64,128]{1,0:T(8,128)S(1)} %select_add_fusion), channel_id=1, source_target_pairs={{0,6},{1,7},{2,4},{3,5},{4,2},{5,3},{6,0},{7,1},{8,14},{9,15},{10,... | collective-permute-start | bytes 98312 | tf_op jit(solution)/shard_map/ppermute | solution.py:126
  75.6 4.6 %collective-permute-start.20 = (f32[64,128]{1,0:T(8,128)S(1)}, f32[64,128]{1,0:T(8,128)S(1)}, u32[]{:S(2)}, u32[]{:S(2)}) collective-permute-start(f32[64,128]{1,0:T(8,128)S(1)} %select_add_fusion), channel_id=1, source_target_pairs={{0,4},{1,5},{2,6},{3,7},{4,0},{5,1},{6,2},{7,3},{8,12},{9,13},{10,... | collective-permute-start | bytes 98312 | tf_op jit(solution)/shard_map/ppermute | solution.py:126
  76.2 4.7 %collective-permute-start.19 = (f32[64,128]{1,0:T(8,128)S(1)}, f32[64,128]{1,0:T(8,128)S(1)}, u32[]{:S(2)}, u32[]{:S(2)}) collective-permute-start(f32[64,128]{1,0:T(8,128)S(1)} %select_add_fusion), channel_id=1, source_target_pairs={{0,2},{1,3},{2,0},{3,1},{4,6},{5,7},{6,4},{7,5},{8,10},{9,11},{10,... | collective-permute-start | bytes 98312 | tf_op jit(solution)/shard_map/ppermute | solution.py:126
  80.9 9.8 %collective-permute-start.23 = (bf16[128,128]{1,0:T(8,128)(2,1)S(1)}, bf16[128,128]{1,0:T(8,128)(2,1)S(1)}, u32[]{:S(2)}, u32[]{:S(2)}) collective-permute-start(bf16[128,128]{1,0:T(8,128)(2,1)S(1)} %pad_maximum_fusion), channel_id=1, source_target_pairs={{0,16},{1,17},{2,18},{3,19},{4,20},{5,21},{6,22},{7,23},{8,24},{9,... | collective-permute-start | bytes 98312 | tf_op jit(solution)/shard_map/ppermute | solution.py:126
  82.8 8.0 %collective-permute-start.22 = (bf16[128,128]{1,0:T(8,128)(2,1)S(1)}, bf16[128,128]{1,0:T(8,128)(2,1)S(1)}, u32[]{:S(2)}, u32[]{:S(2)}) collective-permute-start(bf16[128,128]{1,0:T(8,128)(2,1)S(1)} %pad_maximum_fusion), channel_id=1, source_target_pairs={{0,8},{1,9},{2,10},{3,11},{4,12},{5,13},{6,14},{7,15},{8,0},{9,1},... | collective-permute-start | bytes 98312 | tf_op jit(solution)/shard_map/ppermute | solution.py:126
  84.7 6.0 %collective-permute-start.24 = (bf16[128,128]{1,0:T(8,128)(2,1)S(1)}, bf16[128,128]{1,0:T(8,128)(2,1)S(1)}, u32[]{:S(2)}, u32[]{:S(2)}) collective-permute-start(bf16[128,128]{1,0:T(8,128)(2,1)S(1)} %pad_maximum_fusion), channel_id=1, source_target_pairs={{0,24},{1,25},{2,26},{3,27},{4,28},{5,29},{6,30},{7,31},{8,16},{9,... | collective-permute-start | bytes 98312 | tf_op jit(solution)/shard_map/ppermute | solution.py:126
  88.9 5.3 %collective-permute-start.17 = (bf16[16,32,128]{2,1,0:T(8,128)(2,1)S(1)}, bf16[16,32,128]{2,1,0:T(8,128)(2,1)S(1)}, u32[]{:S(2)}, u32[]{:S(2)}) collective-permute-start(bf16[16,32,128]{2,1,0:T(8,128)(2,1)S(1)} %owner_last.1.refs_0_), channel_id=1, source_target_pairs={{0,2},{1,3},{2,0},{3,1},{4,6},{5,7},{6,4},{7,5},{8,10},{9,11},{10,... | collective-permute-start | bytes 393224 | tf_op jit(solution)/shard_map/ppermute | solution.py:26
  90.8 3.9 %collective-permute-start.16 = (bf16[16,32,128]{2,1,0:T(8,128)(2,1)S(1)}, bf16[16,32,128]{2,1,0:T(8,128)(2,1)S(1)}, u32[]{:S(2)}, u32[]{:S(2)}) collective-permute-start(bf16[16,32,128]{2,1,0:T(8,128)(2,1)S(1)} %owner_last.1.refs_0_), channel_id=1, source_target_pairs={{0,1},{1,0},{2,3},{3,2},{4,5},{5,4},{6,7},{7,6},{8,9},{9,8},{10,11... | collective-permute-start | bytes 393224 | tf_op jit(solution)/shard_map/ppermute | solution.py:26
  94.2 1.4 %collective-permute-start.25 = (bf16[16,32,128]{2,1,0:T(8,128)(2,1)S(1)}, bf16[16,32,128]{2,1,0:T(8,128)(2,1)S(1)}, u32[]{:S(2)}, u32[]{:S(2)}) collective-permute-start(bf16[16,32,128]{2,1,0:T(8,128)(2,1)S(1)} %collective-permute-done.17.refs_2_), channel_id=1, source_target_pairs={{0,1},{1,0},{2,3},{3,2},{4,5},{5,4},{6,7},{7,6},{8,9},{9,8},{10,11... | collective-permute-start | bytes 393224 | tf_op jit(solution)/shard_map/ppermute | solution.py:26
  94.2 1.4 %collective-permute-start.26 = (f32[128,128]{1,0:T(8,128)S(1)}, f32[128,128]{1,0:T(8,128)S(1)}, u32[]{:S(2)}, u32[]{:S(2)}) collective-permute-start(f32[128,128]{1,0:T(8,128)S(1)} %add_add_fusion.refs_4_), channel_id=1, source_target_pairs={{0,1},{1,0},{2,3},{3,2},{4,5},{5,4},{6,7},{7,6},{8,9},{9,8},{10,11... | collective-permute-start | bytes 196616 | tf_op jit(solution)/shard_map/ppermute | solution.py:126

commit v5 on v4

--- a/solution.py
+++ b/solution.py
@@ -56,8 +56,7 @@
     far = swap(x, "feat", top) if top else None
     held, other = spread(0, x), None
     if beside is not None:
-        far, beside = lax.optimization_barrier((far, beside))
-        other = swap_all(beside, 1)
+        far, other = lax.optimization_barrier((far, swap_all(beside, 1)))
     if top:
         held.update(spread(top, far))
     return [held[m] for m in sorted(held)], beside, other
@@ -146,33 +145,18 @@
 
 def pick_kernel(masks, ids, rows, w_msg, w_self, *refs):
     n_send, peers = ids.shape
-    *outs, w_msg_out, w_self_out, room, sems, out_sems = refs
+    *outs, w_msg_out, w_self_out, sems = refs
     me = lax.axis_index("edge")
-    slots = [(n, j) for n in range(peers) for j in range(n_send)]
-    ins = [
-        pltpu.make_async_copy(
-            rows.at[ids[j, me ^ masks[n]]], room.at[n * n_send + j], sems.at[n * n_send + j]
-        )
-        for n, j in slots
+    copies = [
+        (rows.at[ids[j, me ^ mask]], out.at[j])
+        for mask, out in zip(masks, outs)
+        for j in range(n_send)
     ]
-    others = [
-        pltpu.make_async_copy(w_msg, w_msg_out, sems.at[len(slots)]),
-        pltpu.make_async_copy(w_self, w_self_out, sems.at[len(slots) + 1]),
-    ]
-    copies = [
-        pltpu.make_async_copy(
-            room.at[n * n_send + j],
-            outs[n].at[j],
-            out_sems.at[n * n_send + j],
-        )
-        for n, j in slots
-    ]
-    for copy in ins + others:
+    copies += [(w_msg, w_msg_out), (w_self, w_self_out)]
+    copies = [pltpu.make_async_copy(a, b, sems.at[n]) for n, (a, b) in enumerate(copies)]
+    for copy in copies:
         copy.start()
-    for one, two in zip(ins, copies):
-        one.wait()
-        two.start()
-    for copy in others + copies:
+    for copy in copies:
         copy.wait()
 
 
@@ -392,7 +376,7 @@
     src = in_hbm(edge_src.reshape(-1))
     dst = in_hbm(edge_dst.reshape(-1))
     count = live.reshape(1)
-    group = math.gcd(16, adj.shape[0])
+    group = math.gcd(64, adj.shape[0])
     me = lax.axis_index("feat").reshape(1).astype(jnp.int32)
     params = pltpu.CompilerParams(vmem_limit_bytes=32 * 2**20)
     stages = stages_of(devices)
@@ -404,7 +388,6 @@
 
     square = pltpu.VMEM((hidden, hidden), BF16)
     sum_part = pltpu.VMEM((hidden, hidden), F32)
-    rows_out = (peers * n_send, block, hidden)
     recv_out = (devices, n_recv, width, hidden)
     send_out_dims = (devices, n_send, width, hidden)
     out_sems = pltpu.SemaphoreType.DMA((peers,))
@@ -412,14 +395,10 @@
     few = (n_send, block, hidden)
     *outgoing, w_msg, w_self = pl.pallas_call(
         functools.partial(pick_kernel, masks),
-        out_shape=[pltpu.HBM(few, BF16)] * peers + [square, square],
+        out_shape=[pltpu.VMEM(few, BF16)] * peers + [square, square],
         in_specs=[SMEM] + [HBM] * 3,
-        out_specs=[HBM] * peers + [VMEM, VMEM],
-        scratch_shapes=[
-            pltpu.VMEM(rows_out, BF16),
-            pltpu.SemaphoreType.DMA((peers * n_send + 2,)),
-            pltpu.SemaphoreType.DMA((peers * n_send,)),
-        ],
+        out_specs=[VMEM] * (peers + 2),
+        scratch_shapes=[pltpu.SemaphoreType.DMA((peers * n_send + 2,))],
         compiler_params=params,
         name="pick_rows",
     )(

time: 96.8 us -> 94.9 us (0.980)
  Pallas kernels: 16.9 us -> 15.3 us
  transfers between devices with their start and end apart: 30 -> 30, of which waited for: 18 -> 19; matrix products, arithmetic and copies ran while one was open for 1% -> 1% of each run, Pallas kernels for 6% -> 6%
where the time goes in v5:
time: 94.9 us; the launch traced here: 94.4 us
  starting transfers between devices  42.3 us (45%)
  waiting for transfers between devices  34.1 us (36%)
  Pallas kernels  15.3 us (16%)
  between operations  1.51 us (2%)
  local copies, waits for them, and re-layouts  1.11 us (1%)
    ppermute x15, starting transfers between devices, swap(): return lax.ppermute(x, axis, [(j, j ^ bit) for j in range(size)])  18.8 us
    ppermute x15, waiting for transfers between devices, swap(): return lax.ppermute(x, axis, [(j, j ^ bit) for j in range(size)])  14.9 us
    ppermute x12, starting transfers between devices, swap_all(): return lax.ppermute(x, BOTH, [(j, j ^ mask) for j in range(count)])  12.2 us
    all_to_all x1, waiting for transfers between devices, body(): got = lax.all_to_all(partials, BOTH, 0, 0, tiled=True)  9.44 us
    ppermute x12, waiting for transfers between devices, swap_all(): return lax.ppermute(x, BOTH, [(j, j ^ mask) for j in range(count)])  6.71 us
    all_to_all x1, starting transfers between devices, body(): got = lax.all_to_all(partials, BOTH, 0, 0, tiled=True)  5.12 us
    all_to_all x1, starting transfers between devices, body(): grad_back = lax.all_to_all(grad_partials, BOTH, 0, 0, tiled=True)  3.09 us
    all_to_all x1, starting transfers between devices, body(): grad_in = lax.all_to_all(grad_out, BOTH, 0, 0, tiled=True)  3.08 us
  transfers between devices with their start and end apart: 30, of which 19 were waited for; matrix products, arithmetic and copies ran while one was open for 1% of the time, Pallas kernels for 6%

profile of v5, /device:TPU:0, one launch (start us, length us, event | category | flops | bytes accessed | tf_op | source)
XLA Modules:
  0.0 94.4 jit_solution(7077277452100614182)
XLA Ops:
  0.6 1.9 %pick_rows.1 = (bf16[2,128,128]{2,1,0:T(8,128)(2,1)S(1)}, bf16[2,128,128]{2,1,0:T(8,128)(2,1)S(1)}, bf16[2,128,128]{2,1,0:T(8,128)(2,1)S(1)}, bf16[2,128,128]{2,...) custom-call(s32[2,8]{1,0:T(2,128)} %bitcast.27, ...), custom_call_target="tpu_custom_call" | custom-call | tf_op jit(solution)/shard_map/pick_rows/pallas_call | solution.py:396
  2.6 6.0 %collective-permute-start.2 = (bf16[2,128,128]{2,1,0:T(8,128)(2,1)S(1)}, bf16[2,128,128]{2,1,0:T(8,128)(2,1)S(1)}, u32[]{:S(2)}, u32[]{:S(2)}) collective-permute-start(bf16[2,128,128]{2,1,0:T(8,128)(2,1)S(1)} %get-tuple-element.44), channel_id=1, source_target_pairs={{0,28},{4,24},{8,20},{12,16},{16,12},{20,8},{24,4},{28,0},{1,29},{... | collective-permute-start | bytes 196616 | tf_op jit(solution)/shard_map/ppermute | solution.py:26
  8.8 0.7 collective-permute-start.4
  9.6 2.0 %collective-permute-start.5 = (bf16[2,128,128]{2,1,0:T(8,128)(2,1)S(1)}, bf16[2,128,128]{2,1,0:T(8,128)(2,1)S(1)}, u32[]{:S(2)}, u32[]{:S(2)}) collective-permute-start(bf16[2,128,128]{2,1,0:T(8,128)(2,1)S(1)} %get-tuple-element.47), channel_id=1, source_target_pairs={{0,16},{4,20},{8,24},{12,28},{16,0},{20,4},{24,8},{28,12},{1,17},{... | collective-permute-start | bytes 196616 | tf_op jit(solution)/shard_map/ppermute | solution.py:26
  11.6 2.3 %collective-permute-start.6 = (bf16[2,128,128]{2,1,0:T(8,128)(2,1)S(1)}, bf16[2,128,128]{2,1,0:T(8,128)(2,1)S(1)}, u32[]{:S(2)}, u32[]{:S(2)}) collective-permute-start(bf16[2,128,128]{2,1,0:T(8,128)(2,1)S(1)} %get-tuple-element.48), channel_id=1, source_target_pairs={{0,12},{4,8},{8,4},{12,0},{16,28},{20,24},{24,20},{28,16},{1,13},{... | collective-permute-start | bytes 196616 | tf_op jit(solution)/shard_map/ppermute | solution.py:26
  13.9 0.8 collective-permute-start.7
  14.8 0.5 collective-permute-start.8
  16.0 1.6 %fetch_edges.1.adj = bf16[64,128,128]{2,1,0:T(8,128)(2,1)S(1)} custom-call(bf16[64,128,128]{2,1,0:T(8,128)(2,1)} %bitcast.22), custom_call_target="tpu_custom_call" | custom-call | bytes 4194304 | tf_op jit(solution)/shard_map/fetch_edges/pallas_call | solution.py:188
  17.6 0.5 collective-permute-done.4.refs_2_
  18.1 1.7 %collective-permute-done.5.refs_3_ = bf16[2,128,128]{2,1,0:T(8,128)(2,1)S(1)} collective-permute-done((bf16[2,128,128]{2,1,0:T(8,128)(2,1)S(1)}, bf16[2,128,128]{2,1,0:T(8,128)(2,1)S(1)}, u32[]{:S(2)}, u32[]{:S(2)}) %collective-permute-start.5) | collective-permute-done | bytes 65568 | tf_op jit(solution)/shard_map/ppermute | solution.py:26
  19.8 0.4 collective-permute-done.7.refs_5_
  20.2 2.5 %edge_forward.1 = bf16[32,2,32,128]{3,2,1,0:T(8,128)(2,1)} custom-call(s32[1]{0:T(128)} %bitcast.20.live, s32[64]{0:T(128)} %bitcast.29, s32[64]{0:T(128)} %bitcast.31, bf16[128,128]{1,0:T(8,128)(2,1)S(1)} %get-tuple-element.43.w_msg, bf16[64,128,128]{2,1,0:T(8,128)(2,1)S(1)} %fetch_edges.1.adj, bf16[2,128,128]{2,1,0:T(8,128)(2,1)S(1)} %collective-permute-done.2.refs_0_, ...), custom_call_target="tpu_custom_call" | custom-call | tf_op jit(solution)/shard_map/edge_forward/pallas_call | solution.py:415
  22.7 5.1 %all-to-all-start = ((bf16[32,2,32,128]{3,2,1,0:T(8,128)(2,1)}), bf16[32,2,32,128]{3,2,1,0:T(8,128)(2,1)S(1)}, u32[]{:S(2)}, u32[]{:S(2)}) async-start(bf16[32,2,32,128]{3,2,1,0:T(8,128)(2,1)} %edge_forward.1), calls=%async_computation | async-start | bytes 1048576 | tf_op jit(solution)/shard_map/all_to_all | solution.py:435
  28.1 0.9 collective-permute-done
  29.1 1.8 %collective-permute-start.1 = (s32[2,8,4]{1,2,0:T(4,128)S(1)}, s32[2,8,4]{1,2,0:T(4,128)S(1)}, u32[]{:S(2)}, u32[]{:S(2)}) collective-permute-start(s32[2,8,4]{1,2,0:T(4,128)S(1)} %add_select_fusion.1), channel_id=1, source_target_pairs={{0,2},{1,3},{2,0},{3,1},{4,6},{5,7},{6,4},{7,5},{8,10},{9,11},{10,... | collective-permute-start | bytes 776 | tf_op jit(solution)/shard_map/ppermute | solution.py:26
  30.8 1.8 %collective-permute-done.1 = s32[2,8,4]{1,2,0:T(4,128)S(1)} collective-permute-done((s32[2,8,4]{1,2,0:T(4,128)S(1)}, s32[2,8,4]{1,2,0:T(4,128)S(1)}, u32[]{:S(2)}, u32[]{:S(2)}) %collective-permute-start.1) | collective-permute-done | bytes 288 | tf_op jit(solution)/shard_map/ppermute | solution.py:26
  32.9 1.0 %fetch_rows.1.rows = bf16[2,16,32,128]{3,2,1,0:T(8,128)(2,1)S(1)} custom-call(bf16[16,4,32,128]{3,2,1,0:T(8,128)(2,1)} %bitcast.24, bf16[16,4,32,128]{3,2,1,0:T(8,128)(2,1)} %bitcast.25), custom_call_target="tpu_custom_call" | custom-call | bytes 524288 | tf_op jit(solution)/shard_map/fetch_rows/pallas_call | solution.py:188
  33.9 9.4 %all-to-all-done.got = bf16[32,2,32,128]{3,2,1,0:T(8,128)(2,1)S(1)} async-done(((bf16[32,2,32,128]{3,2,1,0:T(8,128)(2,1)}), bf16[32,2,32,128]{3,2,1,0:T(8,128)(2,1)S(1)}, u32[]{:S(2)}, u32[]{:S(2)}) %all-to-all-start) | async-done | bytes 524320 | tf_op jit(solution)/shard_map/all_to_all | solution.py:435
  43.3 1.9 %owner_dense.1 = (bf16[16,32,128]{2,1,0:T(8,128)(2,1)}, bf16[16,32,128]{2,1,0:T(8,128)(2,1)}, bf16[32,2,32,128]{3,2,1,0:T(8,128)(2,1)}, f32[128,128]{1,0:T(8,128)S(1)}) custom-call(s32[64]{0:T(128)S(1)} %reshape.78.ids, bf16[32,2,32,128]{3,2,1,0:T(8,128)(2,1)S(1)} %all-to-all-done.got, bf16[2,16,32,128]{3,2,1,0:T(8,128)(2,1)S(1)} %fetch_rows.1.rows, ...), custom_call_target="tpu_custom_call" | custom-call | tf_op jit(solution)/shard_map/owner_dense/pallas_call | solution.py:438
  45.2 3.1 %all-to-all-start.1 = ((bf16[32,2,32,128]{3,2,1,0:T(8,128)(2,1)}), bf16[32,2,32,128]{3,2,1,0:T(8,128)(2,1)S(1)}, u32[]{:S(2)}, u32[]{:S(2)}) async-start(bf16[32,2,32,128]{3,2,1,0:T(8,128)(2,1)} %get-tuple-element.56), calls=%async_computation.1 | async-start | bytes 1048576 | tf_op jit(solution)/shard_map/all_to_all | solution.py:458
  48.6 1.7 %collective-permute-start.10 = (bf16[16,32,128]{2,1,0:T(8,128)(2,1)}, bf16[16,32,128]{2,1,0:T(8,128)(2,1)S(1)}, u32[]{:S(2)}, u32[]{:S(2)}) collective-permute-start(bf16[16,32,128]{2,1,0:T(8,128)(2,1)} %get-tuple-element.68.refs_0_), channel_id=1, source_target_pairs={{0,2},{1,3},{2,0},{3,1},{4,6},{5,7},{6,4},{7,5},{8,10},{9,11},{10,... | collective-permute-start | bytes 393224 | tf_op jit(solution)/shard_map/ppermute | solution.py:26
  50.3 1.9 %collective-permute-start.15 = (f32[64,128]{1,0:T(8,128)S(1)}, f32[64,128]{1,0:T(8,128)S(1)}, u32[]{:S(2)}, u32[]{:S(2)}) collective-permute-start(f32[64,128]{1,0:T(8,128)S(1)} %select_add_fusion.1), channel_id=1, source_target_pairs={{0,6},{1,7},{2,4},{3,5},{4,2},{5,3},{6,0},{7,1},{8,14},{9,15},{10,... | collective-permute-start | bytes 98312 | tf_op jit(solution)/shard_map/ppermute | solution.py:125
  52.3 0.6 collective-permute-start.14
  52.8 1.1 %collective-permute-start.13 = (f32[64,128]{1,0:T(8,128)S(1)}, f32[64,128]{1,0:T(8,128)S(1)}, u32[]{:S(2)}, u32[]{:S(2)}) collective-permute-start(f32[64,128]{1,0:T(8,128)S(1)} %select_add_fusion.1), channel_id=1, source_target_pairs={{0,2},{1,3},{2,0},{3,1},{4,6},{5,7},{6,4},{7,5},{8,10},{9,11},{10,... | collective-permute-start | bytes 98312 | tf_op jit(solution)/shard_map/ppermute | solution.py:125
  53.9 5.9 %collective-permute-done.10.refs_2_ = bf16[16,32,128]{2,1,0:T(8,128)(2,1)S(1)} collective-permute-done((bf16[16,32,128]{2,1,0:T(8,128)(2,1)}, bf16[16,32,128]{2,1,0:T(8,128)(2,1)S(1)}, u32[]{:S(2)}, u32[]{:S(2)}) %collective-permute-start.10) | collective-permute-done | bytes 131104 | tf_op jit(solution)/shard_map/ppermute | solution.py:26
  59.8 0.6 collective-permute-done.13
  60.4 0.7 copy-done.2
  61.2 2.6 %all-to-all-done.1.got = bf16[32,2,32,128]{3,2,1,0:T(8,128)(2,1)S(1)} async-done(((bf16[32,2,32,128]{3,2,1,0:T(8,128)(2,1)}), bf16[32,2,32,128]{3,2,1,0:T(8,128)(2,1)S(1)}, u32[]{:S(2)}, u32[]{:S(2)}) %all-to-all-start.1) | async-done | bytes 524320 | tf_op jit(solution)/shard_map/all_to_all | solution.py:458
  63.9 2.7 %edge_backward.1 = (bf16[32,2,32,128]{3,2,1,0:T(8,128)(2,1)}, f32[128,128]{1,0:T(8,128)S(1)}) custom-call(s32[1]{0:T(128)} %bitcast.21.live, s32[64]{0:T(128)} %bitcast.30, s32[64]{0:T(128)} %bitcast.32, bf16[32,2,32,128]{3,2,1,0:T(8,128)(2,1)S(1)} %all-to-all-done.1.got, bf16[64,128,128]{2,1,0:T(8,128)(2,1)S(1)} %fetch_edges.1.adj, ...), custom_call_target="tpu_custom_call" | custom-call | tf_op jit(solution)/shard_map/edge_backward/pallas_call | solution.py:467
  66.6 3.1 %all-to-all-start.2 = ((bf16[32,2,32,128]{3,2,1,0:T(8,128)(2,1)}), bf16[32,2,32,128]{3,2,1,0:T(8,128)(2,1)S(1)}, u32[]{:S(2)}, u32[]{:S(2)}) async-start(bf16[32,2,32,128]{3,2,1,0:T(8,128)(2,1)} %get-tuple-element.67), calls=%async_computation.2 | async-start | bytes 1048576 | tf_op jit(solution)/shard_map/all_to_all | solution.py:486
  70.0 1.0 %collective-permute-done.18 = f32[64,128]{1,0:T(8,128)S(1)} collective-permute-done((f32[64,128]{1,0:T(8,128)S(1)}, f32[64,128]{1,0:T(8,128)S(1)}, u32[]{:S(2)}, u32[]{:S(2)}) %collective-permute-start.18) | collective-permute-done | bytes 32800 | tf_op jit(solution)/shard_map/ppermute | solution.py:125
  71.0 2.7 %collective-permute-start.21 = (f32[64,128]{1,0:T(8,128)S(1)}, f32[64,128]{1,0:T(8,128)S(1)}, u32[]{:S(2)}, u32[]{:S(2)}) collective-permute-start(f32[64,128]{1,0:T(8,128)S(1)} %select_add_fusion), channel_id=1, source_target_pairs={{0,6},{1,7},{2,4},{3,5},{4,2},{5,3},{6,0},{7,1},{8,14},{9,15},{10,... | collective-permute-start | bytes 98312 | tf_op jit(solution)/shard_map/ppermute | solution.py:125
  73.6 0.6 collective-permute-start.20
  74.5 3.4 %collective-permute-done.21 = f32[64,128]{1,0:T(8,128)S(1)} collective-permute-done((f32[64,128]{1,0:T(8,128)S(1)}, f32[64,128]{1,0:T(8,128)S(1)}, u32[]{:S(2)}, u32[]{:S(2)}) %collective-permute-start.21) | collective-permute-done | bytes 32800 | tf_op jit(solution)/shard_map/ppermute | solution.py:125
  77.8 0.4 collective-permute-done.20
  78.2 0.7 collective-permute-done.19
  78.9 1.8 %collective-permute-start.23 = (bf16[128,128]{1,0:T(8,128)(2,1)S(1)}, bf16[128,128]{1,0:T(8,128)(2,1)S(1)}, u32[]{:S(2)}, u32[]{:S(2)}) collective-permute-start(bf16[128,128]{1,0:T(8,128)(2,1)S(1)} %pad_maximum_fusion), channel_id=1, source_target_pairs={{0,16},{1,17},{2,18},{3,19},{4,20},{5,21},{6,22},{7,23},{8,24},{9,... | collective-permute-start | bytes 98312 | tf_op jit(solution)/shard_map/ppermute | solution.py:125
  80.8 2.0 %collective-permute-start.22 = (bf16[128,128]{1,0:T(8,128)(2,1)S(1)}, bf16[128,128]{1,0:T(8,128)(2,1)S(1)}, u32[]{:S(2)}, u32[]{:S(2)}) collective-permute-start(bf16[128,128]{1,0:T(8,128)(2,1)S(1)} %pad_maximum_fusion), channel_id=1, source_target_pairs={{0,8},{1,9},{2,10},{3,11},{4,12},{5,13},{6,14},{7,15},{8,0},{9,1},... | collective-permute-start | bytes 98312 | tf_op jit(solution)/shard_map/ppermute | solution.py:125
  82.7 0.7 collective-permute-start.24
  83.6 1.8 %join_rows.2 = bf16[16,4,32,128]{3,2,1,0:T(8,128)(2,1)} custom-call(bf16[16,32,128]{2,1,0:T(8,128)(2,1)} %get-tuple-element.68.refs_0_, bf16[16,32,128]{2,1,0:T(8,128)(2,1)} %copy-done.2, bf16[16,32,128]{2,1,0:T(8,128)(2,1)} %copy-done.1, bf16[16,32,128]{2,1,0:T(8,128)(2,1)} %collective-permute-done.11.refs_3_), custom_call_target="tpu_custom_call" | custom-call | tf_op jit(solution)/shard_map/join_rows/pallas_call | solution.py:106
  85.4 0.4 all-to-all-done.2.got
  85.9 1.0 %owner_last.1.refs_0_ = bf16[16,32,128]{2,1,0:T(8,128)(2,1)S(1)} custom-call(s32[64]{0:T(128)S(1)} %reshape.85.ids, bf16[32,2,32,128]{3,2,1,0:T(8,128)(2,1)S(1)} %all-to-all-done.2.got, bf16[16,32,128]{2,1,0:T(8,128)(2,1)S(1)} %copy-done, bf16[128,128]{1,0:T(8,128)(2,1)S(1)} %get-tuple-element.55.w_self, bf16[128,128]{1,0:T(8,128)(2,1)S(1)} %get-tuple-element.43.w_msg), custom_call_target="tpu_custom_call" | custom-call | tf_op jit(solution)/shard_map/owner_last/pallas_call | solution.py:496
  86.9 1.9 %collective-permute-start.17 = (bf16[16,32,128]{2,1,0:T(8,128)(2,1)S(1)}, bf16[16,32,128]{2,1,0:T(8,128)(2,1)S(1)}, u32[]{:S(2)}, u32[]{:S(2)}) collective-permute-start(bf16[16,32,128]{2,1,0:T(8,128)(2,1)S(1)} %owner_last.1.refs_0_), channel_id=1, source_target_pairs={{0,2},{1,3},{2,0},{3,1},{4,6},{5,7},{6,4},{7,5},{8,10},{9,11},{10,... | collective-permute-start | bytes 393224 | tf_op jit(solution)/shard_map/ppermute | solution.py:26
  88.9 0.5 collective-permute-start.16
  89.4 0.7 collective-permute-done.25.refs_5_
  90.1 2.1 %collective-permute-done.17.refs_2_ = bf16[16,32,128]{2,1,0:T(8,128)(2,1)S(1)} collective-permute-done((bf16[16,32,128]{2,1,0:T(8,128)(2,1)S(1)}, bf16[16,32,128]{2,1,0:T(8,128)(2,1)S(1)}, u32[]{:S(2)}, u32[]{:S(2)}) %collective-permute-start.17) | collective-permute-done | bytes 131104 | tf_op jit(solution)/shard_map/ppermute | solution.py:26
  92.2 1.3 %collective-permute-done.26.refs_3_ = bf16[16,32,128]{2,1,0:T(8,128)(2,1)S(1)} collective-permute-done((bf16[16,32,128]{2,1,0:T(8,128)(2,1)S(1)}, bf16[16,32,128]{2,1,0:T(8,128)(2,1)S(1)}, u32[]{:S(2)}, u32[]{:S(2)}) %collective-permute-start.26) | collective-permute-done | bytes 131104 | tf_op jit(solution)/shard_map/ppermute | solution.py:26
  93.5 0.9 join_rows.3
  (47 shorter events, 2.5 us)
Async XLA Ops:
  2.6 11.3 %collective-permute-start.2 = (bf16[2,128,128]{2,1,0:T(8,128)(2,1)S(1)}, bf16[2,128,128]{2,1,0:T(8,128)(2,1)S(1)}, u32[]{:S(2)}, u32[]{:S(2)}) collective-permute-start(bf16[2,128,128]{2,1,0:T(8,128)(2,1)S(1)} %get-tuple-element.44), channel_id=1, source_target_pairs={{0,28},{4,24},{8,20},{12,16},{16,12},{20,8},{24,4},{28,0},{1,29},{... | collective-permute-start | bytes 196616 | tf_op jit(solution)/shard_map/ppermute | solution.py:26
  8.6 6.2 %collective-permute-start.3 = (bf16[2,128,128]{2,1,0:T(8,128)(2,1)S(1)}, bf16[2,128,128]{2,1,0:T(8,128)(2,1)S(1)}, u32[]{:S(2)}, u32[]{:S(2)}) collective-permute-start(bf16[2,128,128]{2,1,0:T(8,128)(2,1)S(1)} %get-tuple-element.45), channel_id=1, source_target_pairs={{0,24},{4,28},{8,16},{12,20},{16,8},{20,12},{24,0},{28,4},{1,25},{... | collective-permute-start | bytes 196616 | tf_op jit(solution)/shard_map/ppermute | solution.py:26
  8.8 9.3 %collective-permute-start.4 = (bf16[2,128,128]{2,1,0:T(8,128)(2,1)S(1)}, bf16[2,128,128]{2,1,0:T(8,128)(2,1)S(1)}, u32[]{:S(2)}, u32[]{:S(2)}) collective-permute-start(bf16[2,128,128]{2,1,0:T(8,128)(2,1)S(1)} %get-tuple-element.46), channel_id=1, source_target_pairs={{0,20},{4,16},{8,28},{12,24},{16,4},{20,0},{24,12},{28,8},{1,21},{... | collective-permute-start | bytes 196616 | tf_op jit(solution)/shard_map/ppermute | solution.py:26
  9.6 10.2 %collective-permute-start.5 = (bf16[2,128,128]{2,1,0:T(8,128)(2,1)S(1)}, bf16[2,128,128]{2,1,0:T(8,128)(2,1)S(1)}, u32[]{:S(2)}, u32[]{:S(2)}) collective-permute-start(bf16[2,128,128]{2,1,0:T(8,128)(2,1)S(1)} %get-tuple-element.47), channel_id=1, source_target_pairs={{0,16},{4,20},{8,24},{12,28},{16,0},{20,4},{24,8},{28,12},{1,17},{... | collective-permute-start | bytes 196616 | tf_op jit(solution)/shard_map/ppermute | solution.py:26
  11.6 8.2 %collective-permute-start.6 = (bf16[2,128,128]{2,1,0:T(8,128)(2,1)S(1)}, bf16[2,128,128]{2,1,0:T(8,128)(2,1)S(1)}, u32[]{:S(2)}, u32[]{:S(2)}) collective-permute-start(bf16[2,128,128]{2,1,0:T(8,128)(2,1)S(1)} %get-tuple-element.48), channel_id=1, source_target_pairs={{0,12},{4,8},{8,4},{12,0},{16,28},{20,24},{24,20},{28,16},{1,13},{... | collective-permute-start | bytes 196616 | tf_op jit(solution)/shard_map/ppermute | solution.py:26
  13.9 6.3 %collective-permute-start.7 = (bf16[2,128,128]{2,1,0:T(8,128)(2,1)S(1)}, bf16[2,128,128]{2,1,0:T(8,128)(2,1)S(1)}, u32[]{:S(2)}, u32[]{:S(2)}) collective-permute-start(bf16[2,128,128]{2,1,0:T(8,128)(2,1)S(1)} %get-tuple-element.49), channel_id=1, source_target_pairs={{0,8},{4,12},{8,0},{12,4},{16,24},{20,28},{24,16},{28,20},{1,9},{5... | collective-permute-start | bytes 196616 | tf_op jit(solution)/shard_map/ppermute | solution.py:26
  14.8 5.4 %collective-permute-start.8 = (bf16[2,128,128]{2,1,0:T(8,128)(2,1)S(1)}, bf16[2,128,128]{2,1,0:T(8,128)(2,1)S(1)}, u32[]{:S(2)}, u32[]{:S(2)}) collective-permute-start(bf16[2,128,128]{2,1,0:T(8,128)(2,1)S(1)} %get-tuple-element.50), channel_id=1, source_target_pairs={{0,4},{4,0},{8,12},{12,8},{16,20},{20,16},{24,28},{28,24},{1,5},{5... | collective-permute-start | bytes 196616 | tf_op jit(solution)/shard_map/ppermute | solution.py:26
  20.2 7.6 %copy-start.3 = (s32[1,1,8,2]{2,3,1,0:T(2,128)S(1)}, s32[1,1,8,2]{2,3,1,0:T(2,128)}, u32[]{:S(2)}) copy-start(s32[1,1,8,2]{2,3,1,0:T(2,128)} %param.17) | copy-start | bytes 196
  20.2 7.6 %copy-start.4 = (s32[1,1,8,2]{2,3,1,0:T(2,128)S(1)}, s32[1,1,8,2]{2,3,1,0:T(2,128)}, u32[]{:S(2)}) copy-start(s32[1,1,8,2]{2,3,1,0:T(2,128)} %param.18) | copy-start | bytes 196
  22.7 20.7 %all-to-all-start = ((bf16[32,2,32,128]{3,2,1,0:T(8,128)(2,1)}), bf16[32,2,32,128]{3,2,1,0:T(8,128)(2,1)S(1)}, u32[]{:S(2)}, u32[]{:S(2)}) async-start(bf16[32,2,32,128]{3,2,1,0:T(8,128)(2,1)} %edge_forward.1), calls=%async_computation | async-start | bytes 1048576 | tf_op jit(solution)/shard_map/all_to_all | solution.py:435
  27.8 1.2 %collective-permute-start = (s32[1,8,4]{1,2,0:T(4,128)S(1)}, s32[1,8,4]{1,2,0:T(4,128)S(1)}, u32[]{:S(2)}, u32[]{:S(2)}) collective-permute-start(s32[1,8,4]{1,2,0:T(4,128)S(1)} %add_bitcast_fusion), channel_id=1, source_target_pairs={{0,1},{1,0},{2,3},{3,2},{4,5},{5,4},{6,7},{7,6},{8,9},{9,8},{10,11... | collective-permute-start | bytes 392 | tf_op jit(solution)/shard_map/ppermute | solution.py:26
  29.1 3.6 %collective-permute-start.1 = (s32[2,8,4]{1,2,0:T(4,128)S(1)}, s32[2,8,4]{1,2,0:T(4,128)S(1)}, u32[]{:S(2)}, u32[]{:S(2)}) collective-permute-start(s32[2,8,4]{1,2,0:T(4,128)S(1)} %add_select_fusion.1), channel_id=1, source_target_pairs={{0,2},{1,3},{2,0},{3,1},{4,6},{5,7},{6,4},{7,5},{8,10},{9,11},{10,... | collective-permute-start | bytes 776 | tf_op jit(solution)/shard_map/ppermute | solution.py:26
  45.2 18.6 %all-to-all-start.1 = ((bf16[32,2,32,128]{3,2,1,0:T(8,128)(2,1)}), bf16[32,2,32,128]{3,2,1,0:T(8,128)(2,1)S(1)}, u32[]{:S(2)}, u32[]{:S(2)}) async-start(bf16[32,2,32,128]{3,2,1,0:T(8,128)(2,1)} %get-tuple-element.56), calls=%async_computation.1 | async-start | bytes 1048576 | tf_op jit(solution)/shard_map/all_to_all | solution.py:458
  48.3 2.0 %collective-permute-start.12 = (f32[64,128]{1,0:T(8,128)S(1)}, f32[64,128]{1,0:T(8,128)S(1)}, u32[]{:S(2)}, u32[]{:S(2)}) collective-permute-start(f32[64,128]{1,0:T(8,128)S(1)} %slice_select_fusion.1), channel_id=1, source_target_pairs={{0,1},{1,0},{2,3},{3,2},{4,5},{5,4},{6,7},{7,6},{8,9},{9,8},{10,11... | collective-permute-start | bytes 98312 | tf_op jit(solution)/shard_map/ppermute | solution.py:125
  48.6 11.1 %collective-permute-start.10 = (bf16[16,32,128]{2,1,0:T(8,128)(2,1)}, bf16[16,32,128]{2,1,0:T(8,128)(2,1)S(1)}, u32[]{:S(2)}, u32[]{:S(2)}) collective-permute-start(bf16[16,32,128]{2,1,0:T(8,128)(2,1)} %get-tuple-element.68.refs_0_), channel_id=1, source_target_pairs={{0,2},{1,3},{2,0},{3,1},{4,6},{5,7},{6,4},{7,5},{8,10},{9,11},{10,... | collective-permute-start | bytes 393224 | tf_op jit(solution)/shard_map/ppermute | solution.py:26
  50.3 9.4 %collective-permute-start.15 = (f32[64,128]{1,0:T(8,128)S(1)}, f32[64,128]{1,0:T(8,128)S(1)}, u32[]{:S(2)}, u32[]{:S(2)}) collective-permute-start(f32[64,128]{1,0:T(8,128)S(1)} %select_add_fusion.1), channel_id=1, source_target_pairs={{0,6},{1,7},{2,4},{3,5},{4,2},{5,3},{6,0},{7,1},{8,14},{9,15},{10,... | collective-permute-start | bytes 98312 | tf_op jit(solution)/shard_map/ppermute | solution.py:125
  52.3 7.5 %collective-permute-start.14 = (f32[64,128]{1,0:T(8,128)S(1)}, f32[64,128]{1,0:T(8,128)S(1)}, u32[]{:S(2)}, u32[]{:S(2)}) collective-permute-start(f32[64,128]{1,0:T(8,128)S(1)} %select_add_fusion.1), channel_id=1, source_target_pairs={{0,4},{1,5},{2,6},{3,7},{4,0},{5,1},{6,2},{7,3},{8,12},{9,13},{10,... | collective-permute-start | bytes 98312 | tf_op jit(solution)/shard_map/ppermute | solution.py:125
  52.8 7.5 %collective-permute-start.13 = (f32[64,128]{1,0:T(8,128)S(1)}, f32[64,128]{1,0:T(8,128)S(1)}, u32[]{:S(2)}, u32[]{:S(2)}) collective-permute-start(f32[64,128]{1,0:T(8,128)S(1)} %select_add_fusion.1), channel_id=1, source_target_pairs={{0,2},{1,3},{2,0},{3,1},{4,6},{5,7},{6,4},{7,5},{8,10},{9,11},{10,... | collective-permute-start | bytes 98312 | tf_op jit(solution)/shard_map/ppermute | solution.py:125
  53.9 6.4 %collective-permute-start.9 = (bf16[16,32,128]{2,1,0:T(8,128)(2,1)}, bf16[16,32,128]{2,1,0:T(8,128)(2,1)S(1)}, u32[]{:S(2)}, u32[]{:S(2)}) collective-permute-start(bf16[16,32,128]{2,1,0:T(8,128)(2,1)} %get-tuple-element.68.refs_0_), channel_id=1, source_target_pairs={{0,1},{1,0},{2,3},{3,2},{4,5},{5,4},{6,7},{7,6},{8,9},{9,8},{10,11... | collective-permute-start | bytes 393224 | tf_op jit(solution)/shard_map/ppermute | solution.py:26
  59.7 4.1 %copy-start.1 = (bf16[16,32,128]{2,1,0:T(8,128)(2,1)}, bf16[16,32,128]{2,1,0:T(8,128)(2,1)S(1)}, u32[]{:S(2)}) copy-start(bf16[16,32,128]{2,1,0:T(8,128)(2,1)S(1)} %collective-permute-done.10.refs_2_) | copy-start | bytes 393220
  59.7 1.5 %collective-permute-start.11 = (bf16[16,32,128]{2,1,0:T(8,128)(2,1)S(1)}, bf16[16,32,128]{2,1,0:T(8,128)(2,1)}, u32[]{:S(2)}, u32[]{:S(2)}) collective-permute-start(bf16[16,32,128]{2,1,0:T(8,128)(2,1)S(1)} %collective-permute-done.10.refs_2_), channel_id=1, source_target_pairs={{0,1},{1,0},{2,3},{3,2},{4,5},{5,4},{6,7},{7,6},{8,9},{9,8},{10,11... | collective-permute-start | bytes 393224 | tf_op jit(solution)/shard_map/ppermute | solution.py:26
  60.3 0.7 copy-start.2
  63.9 22.0 %copy-start = (bf16[16,32,128]{2,1,0:T(8,128)(2,1)S(1)}, bf16[16,32,128]{2,1,0:T(8,128)(2,1)}, u32[]{:S(2)}) copy-start(bf16[16,32,128]{2,1,0:T(8,128)(2,1)} %get-tuple-element.74.grad_pre) | copy-start | bytes 393220
  66.6 19.3 %all-to-all-start.2 = ((bf16[32,2,32,128]{3,2,1,0:T(8,128)(2,1)}), bf16[32,2,32,128]{3,2,1,0:T(8,128)(2,1)S(1)}, u32[]{:S(2)}, u32[]{:S(2)}) async-start(bf16[32,2,32,128]{3,2,1,0:T(8,128)(2,1)} %get-tuple-element.67), calls=%async_computation.2 | async-start | bytes 1048576 | tf_op jit(solution)/shard_map/all_to_all | solution.py:486
  69.7 1.3 %collective-permute-start.18 = (f32[64,128]{1,0:T(8,128)S(1)}, f32[64,128]{1,0:T(8,128)S(1)}, u32[]{:S(2)}, u32[]{:S(2)}) collective-permute-start(f32[64,128]{1,0:T(8,128)S(1)} %slice_select_fusion), channel_id=1, source_target_pairs={{0,1},{1,0},{2,3},{3,2},{4,5},{5,4},{6,7},{7,6},{8,9},{9,8},{10,11... | collective-permute-start | bytes 98312 | tf_op jit(solution)/shard_map/ppermute | solution.py:125
  71.0 6.9 %collective-permute-start.21 = (f32[64,128]{1,0:T(8,128)S(1)}, f32[64,128]{1,0:T(8,128)S(1)}, u32[]{:S(2)}, u32[]{:S(2)}) collective-permute-start(f32[64,128]{1,0:T(8,128)S(1)} %select_add_fusion), channel_id=1, source_target_pairs={{0,6},{1,7},{2,4},{3,5},{4,2},{5,3},{6,0},{7,1},{8,14},{9,15},{10,... | collective-permute-start | bytes 98312 | tf_op jit(solution)/shard_map/ppermute | solution.py:125
  73.6 4.6 %collective-permute-start.20 = (f32[64,128]{1,0:T(8,128)S(1)}, f32[64,128]{1,0:T(8,128)S(1)}, u32[]{:S(2)}, u32[]{:S(2)}) collective-permute-start(f32[64,128]{1,0:T(8,128)S(1)} %select_add_fusion), channel_id=1, source_target_pairs={{0,4},{1,5},{2,6},{3,7},{4,0},{5,1},{6,2},{7,3},{8,12},{9,13},{10,... | collective-permute-start | bytes 98312 | tf_op jit(solution)/shard_map/ppermute | solution.py:125
  74.2 4.7 %collective-permute-start.19 = (f32[64,128]{1,0:T(8,128)S(1)}, f32[64,128]{1,0:T(8,128)S(1)}, u32[]{:S(2)}, u32[]{:S(2)}) collective-permute-start(f32[64,128]{1,0:T(8,128)S(1)} %select_add_fusion), channel_id=1, source_target_pairs={{0,2},{1,3},{2,0},{3,1},{4,6},{5,7},{6,4},{7,5},{8,10},{9,11},{10,... | collective-permute-start | bytes 98312 | tf_op jit(solution)/shard_map/ppermute | solution.py:125
  78.9 9.8 %collective-permute-start.23 = (bf16[128,128]{1,0:T(8,128)(2,1)S(1)}, bf16[128,128]{1,0:T(8,128)(2,1)S(1)}, u32[]{:S(2)}, u32[]{:S(2)}) collective-permute-start(bf16[128,128]{1,0:T(8,128)(2,1)S(1)} %pad_maximum_fusion), channel_id=1, source_target_pairs={{0,16},{1,17},{2,18},{3,19},{4,20},{5,21},{6,22},{7,23},{8,24},{9,... | collective-permute-start | bytes 98312 | tf_op jit(solution)/shard_map/ppermute | solution.py:125
  80.8 8.0 %collective-permute-start.22 = (bf16[128,128]{1,0:T(8,128)(2,1)S(1)}, bf16[128,128]{1,0:T(8,128)(2,1)S(1)}, u32[]{:S(2)}, u32[]{:S(2)}) collective-permute-start(bf16[128,128]{1,0:T(8,128)(2,1)S(1)} %pad_maximum_fusion), channel_id=1, source_target_pairs={{0,8},{1,9},{2,10},{3,11},{4,12},{5,13},{6,14},{7,15},{8,0},{9,1},... | collective-permute-start | bytes 98312 | tf_op jit(solution)/shard_map/ppermute | solution.py:125
  82.7 6.0 %collective-permute-start.24 = (bf16[128,128]{1,0:T(8,128)(2,1)S(1)}, bf16[128,128]{1,0:T(8,128)(2,1)S(1)}, u32[]{:S(2)}, u32[]{:S(2)}) collective-permute-start(bf16[128,128]{1,0:T(8,128)(2,1)S(1)} %pad_maximum_fusion), channel_id=1, source_target_pairs={{0,24},{1,25},{2,26},{3,27},{4,28},{5,29},{6,30},{7,31},{8,16},{9,... | collective-permute-start | bytes 98312 | tf_op jit(solution)/shard_map/ppermute | solution.py:125
  86.9 5.3 %collective-permute-start.17 = (bf16[16,32,128]{2,1,0:T(8,128)(2,1)S(1)}, bf16[16,32,128]{2,1,0:T(8,128)(2,1)S(1)}, u32[]{:S(2)}, u32[]{:S(2)}) collective-permute-start(bf16[16,32,128]{2,1,0:T(8,128)(2,1)S(1)} %owner_last.1.refs_0_), channel_id=1, source_target_pairs={{0,2},{1,3},{2,0},{3,1},{4,6},{5,7},{6,4},{7,5},{8,10},{9,11},{10,... | collective-permute-start | bytes 393224 | tf_op jit(solution)/shard_map/ppermute | solution.py:26
  88.8 1.3 %collective-permute-start.25 = (f32[128,128]{1,0:T(8,128)S(1)}, f32[128,128]{1,0:T(8,128)S(1)}, u32[]{:S(2)}, u32[]{:S(2)}) collective-permute-start(f32[128,128]{1,0:T(8,128)S(1)} %add_add_fusion.refs_4_), channel_id=1, source_target_pairs={{0,1},{1,0},{2,3},{3,2},{4,5},{5,4},{6,7},{7,6},{8,9},{9,8},{10,11... | collective-permute-start | bytes 196616 | tf_op jit(solution)/shard_map/ppermute | solution.py:125
  88.9 3.3 %collective-permute-start.16 = (bf16[16,32,128]{2,1,0:T(8,128)(2,1)S(1)}, bf16[16,32,128]{2,1,0:T(8,128)(2,1)S(1)}, u32[]{:S(2)}, u32[]{:S(2)}) collective-permute-start(bf16[16,32,128]{2,1,0:T(8,128)(2,1)S(1)} %owner_last.1.refs_0_), channel_id=1, source_target_pairs={{0,1},{1,0},{2,3},{3,2},{4,5},{5,4},{6,7},{7,6},{8,9},{9,8},{10,11... | collective-permute-start | bytes 393224 | tf_op jit(solution)/shard_map/ppermute | solution.py:26
  92.2 1.3 %collective-permute-start.26 = (bf16[16,32,128]{2,1,0:T(8,128)(2,1)S(1)}, bf16[16,32,128]{2,1,0:T(8,128)(2,1)S(1)}, u32[]{:S(2)}, u32[]{:S(2)}) collective-permute-start(bf16[16,32,128]{2,1,0:T(8,128)(2,1)S(1)} %collective-permute-done.17.refs_2_), channel_id=1, source_target_pairs={{0,1},{1,0},{2,3},{3,2},{4,5},{5,4},{6,7},{7,6},{8,9},{9,8},{10,11... | collective-permute-start | bytes 393224 | tf_op jit(solution)/shard_map/ppermute | solution.py:26

commit v6 on v5

--- a/solution.py
+++ b/solution.py
@@ -43,7 +43,7 @@
     return held
 
 
-def pieces_feat(x, beside=None):
+def pieces_feat(x, beside=None, along=None):
     top = lax.axis_size("feat") // 2
     low = [1 << n for n in range(top.bit_length() - 1)][::-1]
 
@@ -56,10 +56,10 @@
     far = swap(x, "feat", top) if top else None
     held, other = spread(0, x), None
     if beside is not None:
-        far, other = lax.optimization_barrier((far, swap_all(beside, 1)))
+        far, other, along = lax.optimization_barrier((far, swap_all(beside, 1), along))
     if top:
         held.update(spread(top, far))
-    return [held[m] for m in sorted(held)], beside, other
+    return [held[m] for m in sorted(held)], beside, other, along
 
 
 def join_kernel(planes, bounce, *refs):
@@ -456,7 +456,7 @@
         name="owner_dense",
     )(recv_all, got, rows, w_self)
     grad_in = lax.all_to_all(grad_out, BOTH, 0, 0, tiled=True)
-    out_pieces, _, _ = pieces_feat(out_part)
+    out_pieces = pieces_feat(out_part)[0]
     wself_part = split_core(wself_part, me)
     for bits in stages[1:2]:
         wself_part = sum_stage(wself_part, bits)
@@ -482,16 +482,16 @@
     grad_partials, wmsg_part, wself_part, out_pieces = lax.optimization_barrier(
         (grad_partials, wmsg_part, wself_part, out_pieces)
     )
-    (out_feat,) = join_feat(out_pieces, [], params)
     grad_back = lax.all_to_all(grad_partials, BOTH, 0, 0, tiled=True)
     wmsg_part = split_core(wmsg_part, me)
     for bits in stages[1:2]:
         wmsg_part = sum_stage(wmsg_part, bits)
     sums = jnp.concatenate([wself_part, wmsg_part], 0)
-    for bits in stages[2:]:
-        sums = sum_stage(sums.astype(BF16), bits)
-
-    grad_back, out_feat = lax.optimization_barrier((grad_back, out_feat))
+    last = [bit for bits in stages[2:] for bit in bits]
+    for bit in last[:-1]:
+        sums = sum_stage(sums, [bit])
+    for bit in last[-1:]:
+        sums = sum_stage(sums.astype(BF16), [bit])
 
     grad_part = pl.pallas_call(
         last_kernel,
@@ -502,7 +502,9 @@
         compiler_params=params,
         name="owner_last",
     )(send_all, grad_back, grad_pre, w_self, w_msg)
-    grad_pieces, sums, other = pieces_feat(grad_part, sums)
+    grad_part, out_pieces = lax.optimization_barrier((grad_part, out_pieces))
+    (out_feat,) = join_feat(out_pieces, [], params)
+    grad_pieces, sums, other, out_feat = pieces_feat(grad_part, sums, out_feat)
     grad_feat, grad_wself, grad_wmsg = join_feat(grad_pieces, [sums, other], params)
     return (out_feat, grad_feat, grad_wmsg, grad_wself)
 

time: 94.9 us -> 94.6 us (level)
  starting transfers between devices: 42.3 us -> 39.6 us
  waiting for transfers between devices: 34.1 us -> 36.3 us
    ppermute x12 -> x11, waiting for transfers between devices: 6.71 us -> 11.7 us  [swap_all(): return lax.ppermute(x, BOTH, [(j, j ^ mask) for j in range(count)])]
    ppermute x12 -> x11, starting transfers between devices: 12.2 us -> 9.72 us  [swap_all(): return lax.ppermute(x, BOTH, [(j, j ^ mask) for j in range(count)])]
    ppermute x15, waiting for transfers between devices: 14.9 us -> 12.5 us  [swap(): return lax.ppermute(x, axis, [(j, j ^ bit) for j in range(size)])]
  transfers between devices with their start and end apart: 30 -> 29, of which waited for: 19 -> 18; matrix products, arithmetic and copies ran while one was open for 1% -> 1% of each run, Pallas kernels for 6% -> 6%
where the time goes in v6:
time: 94.6 us; the launch traced here: 93.9 us
  starting transfers between devices  39.6 us (42%)
  waiting for transfers between devices  36.3 us (38%)
  Pallas kernels  15.3 us (16%)
  between operations  1.53 us (2%)
  local copies, waits for them, and re-layouts  1.1 us (1%)
    ppermute x15, starting transfers between devices, swap(): return lax.ppermute(x, axis, [(j, j ^ bit) for j in range(size)])  18.7 us
    ppermute x15, waiting for transfers between devices, swap(): return lax.ppermute(x, axis, [(j, j ^ bit) for j in range(size)])  12.5 us
    ppermute x11, waiting for transfers between devices, swap_all(): return lax.ppermute(x, BOTH, [(j, j ^ mask) for j in range(count)])  11.7 us
    ppermute x11, starting transfers between devices, swap_all(): return lax.ppermute(x, BOTH, [(j, j ^ mask) for j in range(count)])  9.72 us
    all_to_all x1, waiting for transfers between devices, body(): got = lax.all_to_all(partials, BOTH, 0, 0, tiled=True)  9.44 us
    all_to_all x1, starting transfers between devices, body(): got = lax.all_to_all(partials, BOTH, 0, 0, tiled=True)  5.1 us
    all_to_all x1, starting transfers between devices, body(): grad_back = lax.all_to_all(grad_partials, BOTH, 0, 0, tiled=True)  3.08 us
    all_to_all x1, starting transfers between devices, body(): grad_in = lax.all_to_all(grad_out, BOTH, 0, 0, tiled=True)  3.08 us
  transfers between devices with their start and end apart: 29, of which 18 were waited for; matrix products, arithmetic and copies ran while one was open for 1% of the time, Pallas kernels for 6%

profile of v6, /device:TPU:0, one launch (start us, length us, event | category | flops | bytes accessed | tf_op | source)
XLA Modules:
  0.0 93.9 jit_solution(14680608989121230809)
XLA Ops:
  0.6 1.9 %pick_rows.1 = (bf16[2,128,128]{2,1,0:T(8,128)(2,1)S(1)}, bf16[2,128,128]{2,1,0:T(8,128)(2,1)S(1)}, bf16[2,128,128]{2,1,0:T(8,128)(2,1)S(1)}, bf16[2,128,128]{2,...) custom-call(s32[2,8]{1,0:T(2,128)} %bitcast.27, ...), custom_call_target="tpu_custom_call" | custom-call | tf_op jit(solution)/shard_map/pick_rows/pallas_call | solution.py:396
  2.5 6.1 %collective-permute-start.2 = (bf16[2,128,128]{2,1,0:T(8,128)(2,1)S(1)}, bf16[2,128,128]{2,1,0:T(8,128)(2,1)S(1)}, u32[]{:S(2)}, u32[]{:S(2)}) collective-permute-start(bf16[2,128,128]{2,1,0:T(8,128)(2,1)S(1)} %get-tuple-element.48), channel_id=1, source_target_pairs={{0,28},{4,24},{8,20},{12,16},{16,12},{20,8},{24,4},{28,0},{1,29},{... | collective-permute-start | bytes 196616 | tf_op jit(solution)/shard_map/ppermute | solution.py:26
  8.8 0.8 collective-permute-start.4
  9.6 2.1 %collective-permute-start.5 = (bf16[2,128,128]{2,1,0:T(8,128)(2,1)S(1)}, bf16[2,128,128]{2,1,0:T(8,128)(2,1)S(1)}, u32[]{:S(2)}, u32[]{:S(2)}) collective-permute-start(bf16[2,128,128]{2,1,0:T(8,128)(2,1)S(1)} %get-tuple-element.51), channel_id=1, source_target_pairs={{0,16},{4,20},{8,24},{12,28},{16,0},{20,4},{24,8},{28,12},{1,17},{... | collective-permute-start | bytes 196616 | tf_op jit(solution)/shard_map/ppermute | solution.py:26
  11.6 2.3 %collective-permute-start.6 = (bf16[2,128,128]{2,1,0:T(8,128)(2,1)S(1)}, bf16[2,128,128]{2,1,0:T(8,128)(2,1)S(1)}, u32[]{:S(2)}, u32[]{:S(2)}) collective-permute-start(bf16[2,128,128]{2,1,0:T(8,128)(2,1)S(1)} %get-tuple-element.52), channel_id=1, source_target_pairs={{0,12},{4,8},{8,4},{12,0},{16,28},{20,24},{24,20},{28,16},{1,13},{... | collective-permute-start | bytes 196616 | tf_op jit(solution)/shard_map/ppermute | solution.py:26
  13.9 0.7 collective-permute-start.7
  14.8 0.8 collective-permute-start.8
  16.3 1.6 %fetch_edges.1.adj = bf16[64,128,128]{2,1,0:T(8,128)(2,1)S(1)} custom-call(bf16[64,128,128]{2,1,0:T(8,128)(2,1)} %bitcast.22), custom_call_target="tpu_custom_call" | custom-call | bytes 4194304 | tf_op jit(solution)/shard_map/fetch_edges/pallas_call | solution.py:188
  18.1 1.7 %collective-permute-done.5.refs_3_ = bf16[2,128,128]{2,1,0:T(8,128)(2,1)S(1)} collective-permute-done((bf16[2,128,128]{2,1,0:T(8,128)(2,1)S(1)}, bf16[2,128,128]{2,1,0:T(8,128)(2,1)S(1)}, u32[]{:S(2)}, u32[]{:S(2)}) %collective-permute-start.5) | collective-permute-done | bytes 65568 | tf_op jit(solution)/shard_map/ppermute | solution.py:26
  19.8 0.4 collective-permute-done.7.refs_5_
  20.2 2.5 %edge_forward.1 = bf16[32,2,32,128]{3,2,1,0:T(8,128)(2,1)} custom-call(s32[1]{0:T(128)} %bitcast.20.live, s32[64]{0:T(128)} %bitcast.29, s32[64]{0:T(128)} %bitcast.31, bf16[128,128]{1,0:T(8,128)(2,1)S(1)} %get-tuple-element.47.w_msg, bf16[64,128,128]{2,1,0:T(8,128)(2,1)S(1)} %fetch_edges.1.adj, bf16[2,128,128]{2,1,0:T(8,128)(2,1)S(1)} %collective-permute-done.2.refs_0_, ...), custom_call_target="tpu_custom_call" | custom-call | tf_op jit(solution)/shard_map/edge_forward/pallas_call | solution.py:415
  22.7 5.1 %all-to-all-start = ((bf16[32,2,32,128]{3,2,1,0:T(8,128)(2,1)}), bf16[32,2,32,128]{3,2,1,0:T(8,128)(2,1)S(1)}, u32[]{:S(2)}, u32[]{:S(2)}) async-start(bf16[32,2,32,128]{3,2,1,0:T(8,128)(2,1)} %edge_forward.1), calls=%async_computation | async-start | bytes 1048576 | tf_op jit(solution)/shard_map/all_to_all | solution.py:435
  27.8 0.3 collective-permute-start
  28.1 0.9 collective-permute-done
  29.0 1.8 %collective-permute-start.1 = (s32[2,8,4]{1,2,0:T(4,128)S(1)}, s32[2,8,4]{1,2,0:T(4,128)S(1)}, u32[]{:S(2)}, u32[]{:S(2)}) collective-permute-start(s32[2,8,4]{1,2,0:T(4,128)S(1)} %add_select_fusion.1), channel_id=1, source_target_pairs={{0,2},{1,3},{2,0},{3,1},{4,6},{5,7},{6,4},{7,5},{8,10},{9,11},{10,... | collective-permute-start | bytes 776 | tf_op jit(solution)/shard_map/ppermute | solution.py:26
  30.8 1.8 %collective-permute-done.1 = s32[2,8,4]{1,2,0:T(4,128)S(1)} collective-permute-done((s32[2,8,4]{1,2,0:T(4,128)S(1)}, s32[2,8,4]{1,2,0:T(4,128)S(1)}, u32[]{:S(2)}, u32[]{:S(2)}) %collective-permute-start.1) | collective-permute-done | bytes 288 | tf_op jit(solution)/shard_map/ppermute | solution.py:26
  32.9 1.0 %fetch_rows.1.rows = bf16[2,16,32,128]{3,2,1,0:T(8,128)(2,1)S(1)} custom-call(bf16[16,4,32,128]{3,2,1,0:T(8,128)(2,1)} %bitcast.24, bf16[16,4,32,128]{3,2,1,0:T(8,128)(2,1)} %bitcast.25), custom_call_target="tpu_custom_call" | custom-call | bytes 524288 | tf_op jit(solution)/shard_map/fetch_rows/pallas_call | solution.py:188
  33.9 9.4 %all-to-all-done.got = bf16[32,2,32,128]{3,2,1,0:T(8,128)(2,1)S(1)} async-done(((bf16[32,2,32,128]{3,2,1,0:T(8,128)(2,1)}), bf16[32,2,32,128]{3,2,1,0:T(8,128)(2,1)S(1)}, u32[]{:S(2)}, u32[]{:S(2)}) %all-to-all-start) | async-done | bytes 524320 | tf_op jit(solution)/shard_map/all_to_all | solution.py:435
  43.3 1.9 %owner_dense.1 = (bf16[16,32,128]{2,1,0:T(8,128)(2,1)}, bf16[16,32,128]{2,1,0:T(8,128)(2,1)}, bf16[32,2,32,128]{3,2,1,0:T(8,128)(2,1)}, f32[128,128]{1,0:T(8,128)S(1)}) custom-call(s32[64]{0:T(128)S(1)} %reshape.79.ids, bf16[32,2,32,128]{3,2,1,0:T(8,128)(2,1)S(1)} %all-to-all-done.got, bf16[2,16,32,128]{3,2,1,0:T(8,128)(2,1)S(1)} %fetch_rows.1.rows, ...), custom_call_target="tpu_custom_call" | custom-call | tf_op jit(solution)/shard_map/owner_dense/pallas_call | solution.py:438
  45.2 3.1 %all-to-all-start.1 = ((bf16[32,2,32,128]{3,2,1,0:T(8,128)(2,1)}), bf16[32,2,32,128]{3,2,1,0:T(8,128)(2,1)S(1)}, u32[]{:S(2)}, u32[]{:S(2)}) async-start(bf16[32,2,32,128]{3,2,1,0:T(8,128)(2,1)} %get-tuple-element.60), calls=%async_computation.1 | async-start | bytes 1048576 | tf_op jit(solution)/shard_map/all_to_all | solution.py:458
  48.3 0.3 collective-permute-start.12
  48.6 1.7 %collective-permute-start.10 = (bf16[16,32,128]{2,1,0:T(8,128)(2,1)}, bf16[16,32,128]{2,1,0:T(8,128)(2,1)S(1)}, u32[]{:S(2)}, u32[]{:S(2)}) collective-permute-start(bf16[16,32,128]{2,1,0:T(8,128)(2,1)} %get-tuple-element.80.refs_0_), channel_id=1, source_target_pairs={{0,2},{1,3},{2,0},{3,1},{4,6},{5,7},{6,4},{7,5},{8,10},{9,11},{10,... | collective-permute-start | bytes 393224 | tf_op jit(solution)/shard_map/ppermute | solution.py:26
  50.3 1.9 %collective-permute-start.15 = (f32[64,128]{1,0:T(8,128)S(1)}, f32[64,128]{1,0:T(8,128)S(1)}, u32[]{:S(2)}, u32[]{:S(2)}) collective-permute-start(f32[64,128]{1,0:T(8,128)S(1)} %select_add_fusion.1), channel_id=1, source_target_pairs={{0,6},{1,7},{2,4},{3,5},{4,2},{5,3},{6,0},{7,1},{8,14},{9,15},{10,... | collective-permute-start | bytes 98312 | tf_op jit(solution)/shard_map/ppermute | solution.py:125
  52.2 0.6 collective-permute-start.14
  52.8 1.1 %collective-permute-start.13 = (f32[64,128]{1,0:T(8,128)S(1)}, f32[64,128]{1,0:T(8,128)S(1)}, u32[]{:S(2)}, u32[]{:S(2)}) collective-permute-start(f32[64,128]{1,0:T(8,128)S(1)} %select_add_fusion.1), channel_id=1, source_target_pairs={{0,2},{1,3},{2,0},{3,1},{4,6},{5,7},{6,4},{7,5},{8,10},{9,11},{10,... | collective-permute-start | bytes 98312 | tf_op jit(solution)/shard_map/ppermute | solution.py:125
  53.9 5.9 %collective-permute-done.10.refs_2_ = bf16[16,32,128]{2,1,0:T(8,128)(2,1)S(1)} collective-permute-done((bf16[16,32,128]{2,1,0:T(8,128)(2,1)}, bf16[16,32,128]{2,1,0:T(8,128)(2,1)S(1)}, u32[]{:S(2)}, u32[]{:S(2)}) %collective-permute-start.10) | collective-permute-done | bytes 131104 | tf_op jit(solution)/shard_map/ppermute | solution.py:26
  59.7 0.6 collective-permute-done.13
  60.3 0.6 copy-done.2
  61.2 2.6 %all-to-all-done.1.got = bf16[32,2,32,128]{3,2,1,0:T(8,128)(2,1)S(1)} async-done(((bf16[32,2,32,128]{3,2,1,0:T(8,128)(2,1)}), bf16[32,2,32,128]{3,2,1,0:T(8,128)(2,1)S(1)}, u32[]{:S(2)}, u32[]{:S(2)}) %all-to-all-start.1) | async-done | bytes 524320 | tf_op jit(solution)/shard_map/all_to_all | solution.py:458
  63.8 2.7 %edge_backward.1 = (bf16[32,2,32,128]{3,2,1,0:T(8,128)(2,1)}, f32[128,128]{1,0:T(8,128)S(1)}) custom-call(s32[1]{0:T(128)} %bitcast.21.live, s32[64]{0:T(128)} %bitcast.30, s32[64]{0:T(128)} %bitcast.32, bf16[32,2,32,128]{3,2,1,0:T(8,128)(2,1)S(1)} %all-to-all-done.1.got, bf16[64,128,128]{2,1,0:T(8,128)(2,1)S(1)} %fetch_edges.1.adj, ...), custom_call_target="tpu_custom_call" | custom-call | tf_op jit(solution)/shard_map/edge_backward/pallas_call | solution.py:467
  66.6 3.1 %all-to-all-start.2 = ((bf16[32,2,32,128]{3,2,1,0:T(8,128)(2,1)}), bf16[32,2,32,128]{3,2,1,0:T(8,128)(2,1)S(1)}, u32[]{:S(2)}, u32[]{:S(2)}) async-start(bf16[32,2,32,128]{3,2,1,0:T(8,128)(2,1)} %get-tuple-element.71), calls=%async_computation.2 | async-start | bytes 1048576 | tf_op jit(solution)/shard_map/all_to_all | solution.py:485
  69.7 0.3 collective-permute-start.17
  70.0 1.0 %collective-permute-done.17 = f32[64,128]{1,0:T(8,128)S(1)} collective-permute-done((f32[64,128]{1,0:T(8,128)S(1)}, f32[64,128]{1,0:T(8,128)S(1)}, u32[]{:S(2)}, u32[]{:S(2)}) %collective-permute-start.17) | collective-permute-done | bytes 32800 | tf_op jit(solution)/shard_map/ppermute | solution.py:125
  71.0 2.7 %collective-permute-start.20 = (f32[64,128]{1,0:T(8,128)S(1)}, f32[64,128]{1,0:T(8,128)S(1)}, u32[]{:S(2)}, u32[]{:S(2)}) collective-permute-start(f32[64,128]{1,0:T(8,128)S(1)} %select_add_fusion), channel_id=1, source_target_pairs={{0,6},{1,7},{2,4},{3,5},{4,2},{5,3},{6,0},{7,1},{8,14},{9,15},{10,... | collective-permute-start | bytes 98312 | tf_op jit(solution)/shard_map/ppermute | solution.py:125
  73.6 0.6 collective-permute-start.19
  74.4 3.4 %collective-permute-done.20 = f32[64,128]{1,0:T(8,128)S(1)} collective-permute-done((f32[64,128]{1,0:T(8,128)S(1)}, f32[64,128]{1,0:T(8,128)S(1)}, u32[]{:S(2)}, u32[]{:S(2)}) %collective-permute-start.20) | collective-permute-done | bytes 32800 | tf_op jit(solution)/shard_map/ppermute | solution.py:125
  77.8 0.4 collective-permute-done.19
  78.2 0.7 collective-permute-done.18
  78.9 1.1 %collective-permute-start.21 = (f32[128,128]{1,0:T(8,128)S(1)}, f32[128,128]{1,0:T(8,128)S(1)}, u32[]{:S(2)}, u32[]{:S(2)}) collective-permute-start(f32[128,128]{1,0:T(8,128)S(1)} %pad_maximum_fusion), channel_id=1, source_target_pairs={{0,8},{1,9},{2,10},{3,11},{4,12},{5,13},{6,14},{7,15},{8,0},{9,1},... | collective-permute-start | bytes 196616 | tf_op jit(solution)/shard_map/ppermute | solution.py:125
  80.1 4.2 %collective-permute-done.21 = f32[128,128]{1,0:T(8,128)S(1)} collective-permute-done((f32[128,128]{1,0:T(8,128)S(1)}, f32[128,128]{1,0:T(8,128)S(1)}, u32[]{:S(2)}, u32[]{:S(2)}) %collective-permute-start.21) | collective-permute-done | bytes 65568 | tf_op jit(solution)/shard_map/ppermute | solution.py:125
  84.2 0.8 collective-permute-start.22
  85.3 1.0 %owner_last.1.refs_0_ = bf16[16,32,128]{2,1,0:T(8,128)(2,1)S(1)} custom-call(s32[64]{0:T(128)S(1)} %reshape.75.ids, bf16[32,2,32,128]{3,2,1,0:T(8,128)(2,1)S(1)} %all-to-all-done.2.got, bf16[16,32,128]{2,1,0:T(8,128)(2,1)S(1)} %copy-done, bf16[128,128]{1,0:T(8,128)(2,1)S(1)} %get-tuple-element.59.w_self, bf16[128,128]{1,0:T(8,128)(2,1)S(1)} %get-tuple-element.47.w_msg), custom_call_target="tpu_custom_call" | custom-call | tf_op jit(solution)/shard_map/owner_last/pallas_call | solution.py:496
  86.3 1.3 %collective-permute-start.16 = (bf16[16,32,128]{2,1,0:T(8,128)(2,1)S(1)}, bf16[16,32,128]{2,1,0:T(8,128)(2,1)S(1)}, u32[]{:S(2)}, u32[]{:S(2)}) collective-permute-start(bf16[16,32,128]{2,1,0:T(8,128)(2,1)S(1)} %owner_last.1.refs_0_), channel_id=1, source_target_pairs={{0,2},{1,3},{2,0},{3,1},{4,6},{5,7},{6,4},{7,5},{8,10},{9,11},{10,... | collective-permute-start | bytes 393224 | tf_op jit(solution)/shard_map/ppermute | solution.py:26
  87.6 1.5 %collective-permute-done.22 = bf16[128,128]{1,0:T(8,128)(2,1)S(1)} collective-permute-done((bf16[128,128]{1,0:T(8,128)(2,1)S(1)}, bf16[128,128]{1,0:T(8,128)(2,1)S(1)}, u32[]{:S(2)}, u32[]{:S(2)}) %collective-permute-start.22) | collective-permute-done | bytes 32800 | tf_op jit(solution)/shard_map/ppermute | solution.py:125
  89.3 0.5 collective-permute-start.24
  89.8 1.8 %join_rows.2 = bf16[16,4,32,128]{3,2,1,0:T(8,128)(2,1)} custom-call(bf16[16,32,128]{2,1,0:T(8,128)(2,1)} %get-tuple-element.80.refs_0_, bf16[16,32,128]{2,1,0:T(8,128)(2,1)} %copy-done.2, bf16[16,32,128]{2,1,0:T(8,128)(2,1)} %copy-done.1, bf16[16,32,128]{2,1,0:T(8,128)(2,1)} %collective-permute-done.11.refs_3_), custom_call_target="tpu_custom_call" | custom-call | tf_op jit(solution)/shard_map/join_rows/pallas_call | solution.py:106
  91.8 1.3 %collective-permute-done.25.refs_3_ = bf16[16,32,128]{2,1,0:T(8,128)(2,1)S(1)} collective-permute-done((bf16[16,32,128]{2,1,0:T(8,128)(2,1)S(1)}, bf16[16,32,128]{2,1,0:T(8,128)(2,1)S(1)}, u32[]{:S(2)}, u32[]{:S(2)}) %collective-permute-start.25) | collective-permute-done | bytes 131104 | tf_op jit(solution)/shard_map/ppermute | solution.py:26
  93.0 0.9 join_rows.3
  (46 shorter events, 1.8 us)
Async XLA Ops:
  2.5 11.4 %collective-permute-start.2 = (bf16[2,128,128]{2,1,0:T(8,128)(2,1)S(1)}, bf16[2,128,128]{2,1,0:T(8,128)(2,1)S(1)}, u32[]{:S(2)}, u32[]{:S(2)}) collective-permute-start(bf16[2,128,128]{2,1,0:T(8,128)(2,1)S(1)} %get-tuple-element.48), channel_id=1, source_target_pairs={{0,28},{4,24},{8,20},{12,16},{16,12},{20,8},{24,4},{28,0},{1,29},{... | collective-permute-start | bytes 196616 | tf_op jit(solution)/shard_map/ppermute | solution.py:26
  8.6 6.2 %collective-permute-start.3 = (bf16[2,128,128]{2,1,0:T(8,128)(2,1)S(1)}, bf16[2,128,128]{2,1,0:T(8,128)(2,1)S(1)}, u32[]{:S(2)}, u32[]{:S(2)}) collective-permute-start(bf16[2,128,128]{2,1,0:T(8,128)(2,1)S(1)} %get-tuple-element.49), channel_id=1, source_target_pairs={{0,24},{4,28},{8,16},{12,20},{16,8},{20,12},{24,0},{28,4},{1,25},{... | collective-permute-start | bytes 196616 | tf_op jit(solution)/shard_map/ppermute | solution.py:26
  8.8 9.3 %collective-permute-start.4 = (bf16[2,128,128]{2,1,0:T(8,128)(2,1)S(1)}, bf16[2,128,128]{2,1,0:T(8,128)(2,1)S(1)}, u32[]{:S(2)}, u32[]{:S(2)}) collective-permute-start(bf16[2,128,128]{2,1,0:T(8,128)(2,1)S(1)} %get-tuple-element.50), channel_id=1, source_target_pairs={{0,20},{4,16},{8,28},{12,24},{16,4},{20,0},{24,12},{28,8},{1,21},{... | collective-permute-start | bytes 196616 | tf_op jit(solution)/shard_map/ppermute | solution.py:26
  9.6 10.2 %collective-permute-start.5 = (bf16[2,128,128]{2,1,0:T(8,128)(2,1)S(1)}, bf16[2,128,128]{2,1,0:T(8,128)(2,1)S(1)}, u32[]{:S(2)}, u32[]{:S(2)}) collective-permute-start(bf16[2,128,128]{2,1,0:T(8,128)(2,1)S(1)} %get-tuple-element.51), channel_id=1, source_target_pairs={{0,16},{4,20},{8,24},{12,28},{16,0},{20,4},{24,8},{28,12},{1,17},{... | collective-permute-start | bytes 196616 | tf_op jit(solution)/shard_map/ppermute | solution.py:26
  11.6 8.2 %collective-permute-start.6 = (bf16[2,128,128]{2,1,0:T(8,128)(2,1)S(1)}, bf16[2,128,128]{2,1,0:T(8,128)(2,1)S(1)}, u32[]{:S(2)}, u32[]{:S(2)}) collective-permute-start(bf16[2,128,128]{2,1,0:T(8,128)(2,1)S(1)} %get-tuple-element.52), channel_id=1, source_target_pairs={{0,12},{4,8},{8,4},{12,0},{16,28},{20,24},{24,20},{28,16},{1,13},{... | collective-permute-start | bytes 196616 | tf_op jit(solution)/shard_map/ppermute | solution.py:26
  13.9 6.2 %collective-permute-start.7 = (bf16[2,128,128]{2,1,0:T(8,128)(2,1)S(1)}, bf16[2,128,128]{2,1,0:T(8,128)(2,1)S(1)}, u32[]{:S(2)}, u32[]{:S(2)}) collective-permute-start(bf16[2,128,128]{2,1,0:T(8,128)(2,1)S(1)} %get-tuple-element.53), channel_id=1, source_target_pairs={{0,8},{4,12},{8,0},{12,4},{16,24},{20,28},{24,16},{28,20},{1,9},{5... | collective-permute-start | bytes 196616 | tf_op jit(solution)/shard_map/ppermute | solution.py:26
  14.8 5.3 %collective-permute-start.8 = (bf16[2,128,128]{2,1,0:T(8,128)(2,1)S(1)}, bf16[2,128,128]{2,1,0:T(8,128)(2,1)S(1)}, u32[]{:S(2)}, u32[]{:S(2)}) collective-permute-start(bf16[2,128,128]{2,1,0:T(8,128)(2,1)S(1)} %get-tuple-element.54), channel_id=1, source_target_pairs={{0,4},{4,0},{8,12},{12,8},{16,20},{20,16},{24,28},{28,24},{1,5},{5... | collective-permute-start | bytes 196616 | tf_op jit(solution)/shard_map/ppermute | solution.py:26
  20.2 7.6 %copy-start.3 = (s32[1,1,8,2]{2,3,1,0:T(2,128)S(1)}, s32[1,1,8,2]{2,3,1,0:T(2,128)}, u32[]{:S(2)}) copy-start(s32[1,1,8,2]{2,3,1,0:T(2,128)} %param.17) | copy-start | bytes 196
  20.2 7.6 %copy-start.4 = (s32[1,1,8,2]{2,3,1,0:T(2,128)S(1)}, s32[1,1,8,2]{2,3,1,0:T(2,128)}, u32[]{:S(2)}) copy-start(s32[1,1,8,2]{2,3,1,0:T(2,128)} %param.18) | copy-start | bytes 196
  22.7 20.7 %all-to-all-start = ((bf16[32,2,32,128]{3,2,1,0:T(8,128)(2,1)}), bf16[32,2,32,128]{3,2,1,0:T(8,128)(2,1)S(1)}, u32[]{:S(2)}, u32[]{:S(2)}) async-start(bf16[32,2,32,128]{3,2,1,0:T(8,128)(2,1)} %edge_forward.1), calls=%async_computation | async-start | bytes 1048576 | tf_op jit(solution)/shard_map/all_to_all | solution.py:435
  27.8 1.2 %collective-permute-start = (s32[1,8,4]{1,2,0:T(4,128)S(1)}, s32[1,8,4]{1,2,0:T(4,128)S(1)}, u32[]{:S(2)}, u32[]{:S(2)}) collective-permute-start(s32[1,8,4]{1,2,0:T(4,128)S(1)} %add_bitcast_fusion), channel_id=1, source_target_pairs={{0,1},{1,0},{2,3},{3,2},{4,5},{5,4},{6,7},{7,6},{8,9},{9,8},{10,11... | collective-permute-start | bytes 392 | tf_op jit(solution)/shard_map/ppermute | solution.py:26
  29.0 3.6 %collective-permute-start.1 = (s32[2,8,4]{1,2,0:T(4,128)S(1)}, s32[2,8,4]{1,2,0:T(4,128)S(1)}, u32[]{:S(2)}, u32[]{:S(2)}) collective-permute-start(s32[2,8,4]{1,2,0:T(4,128)S(1)} %add_select_fusion.1), channel_id=1, source_target_pairs={{0,2},{1,3},{2,0},{3,1},{4,6},{5,7},{6,4},{7,5},{8,10},{9,11},{10,... | collective-permute-start | bytes 776 | tf_op jit(solution)/shard_map/ppermute | solution.py:26
  45.2 18.6 %all-to-all-start.1 = ((bf16[32,2,32,128]{3,2,1,0:T(8,128)(2,1)}), bf16[32,2,32,128]{3,2,1,0:T(8,128)(2,1)S(1)}, u32[]{:S(2)}, u32[]{:S(2)}) async-start(bf16[32,2,32,128]{3,2,1,0:T(8,128)(2,1)} %get-tuple-element.60), calls=%async_computation.1 | async-start | bytes 1048576 | tf_op jit(solution)/shard_map/all_to_all | solution.py:458
  48.3 2.0 %collective-permute-start.12 = (f32[64,128]{1,0:T(8,128)S(1)}, f32[64,128]{1,0:T(8,128)S(1)}, u32[]{:S(2)}, u32[]{:S(2)}) collective-permute-start(f32[64,128]{1,0:T(8,128)S(1)} %slice_select_fusion.1), channel_id=1, source_target_pairs={{0,1},{1,0},{2,3},{3,2},{4,5},{5,4},{6,7},{7,6},{8,9},{9,8},{10,11... | collective-permute-start | bytes 98312 | tf_op jit(solution)/shard_map/ppermute | solution.py:125
  48.6 11.1 %collective-permute-start.10 = (bf16[16,32,128]{2,1,0:T(8,128)(2,1)}, bf16[16,32,128]{2,1,0:T(8,128)(2,1)S(1)}, u32[]{:S(2)}, u32[]{:S(2)}) collective-permute-start(bf16[16,32,128]{2,1,0:T(8,128)(2,1)} %get-tuple-element.80.refs_0_), channel_id=1, source_target_pairs={{0,2},{1,3},{2,0},{3,1},{4,6},{5,7},{6,4},{7,5},{8,10},{9,11},{10,... | collective-permute-start | bytes 393224 | tf_op jit(solution)/shard_map/ppermute | solution.py:26
  50.3 9.4 %collective-permute-start.15 = (f32[64,128]{1,0:T(8,128)S(1)}, f32[64,128]{1,0:T(8,128)S(1)}, u32[]{:S(2)}, u32[]{:S(2)}) collective-permute-start(f32[64,128]{1,0:T(8,128)S(1)} %select_add_fusion.1), channel_id=1, source_target_pairs={{0,6},{1,7},{2,4},{3,5},{4,2},{5,3},{6,0},{7,1},{8,14},{9,15},{10,... | collective-permute-start | bytes 98312 | tf_op jit(solution)/shard_map/ppermute | solution.py:125
  52.2 7.5 %collective-permute-start.14 = (f32[64,128]{1,0:T(8,128)S(1)}, f32[64,128]{1,0:T(8,128)S(1)}, u32[]{:S(2)}, u32[]{:S(2)}) collective-permute-start(f32[64,128]{1,0:T(8,128)S(1)} %select_add_fusion.1), channel_id=1, source_target_pairs={{0,4},{1,5},{2,6},{3,7},{4,0},{5,1},{6,2},{7,3},{8,12},{9,13},{10,... | collective-permute-start | bytes 98312 | tf_op jit(solution)/shard_map/ppermute | solution.py:125
  52.8 7.5 %collective-permute-start.13 = (f32[64,128]{1,0:T(8,128)S(1)}, f32[64,128]{1,0:T(8,128)S(1)}, u32[]{:S(2)}, u32[]{:S(2)}) collective-permute-start(f32[64,128]{1,0:T(8,128)S(1)} %select_add_fusion.1), channel_id=1, source_target_pairs={{0,2},{1,3},{2,0},{3,1},{4,6},{5,7},{6,4},{7,5},{8,10},{9,11},{10,... | collective-permute-start | bytes 98312 | tf_op jit(solution)/shard_map/ppermute | solution.py:125
  53.9 6.4 %collective-permute-start.9 = (bf16[16,32,128]{2,1,0:T(8,128)(2,1)}, bf16[16,32,128]{2,1,0:T(8,128)(2,1)S(1)}, u32[]{:S(2)}, u32[]{:S(2)}) collective-permute-start(bf16[16,32,128]{2,1,0:T(8,128)(2,1)} %get-tuple-element.80.refs_0_), channel_id=1, source_target_pairs={{0,1},{1,0},{2,3},{3,2},{4,5},{5,4},{6,7},{7,6},{8,9},{9,8},{10,11... | collective-permute-start | bytes 393224 | tf_op jit(solution)/shard_map/ppermute | solution.py:26
  59.7 4.1 %copy-start.1 = (bf16[16,32,128]{2,1,0:T(8,128)(2,1)}, bf16[16,32,128]{2,1,0:T(8,128)(2,1)S(1)}, u32[]{:S(2)}) copy-start(bf16[16,32,128]{2,1,0:T(8,128)(2,1)S(1)} %collective-permute-done.10.refs_2_) | copy-start | bytes 393220
  59.7 1.5 %collective-permute-start.11 = (bf16[16,32,128]{2,1,0:T(8,128)(2,1)S(1)}, bf16[16,32,128]{2,1,0:T(8,128)(2,1)}, u32[]{:S(2)}, u32[]{:S(2)}) collective-permute-start(bf16[16,32,128]{2,1,0:T(8,128)(2,1)S(1)} %collective-permute-done.10.refs_2_), channel_id=1, source_target_pairs={{0,1},{1,0},{2,3},{3,2},{4,5},{5,4},{6,7},{7,6},{8,9},{9,8},{10,11... | collective-permute-start | bytes 393224 | tf_op jit(solution)/shard_map/ppermute | solution.py:26
  60.3 0.7 copy-start.2
  63.8 21.5 %copy-start = (bf16[16,32,128]{2,1,0:T(8,128)(2,1)S(1)}, bf16[16,32,128]{2,1,0:T(8,128)(2,1)}, u32[]{:S(2)}) copy-start(bf16[16,32,128]{2,1,0:T(8,128)(2,1)} %get-tuple-element.72.grad_pre) | copy-start | bytes 393220
  66.6 18.7 %all-to-all-start.2 = ((bf16[32,2,32,128]{3,2,1,0:T(8,128)(2,1)}), bf16[32,2,32,128]{3,2,1,0:T(8,128)(2,1)S(1)}, u32[]{:S(2)}, u32[]{:S(2)}) async-start(bf16[32,2,32,128]{3,2,1,0:T(8,128)(2,1)} %get-tuple-element.71), calls=%async_computation.2 | async-start | bytes 1048576 | tf_op jit(solution)/shard_map/all_to_all | solution.py:485
  69.7 1.3 %collective-permute-start.17 = (f32[64,128]{1,0:T(8,128)S(1)}, f32[64,128]{1,0:T(8,128)S(1)}, u32[]{:S(2)}, u32[]{:S(2)}) collective-permute-start(f32[64,128]{1,0:T(8,128)S(1)} %slice_select_fusion), channel_id=1, source_target_pairs={{0,1},{1,0},{2,3},{3,2},{4,5},{5,4},{6,7},{7,6},{8,9},{9,8},{10,11... | collective-permute-start | bytes 98312 | tf_op jit(solution)/shard_map/ppermute | solution.py:125
  71.0 6.9 %collective-permute-start.20 = (f32[64,128]{1,0:T(8,128)S(1)}, f32[64,128]{1,0:T(8,128)S(1)}, u32[]{:S(2)}, u32[]{:S(2)}) collective-permute-start(f32[64,128]{1,0:T(8,128)S(1)} %select_add_fusion), channel_id=1, source_target_pairs={{0,6},{1,7},{2,4},{3,5},{4,2},{5,3},{6,0},{7,1},{8,14},{9,15},{10,... | collective-permute-start | bytes 98312 | tf_op jit(solution)/shard_map/ppermute | solution.py:125
  73.6 4.6 %collective-permute-start.19 = (f32[64,128]{1,0:T(8,128)S(1)}, f32[64,128]{1,0:T(8,128)S(1)}, u32[]{:S(2)}, u32[]{:S(2)}) collective-permute-start(f32[64,128]{1,0:T(8,128)S(1)} %select_add_fusion), channel_id=1, source_target_pairs={{0,4},{1,5},{2,6},{3,7},{4,0},{5,1},{6,2},{7,3},{8,12},{9,13},{10,... | collective-permute-start | bytes 98312 | tf_op jit(solution)/shard_map/ppermute | solution.py:125
  74.2 4.7 %collective-permute-start.18 = (f32[64,128]{1,0:T(8,128)S(1)}, f32[64,128]{1,0:T(8,128)S(1)}, u32[]{:S(2)}, u32[]{:S(2)}) collective-permute-start(f32[64,128]{1,0:T(8,128)S(1)} %select_add_fusion), channel_id=1, source_target_pairs={{0,2},{1,3},{2,0},{3,1},{4,6},{5,7},{6,4},{7,5},{8,10},{9,11},{10,... | collective-permute-start | bytes 98312 | tf_op jit(solution)/shard_map/ppermute | solution.py:125
  78.9 5.3 %collective-permute-start.21 = (f32[128,128]{1,0:T(8,128)S(1)}, f32[128,128]{1,0:T(8,128)S(1)}, u32[]{:S(2)}, u32[]{:S(2)}) collective-permute-start(f32[128,128]{1,0:T(8,128)S(1)} %pad_maximum_fusion), channel_id=1, source_target_pairs={{0,8},{1,9},{2,10},{3,11},{4,12},{5,13},{6,14},{7,15},{8,0},{9,1},... | collective-permute-start | bytes 196616 | tf_op jit(solution)/shard_map/ppermute | solution.py:125
  84.2 5.0 %collective-permute-start.22 = (bf16[128,128]{1,0:T(8,128)(2,1)S(1)}, bf16[128,128]{1,0:T(8,128)(2,1)S(1)}, u32[]{:S(2)}, u32[]{:S(2)}) collective-permute-start(bf16[128,128]{1,0:T(8,128)(2,1)S(1)} %add_convert_fusion), channel_id=1, source_target_pairs={{0,16},{1,17},{2,18},{3,19},{4,20},{5,21},{6,22},{7,23},{8,24},{9,... | collective-permute-start | bytes 98312 | tf_op jit(solution)/shard_map/ppermute | solution.py:125
  86.3 5.3 %collective-permute-start.16 = (bf16[16,32,128]{2,1,0:T(8,128)(2,1)S(1)}, bf16[16,32,128]{2,1,0:T(8,128)(2,1)S(1)}, u32[]{:S(2)}, u32[]{:S(2)}) collective-permute-start(bf16[16,32,128]{2,1,0:T(8,128)(2,1)S(1)} %owner_last.1.refs_0_), channel_id=1, source_target_pairs={{0,2},{1,3},{2,0},{3,1},{4,6},{5,7},{6,4},{7,5},{8,10},{9,11},{10,... | collective-permute-start | bytes 393224 | tf_op jit(solution)/shard_map/ppermute | solution.py:26
  89.2 2.4 %collective-permute-start.23 = (f32[128,128]{1,0:T(8,128)S(1)}, f32[128,128]{1,0:T(8,128)S(1)}, u32[]{:S(2)}, u32[]{:S(2)}) collective-permute-start(f32[128,128]{1,0:T(8,128)S(1)} %convert_add_fusion.refs_4_), channel_id=1, source_target_pairs={{0,1},{1,0},{2,3},{3,2},{4,5},{5,4},{6,7},{7,6},{8,9},{9,8},{10,11... | collective-permute-start | bytes 196616 | tf_op jit(solution)/shard_map/ppermute | solution.py:125
  89.3 2.5 %collective-permute-start.24 = (bf16[16,32,128]{2,1,0:T(8,128)(2,1)S(1)}, bf16[16,32,128]{2,1,0:T(8,128)(2,1)S(1)}, u32[]{:S(2)}, u32[]{:S(2)}) collective-permute-start(bf16[16,32,128]{2,1,0:T(8,128)(2,1)S(1)} %owner_last.1.refs_0_), channel_id=1, source_target_pairs={{0,1},{1,0},{2,3},{3,2},{4,5},{5,4},{6,7},{7,6},{8,9},{9,8},{10,11... | collective-permute-start | bytes 393224 | tf_op jit(solution)/shard_map/ppermute | solution.py:26
  91.6 1.4 %collective-permute-start.25 = (bf16[16,32,128]{2,1,0:T(8,128)(2,1)S(1)}, bf16[16,32,128]{2,1,0:T(8,128)(2,1)S(1)}, u32[]{:S(2)}, u32[]{:S(2)}) collective-permute-start(bf16[16,32,128]{2,1,0:T(8,128)(2,1)S(1)} %collective-permute-done.16.refs_2_), channel_id=1, source_target_pairs={{0,1},{1,0},{2,3},{3,2},{4,5},{5,4},{6,7},{7,6},{8,9},{9,8},{10,11... | collective-permute-start | bytes 393224 | tf_op jit(solution)/shard_map/ppermute | solution.py:26
